TPU v7x, 32 devices: a whole 2x2x4 slice. The times are simulated.
32 devices in a mesh: dp: 8 (over z, core), tensor: 4 (over y, x).
Axes of the slice: x: 2, y: 2, z: 4, core: 2. Of those that a mesh axis runs over, the one named last changes fastest.
Arguments:
- tokens: bfloat16 [8192, 1024], P(('dp', 'tensor')), as said below
- upstream: bfloat16 [8192, 1024], P(('dp', 'tensor')), may hold values from -6 to 6
- segment_ids: int32 [8192], P('dp'), may hold values from 0 to 5, as said below
- query_proj: bfloat16 [2, 1024, 1024], P(None, None, 'tensor'), may hold values from -0.1875 to 0.1875
- key_proj: bfloat16 [2, 1024, 1024], P(None, None, 'tensor'), may hold values from -0.1875 to 0.1875
- value_proj: bfloat16 [2, 1024, 1024], P(None, None, 'tensor'), may hold values from -0.1875 to 0.1875
- gate_proj: bfloat16 [2, 1024, 1024], P(None, None, 'tensor'), may hold values from -0.1875 to 0.1875
- output_proj: bfloat16 [2, 1024, 1024], P(None, 'tensor'), may hold values from -0.1875 to 0.1875
- left_proj: bfloat16 [2, 1024, 2816], P(None, None, 'tensor'), may hold values from -0.1875 to 0.1875
- right_proj: bfloat16 [2, 1024, 2816], P(None, None, 'tensor'), may hold values from -0.1875 to 0.1875
- down_proj: bfloat16 [2, 2816, 1024], P(None, 'tensor'), may hold values from -0.109375 to 0.109375
Outputs:
- block_out: bfloat16 [8192, 1024], P(('dp', 'tensor'))
- input_grad: bfloat16 [8192, 1024], P(('dp', 'tensor'))
- query_grad: float32 [2, 1024, 1024], P(None, None, 'tensor')
- key_grad: float32 [2, 1024, 1024], P(None, None, 'tensor')
- value_grad: float32 [2, 1024, 1024], P(None, None, 'tensor')
- gate_grad: float32 [2, 1024, 1024], P(None, None, 'tensor')
- output_grad: float32 [2, 1024, 1024], P(None, 'tensor')
- left_grad: float32 [2, 1024, 2816], P(None, None, 'tensor')
- right_grad: float32 [2, 1024, 2816], P(None, None, 'tensor')
- down_grad: float32 [2, 2816, 1024], P(None, 'tensor')
- rms_stats: float32 [2, 3], replicated
Inputs may be any that keep to these rules, and one draw needn't show every extreme that they name: `tokens`: input activations. `segment_ids`: in each sequence of 1024 tokens the ids start at 0 and rise by one at the first token of each document; every document but the last one of a sequence has 200 to 2000 tokens.
All inputs are finite; a program needn't handle non-finite values.
Results may differ from a plain program's by a relative error of at most 0.034.
Values may be sent and summed in bfloat16 or wider, within the bound.
A program may use at most 256 MiB of HBM per device.

v0:
```python
import math

import jax
import jax.numpy as jnp
from jax import lax
from jax.sharding import PartitionSpec as P

HEADS = 8
HDIM = 128
BLK = 512


epsilon = 1e-06
depth_start = 0.5
depth_step = 1.0 / 24.0
highest = lax.Precision.HIGHEST


def rms_rows(values):
    return values * lax.rsqrt(jnp.mean(values * values, axis=1, keepdims=True) + epsilon)


def rms_back(values, gradient):
    scaling = lax.rsqrt(jnp.mean(values * values, axis=1, keepdims=True) + epsilon)
    normed = values * scaling
    return scaling * (gradient - normed * jnp.mean(gradient * normed, axis=1, keepdims=True))


def contract_last(left_part, right_part):
    return lax.dot_general(
        left_part, right_part, (((1,), (1,)), ((), ())), preferred_element_type=jnp.float32
    )


def contract_first(left_part, right_part):
    return lax.dot_general(
        left_part, right_part, (((0,), (0,)), ((), ())), preferred_element_type=jnp.float32
    )


def rotate(values, cosine, sine_table):
    return jnp.concatenate([values * cosine[:, None, :], values * sine_table[:, None, :]], axis=2)


def unrotate(gradient, cosine, sine_table):
    half_width = gradient.shape[2] // 2
    return (
        gradient[:, :, :half_width] * cosine[:, None, :]
        + gradient[:, :, half_width:] * sine_table[:, None, :]
    )


def split_blocks(array, block_count):
    return array.reshape((block_count, BLK) + array.shape[1:])


def block_weights(seg_block, next_seg, decay_log):
    block_width = seg_block.shape[0]
    places = jnp.arange(block_width, dtype=jnp.float32)
    distance = places[:, None] - places[None, :]
    allowed = (distance >= 0) & (seg_block[:, None] == seg_block[None, :])
    decay_grid = jnp.where(
        allowed[None], jnp.exp(decay_log[:, None, None] * jnp.maximum(distance, 0.0)[None]), 0.0
    )
    first_seg = seg_block[0]
    query_gain = jnp.where(
        (seg_block == first_seg)[:, None], jnp.exp(places[:, None] * decay_log[None, :]), 0.0
    )
    key_gain = jnp.where(
        (seg_block == next_seg)[:, None],
        jnp.exp((block_width - places)[:, None] * decay_log[None, :]),
        0.0,
    )
    carry_gain = jnp.where(first_seg == next_seg, jnp.exp(decay_log * block_width), 0.0)
    return (decay_grid, query_gain, key_gain, carry_gain)


def next_segments(segments, block_count):
    seg_blocks = segments.reshape(block_count, BLK)
    return (seg_blocks, jnp.concatenate([seg_blocks[1:, 0], jnp.full((1,), -1, jnp.int32)]))


def attend_forward(queries, keys_rot, values, segments, decay_log):
    length, heads_here, pair_width = queries.shape
    block_count = length // BLK
    seg_blocks, next_segs = next_segments(segments, block_count)

    def advance(state_now, block_items):
        query_block, key_block, value_block, seg_block, next_seg = block_items
        query_float = query_block.astype(jnp.float32)
        key_float = key_block.astype(jnp.float32)
        value_float = value_block.astype(jnp.float32)
        decay_grid, query_gain, key_gain, carry_gain = block_weights(seg_block, next_seg, decay_log)
        scores = (
            jnp.einsum("rhd,shd->hrs", query_block, key_block, preferred_element_type=jnp.float32)
            * decay_grid
        )
        block_out = jnp.einsum("hrs,she->rhe", scores, value_float, precision=highest)
        block_out = (
            block_out
            + jnp.einsum("rhd,hde->rhe", query_float, state_now, precision=highest)
            * query_gain[:, :, None]
        )
        new_state = carry_gain[:, None, None] * state_now + jnp.einsum(
            "shd,she->hde", key_float * key_gain[:, :, None], value_float, precision=highest
        )
        return (new_state, (block_out, state_now))

    zero_state = jnp.zeros((heads_here, pair_width, pair_width // 2), jnp.float32)
    _, (block_outs, states) = lax.scan(
        advance,
        zero_state,
        (
            split_blocks(queries, block_count),
            split_blocks(keys_rot, block_count),
            split_blocks(values, block_count),
            seg_blocks,
            next_segs,
        ),
    )
    return (block_outs.reshape(length, heads_here * (pair_width // 2)), states)


def attend_backward(queries, keys_rot, values, segments, decay_log, states, grad_heads):
    length, heads_here, pair_width = queries.shape
    block_count = length // BLK
    seg_blocks, next_segs = next_segments(segments, block_count)

    def retreat(later_grad, block_items):
        query_block, key_block, value_block, seg_block, next_seg, state_now, grad_block = (
            block_items
        )
        query_float = query_block.astype(jnp.float32)
        key_float = key_block.astype(jnp.float32)
        value_float = value_block.astype(jnp.float32)
        decay_grid, query_gain, key_gain, carry_gain = block_weights(seg_block, next_seg, decay_log)
        scores = (
            jnp.einsum("rhd,shd->hrs", query_block, key_block, preferred_element_type=jnp.float32)
            * decay_grid
        )
        pulled = jnp.einsum("rhe,she->hrs", grad_block, value_float, precision=highest) * decay_grid
        grad_query = jnp.einsum("hrs,shd->rhd", pulled, key_float, precision=highest)
        grad_query = (
            grad_query
            + jnp.einsum("rhe,hde->rhd", grad_block, state_now, precision=highest)
            * query_gain[:, :, None]
        )
        grad_key = jnp.einsum("hrs,rhd->shd", pulled, query_float, precision=highest)
        grad_key = (
            grad_key
            + jnp.einsum("she,hde->shd", value_float, later_grad, precision=highest)
            * key_gain[:, :, None]
        )
        grad_value = jnp.einsum("hrs,rhe->she", scores, grad_block, precision=highest)
        grad_value = (
            grad_value
            + jnp.einsum("shd,hde->she", key_float, later_grad, precision=highest)
            * key_gain[:, :, None]
        )
        earlier_grad = carry_gain[:, None, None] * later_grad + jnp.einsum(
            "rhd,rhe->hde", query_float * query_gain[:, :, None], grad_block, precision=highest
        )
        return (earlier_grad, (grad_query, grad_key, grad_value))

    zero_state = jnp.zeros((heads_here, pair_width, pair_width // 2), jnp.float32)
    _, (grad_query, grad_key, grad_value) = lax.scan(
        retreat,
        zero_state,
        (
            split_blocks(queries, block_count),
            split_blocks(keys_rot, block_count),
            split_blocks(values, block_count),
            seg_blocks,
            next_segs,
            states,
            split_blocks(grad_heads, block_count),
        ),
        reverse=True,
    )
    return (
        grad_query.reshape(length, heads_here, pair_width),
        grad_key.reshape(length, heads_here, pair_width),
        grad_value.reshape(length, heads_here, pair_width // 2),
    )


def per_device(
    tokens,
    upstream,
    segment_ids,
    query_proj,
    key_proj,
    value_proj,
    gate_proj,
    output_proj,
    left_proj,
    right_proj,
    down_proj,
):
    layers = query_proj.shape[0]
    row_count, model_width = tokens.shape
    length = segment_ids.shape[0]
    local_width = query_proj.shape[2]
    ff_local = left_proj.shape[2]
    heads_here = local_width // HDIM
    positions = jnp.arange(length, dtype=jnp.float32)
    frequency = jnp.exp(-math.log(10000.0) * jnp.arange(HDIM, dtype=jnp.float32) / HDIM)
    angles = positions[:, None] * frequency[None, :]
    cosine = jnp.cos(angles)
    sine_table = jnp.sin(angles)
    head_index = (lax.axis_index("tensor") * heads_here + jnp.arange(heads_here)).astype(
        jnp.float32
    )
    slopes = jnp.exp2(-8.0 * (head_index + 1.0) / HEADS)

    def gather_normed(normed):
        return lax.all_gather(normed, "tensor", axis=0, tiled=True)

    def gather_again(normed):
        return lax.all_gather(normed, "tensor", axis=0, tiled=True)

    def gather_grads(gradient):
        return lax.all_gather(gradient, "tensor", axis=0, tiled=True)

    def branch_sum(operand, matrix):
        return lax.psum_scatter(
            jnp.dot(operand, matrix, preferred_element_type=jnp.float32).astype(jnp.bfloat16),
            "tensor",
            scatter_dimension=0,
            tiled=True,
        ).astype(jnp.float32)

    def input_sum(pieces, matrix):
        operand = jnp.concatenate(pieces, axis=1)
        return lax.psum_scatter(
            contract_last(operand, matrix).astype(jnp.bfloat16),
            "tensor",
            scatter_dimension=0,
            tiled=True,
        ).astype(jnp.float32)

    current = tokens.astype(jnp.float32)
    saved_layers = []
    stat_terms = []
    for layer_index in range(layers):
        residual = current
        normed = rms_rows(residual).astype(jnp.bfloat16)
        full_normed = gather_normed(normed)
        attn_weight = jnp.concatenate(
            [
                query_proj[layer_index],
                key_proj[layer_index],
                value_proj[layer_index],
                gate_proj[layer_index],
            ],
            axis=1,
        )
        projected = jnp.dot(full_normed, attn_weight, preferred_element_type=jnp.float32)
        query_lin = projected[:, :local_width]
        key_lin = projected[:, local_width : 2 * local_width]
        values = (
            projected[:, 2 * local_width : 3 * local_width]
            .astype(jnp.bfloat16)
            .reshape(length, heads_here, HDIM)
        )
        gate_lin = projected[:, 3 * local_width :]
        queries = rotate(
            jax.nn.silu(query_lin).reshape(length, heads_here, HDIM), cosine, sine_table
        ).astype(jnp.bfloat16)
        keys_rot = rotate(
            jax.nn.silu(key_lin).reshape(length, heads_here, HDIM), cosine, sine_table
        ).astype(jnp.bfloat16)
        decay_log = -slopes * (1.0 - depth_start - depth_step * layer_index)
        heads_out, states = attend_forward(queries, keys_rot, values, segment_ids, decay_log)
        squares = lax.psum(jnp.sum(heads_out * heads_out, axis=1), "tensor")
        scaling = lax.rsqrt(squares / model_width + epsilon)[:, None]
        normed_heads = heads_out * scaling
        branch = (normed_heads * gate_lin).astype(jnp.bfloat16)
        attn_rows = branch_sum(branch, output_proj[layer_index])
        middle = residual + attn_rows
        normed_mid = rms_rows(middle).astype(jnp.bfloat16)
        full_mid = gather_normed(normed_mid)
        glu_weight = jnp.concatenate([left_proj[layer_index], right_proj[layer_index]], axis=1)
        gates_both = jnp.dot(full_mid, glu_weight, preferred_element_type=jnp.float32)
        left_lin = gates_both[:, :ff_local]
        right_lin = gates_both[:, ff_local:]
        hidden = (left_lin * right_lin).astype(jnp.bfloat16)
        glu_rows = branch_sum(hidden, down_proj[layer_index])
        current = middle + glu_rows
        stat_terms.append(
            jnp.stack(
                [
                    jnp.sum(attn_rows * attn_rows),
                    jnp.sum(glu_rows * glu_rows),
                    jnp.sum(current * current),
                ]
            )
        )
        saved_layers.append(
            (
                residual,
                middle,
                normed,
                normed_mid,
                full_normed,
                full_mid,
                attn_weight,
                glu_weight,
                query_lin,
                key_lin,
                gate_lin,
                queries,
                keys_rot,
                values,
                decay_log,
                states,
                normed_heads,
                scaling,
                branch,
                left_lin,
                right_lin,
                hidden,
            )
        )
    stat_sums = lax.psum(jnp.stack(stat_terms), ("dp", "tensor"))
    rms_stats = jnp.sqrt(stat_sums / (length * lax.axis_size("dp") * model_width))
    final_rows = current.astype(jnp.bfloat16)
    gradient = upstream.astype(jnp.float32)
    layer_results = [None] * layers
    for layer_index in reversed(range(layers)):
        (
            residual,
            middle,
            normed,
            normed_mid,
            full_normed,
            full_mid,
            attn_weight,
            glu_weight,
            query_lin,
            key_lin,
            gate_lin,
            queries,
            keys_rot,
            values,
            decay_log,
            states,
            normed_heads,
            scaling,
            branch,
            left_lin,
            right_lin,
            hidden,
        ) = saved_layers[layer_index]
        glu_grad = gather_grads(gradient.astype(jnp.bfloat16))
        grad_hidden = contract_last(glu_grad, down_proj[layer_index])
        down_part = contract_first(hidden, glu_grad)
        grad_left = (grad_hidden * right_lin).astype(jnp.bfloat16)
        grad_right = (grad_hidden * left_lin).astype(jnp.bfloat16)
        grad_gates = jnp.concatenate([grad_left, grad_right], axis=1)
        mid_rows = input_sum((grad_left, grad_right), glu_weight)
        source_mid = gather_again(normed_mid)
        glu_part = contract_first(source_mid, grad_gates)
        gradient = gradient + rms_back(middle, mid_rows)
        attn_grad = gather_grads(gradient.astype(jnp.bfloat16))
        output_part = contract_first(branch, attn_grad)
        grad_branch = contract_last(attn_grad, output_proj[layer_index])
        grad_normed = grad_branch * gate_lin
        grad_gate = (grad_branch * normed_heads).astype(jnp.bfloat16)
        inner_sum = lax.psum(jnp.sum(grad_normed * normed_heads, axis=1), "tensor")
        grad_heads = scaling * (grad_normed - normed_heads * (inner_sum / model_width)[:, None])
        grad_query, grad_key, grad_value = attend_backward(
            queries,
            keys_rot,
            values,
            segment_ids,
            decay_log,
            states,
            grad_heads.reshape(length, heads_here, HDIM),
        )
        sigmoid_query = jax.nn.sigmoid(query_lin)
        sigmoid_key = jax.nn.sigmoid(key_lin)
        query_back = unrotate(grad_query, cosine, sine_table).reshape(length, local_width)
        key_back = unrotate(grad_key, cosine, sine_table).reshape(length, local_width)
        grad_query_lin = (
            query_back * (sigmoid_query + query_lin * sigmoid_query * (1.0 - sigmoid_query))
        ).astype(jnp.bfloat16)
        grad_key_lin = (
            key_back * (sigmoid_key + key_lin * sigmoid_key * (1.0 - sigmoid_key))
        ).astype(jnp.bfloat16)
        grad_value_lin = grad_value.reshape(length, local_width).astype(jnp.bfloat16)
        grad_projected = jnp.concatenate(
            [grad_query_lin, grad_key_lin, grad_value_lin, grad_gate], axis=1
        )
        in_rows = input_sum((grad_query_lin, grad_key_lin, grad_value_lin, grad_gate), attn_weight)
        source_normed = gather_again(normed)
        attn_part = contract_first(source_normed, grad_projected)
        gradient = gradient + rms_back(residual, in_rows)
        query_part = attn_part[:, :local_width]
        key_part = attn_part[:, local_width : 2 * local_width]
        value_part = attn_part[:, 2 * local_width : 3 * local_width]
        gate_part = attn_part[:, 3 * local_width :]
        left_part = glu_part[:, :ff_local]
        right_part = glu_part[:, ff_local:]
        layer_results[layer_index] = (
            query_part,
            key_part,
            value_part,
            gate_part,
            output_part,
            left_part,
            right_part,
            down_part,
        )
    stacked = [
        jnp.stack([layer_results[index][member] for index in range(layers)]) for member in range(8)
    ]
    totals = (
        lax.psum(stacked[0].astype(jnp.bfloat16), "dp").astype(jnp.float32),
        lax.psum(stacked[1].astype(jnp.bfloat16), "dp").astype(jnp.float32),
        lax.psum(stacked[2].astype(jnp.bfloat16), "dp").astype(jnp.float32),
        lax.psum(stacked[3].astype(jnp.bfloat16), "dp").astype(jnp.float32),
        lax.psum(stacked[4].astype(jnp.bfloat16), "dp").astype(jnp.float32),
        lax.psum(stacked[5].astype(jnp.bfloat16), "dp").astype(jnp.float32),
        lax.psum(stacked[6].astype(jnp.bfloat16), "dp").astype(jnp.float32),
        lax.psum(stacked[7].astype(jnp.bfloat16), "dp").astype(jnp.float32),
    )
    input_grad = gradient.astype(jnp.bfloat16)
    return (
        final_rows,
        input_grad,
        totals[0],
        totals[1],
        totals[2],
        totals[3],
        totals[4],
        totals[5],
        totals[6],
        totals[7],
        rms_stats,
    )


def solution(mesh):
    return jax.shard_map(
        per_device,
        mesh=mesh,
        in_specs=(
            P(("dp", "tensor"), None),
            P(("dp", "tensor"), None),
            P("dp"),
            P(None, None, "tensor"),
            P(None, None, "tensor"),
            P(None, None, "tensor"),
            P(None, None, "tensor"),
            P(None, "tensor", None),
            P(None, None, "tensor"),
            P(None, None, "tensor"),
            P(None, "tensor", None),
        ),
        out_specs=(
            P(("dp", "tensor"), None),
            P(("dp", "tensor"), None),
            P(None, None, "tensor"),
            P(None, None, "tensor"),
            P(None, None, "tensor"),
            P(None, None, "tensor"),
            P(None, "tensor", None),
            P(None, None, "tensor"),
            P(None, None, "tensor"),
            P(None, "tensor", None),
            P(),
        ),
        check_vma=False,
    )
```

profile of v0, /device:TPU:0, one launch (start us, length us, event | category | flops | bytes accessed | tf_op | source)
XLA Modules:
  0.0 1295.6 jit_solution(18006518163351653731)
XLA Ops:
  18.3 31.1 %all-gather.9.cloned.1.call-done = bf16[1024,1024]{1,0:T(8,128)(2,1)} async-done(((bf16[256,1024]{1,0:T(8,128)(2,1)}), bf16[1024,1024]{1,0:T(8,128)(2,1)}) %all-gather.9.cloned.1.call-update) | async-done | bytes 2097168 | tf_op jit(solution)/shard_map/all_gather | solution.py:217
  49.4 4.1 fusion.289
  67.0 25.2 %while.72 = (s32[]{:T(128)}, f32[2,256,128]{2,1,0:T(8,128)S(1)}, f32[2,512,2,128]{1,3,2,0:T(8,128)}, f32[2,2,256,128]{3,2,1,0:T(8,128)S(1)}, s32[2,512]{1,0:T(2,...) while((s32[]{:T(128)}, f32[2,256,128]{2,1,0:T(8,128)S(1)}, ...), condition=%wide.region_2.3_spmd.clone, body=%wide.region_1.2_spmd.clone.sunk | while | flops 1883313664 | bytes 31230888 | solution.py:110
  73.3 3.3 fusion.424
  85.9 3.3 fusion.424
  95.2 9.1 psum.91
  108.7 35.3 %reduce-scatter.9.cloned.1.call-done = bf16[256,1024]{1,0:T(8,128)(2,1)} async-done(((bf16[1024,1024]{1,0:T(8,128)(2,1)}), bf16[256,1024]{1,0:T(8,128)(2,1)}) %reduce-scatter.9.cloned.1.call-update) | async-done | bytes 524304 | tf_op jit(solution)/shard_map/reduce_scatter | solution.py:226
  147.4 4.5 slice_bitcast_fusion.4
  151.8 30.9 %all-gather.11.cloned.1.call-done = bf16[1024,1024]{1,0:T(8,128)(2,1)} async-done(((bf16[256,1024]{1,0:T(8,128)(2,1)}), bf16[1024,1024]{1,0:T(8,128)(2,1)}) %all-gather.11.cloned.1.call-update) | async-done | bytes 2097168 | tf_op jit(solution)/shard_map/all_gather | solution.py:217
  182.8 5.9 fusion.229
  192.8 3.1 convolution_convert_fusion.11
  196.0 35.3 %reduce-scatter.11.cloned.1.call-done = bf16[256,1024]{1,0:T(8,128)(2,1)} async-done(((bf16[1024,1024]{1,0:T(8,128)(2,1)}), bf16[256,1024]{1,0:T(8,128)(2,1)}) %reduce-scatter.11.cloned.1.call-update) | async-done | bytes 524304 | tf_op jit(solution)/shard_map/reduce_scatter | solution.py:226
  235.8 34.9 %all-gather.13.cloned.1.call-done = bf16[1024,1024]{1,0:T(8,128)(2,1)} async-done(((bf16[256,1024]{1,0:T(8,128)(2,1)}), bf16[1024,1024]{1,0:T(8,128)(2,1)}) %all-gather.13.cloned.1.call-update) | async-done | bytes 2097168 | tf_op jit(solution)/shard_map/all_gather | solution.py:217
  270.7 4.1 fusion.288
  288.2 25.2 %while.73 = (s32[]{:T(128)}, f32[2,256,128]{2,1,0:T(8,128)S(1)}, f32[2,512,2,128]{1,3,2,0:T(8,128)}, f32[2,2,256,128]{3,2,1,0:T(8,128)S(1)}, s32[2,512]{1,0:T(2,...) while((s32[]{:T(128)}, f32[2,256,128]{2,1,0:T(8,128)S(1)}, ...), condition=%wide.region_10.11_spmd.clone, body=%wide.region_9.10_spmd.clone.sunk | while | flops 1883313664 | bytes 31230888 | solution.py:110
  294.6 3.3 fusion.437
  307.1 3.3 fusion.437
  316.0 9.2 psum.92
  329.7 35.3 %reduce-scatter.13.cloned.1.call-done = bf16[256,1024]{1,0:T(8,128)(2,1)} async-done(((bf16[1024,1024]{1,0:T(8,128)(2,1)}), bf16[256,1024]{1,0:T(8,128)(2,1)}) %reduce-scatter.13.cloned.1.call-update) | async-done | bytes 524304 | tf_op jit(solution)/shard_map/reduce_scatter | solution.py:226
  369.1 34.7 %all-gather.15.cloned.1.call-done = bf16[1024,1024]{1,0:T(8,128)(2,1)} async-done(((bf16[256,1024]{1,0:T(8,128)(2,1)}), bf16[1024,1024]{1,0:T(8,128)(2,1)}) %all-gather.15.cloned.1.call-update) | async-done | bytes 2097168 | tf_op jit(solution)/shard_map/all_gather | solution.py:217
  403.7 8.4 fusion.228
  412.1 28.9 %all-gather.17.cloned.1.call-done = bf16[1024,1024]{1,0:T(8,128)(2,1)} async-done(((bf16[256,1024]{1,0:T(8,128)(2,1)}), bf16[1024,1024]{1,0:T(8,128)(2,1)}) %all-gather.17.cloned.1.call-update) | async-done | bytes 2097168 | tf_op jit(solution)/shard_map/all_gather | solution.py:223
  441.1 7.5 multiply_convert_fusion.3
  449.8 3.1 convolution_convert_fusion.10
  452.9 7.5 convolution_convert_fusion.7
  460.5 27.7 %reduce-scatter.15.cloned.1.call-done = bf16[256,1024]{1,0:T(8,128)(2,1)} async-done(((bf16[1024,1024]{1,0:T(8,128)(2,1)}), bf16[256,1024]{1,0:T(8,128)(2,1)}) %reduce-scatter.15.cloned.1.call-update) | async-done | bytes 524304 | tf_op jit(solution)/shard_map/reduce_scatter | solution.py:226
  488.3 38.6 %reduce-scatter.17.cloned.1.call-done = bf16[256,1024]{1,0:T(8,128)(2,1)} async-done(((bf16[1024,1024]{1,0:T(8,128)(2,1)}), bf16[256,1024]{1,0:T(8,128)(2,1)}) %reduce-scatter.17.cloned.1.call-update) | async-done | bytes 524304 | tf_op jit(solution)/shard_map/reduce_scatter | solution.py:235
  526.9 3.5 multiply_reduce_fusion
  535.4 31.7 %all-gather.19.cloned.1.call-done = bf16[1024,1024]{1,0:T(8,128)(2,1)} async-done(((bf16[256,1024]{1,0:T(8,128)(2,1)}), bf16[1024,1024]{1,0:T(8,128)(2,1)}) %all-gather.19.cloned.1.call-update) | async-done | bytes 2097168 | tf_op jit(solution)/shard_map/all_gather | solution.py:223
  567.1 3.8 multiply_reduce_fusion.2
  570.9 8.9 psum.93
  579.8 3.0 subtract_multiply_fusion.1
  582.8 3.1 reshape_reshape.18
  588.9 71.6 %while.74 = (s32[]{:T(128)}, f32[2,256,128]{2,1,0:T(8,128)S(1)}, f32[2,512,2,256]{3,1,0,2:T(8,128)}, f32[2,512,2,256]{3,1,0,2:T(8,128)}, bf16[2,512,2,128]{1,3,2...) while((s32[]{:T(128)}, f32[2,256,128]{2,1,0:T(8,128)S(1)}, ...), condition=%wide.region_21.22_spmd.clone, body=%wide.region_20.21_spmd.clone.sunk | while | flops 6717773312 | bytes 75539592 | solution.py:166
  589.2 3.3 fusion.462
  595.7 4.3 fusion.463
  611.2 2.9 convolution_add_fusion.10
  621.3 2.8 constant_dynamic-update-slice_fusion.6
  624.1 3.3 fusion.462
  630.6 4.3 fusion.463
  647.1 2.9 convolution_add_fusion.10
  657.3 2.8 constant_dynamic-update-slice_fusion.6
  669.5 3.7 convolution_convert_fusion.6
  673.3 35.3 %reduce-scatter.19.cloned.1.call-done = bf16[256,1024]{1,0:T(8,128)(2,1)} async-done(((bf16[1024,1024]{1,0:T(8,128)(2,1)}), bf16[256,1024]{1,0:T(8,128)(2,1)}) %reduce-scatter.19.cloned.1.call-update) | async-done | bytes 524304 | tf_op jit(solution)/shard_map/reduce_scatter | solution.py:235
  712.6 35.4 %all-gather.21.cloned.1.call-done = bf16[1024,1024]{1,0:T(8,128)(2,1)} async-done(((bf16[256,1024]{1,0:T(8,128)(2,1)}), bf16[1024,1024]{1,0:T(8,128)(2,1)}) %all-gather.21.cloned.1.call-update) | async-done | bytes 2097168 | tf_op jit(solution)/shard_map/all_gather | solution.py:223
  748.0 5.8 multiply_convert_fusion.1
  755.4 4.7 convolution_convert_fusion.5
  760.2 35.3 %reduce-scatter.21.cloned.1.call-done = bf16[256,1024]{1,0:T(8,128)(2,1)} async-done(((bf16[1024,1024]{1,0:T(8,128)(2,1)}), bf16[256,1024]{1,0:T(8,128)(2,1)}) %reduce-scatter.21.cloned.1.call-update) | async-done | bytes 524304 | tf_op jit(solution)/shard_map/reduce_scatter | solution.py:235
  800.0 6.0 convolution_convert_fusion
  812.3 3.7 convolution_convert_fusion.2
  816.0 19.3 %all-gather.23.cloned.1.call-done = bf16[1024,1024]{1,0:T(8,128)(2,1)} async-done(((bf16[256,1024]{1,0:T(8,128)(2,1)}), bf16[1024,1024]{1,0:T(8,128)(2,1)}) %all-gather.23.cloned.1.call-update) | async-done | bytes 2097168 | tf_op jit(solution)/shard_map/all_gather | solution.py:223
  837.9 8.9 psum.94
  854.2 66.9 %while.75 = (s32[]{:T(128)}, f32[2,256,128]{2,1,0:T(8,128)}, f32[2,512,2,256]{3,1,0,2:T(8,128)}, f32[2,512,2,256]{3,1,0,2:T(8,128)}, bf16[2,512,2,128]{1,3,2,0:T...) while((s32[]{:T(128)}, f32[2,256,128]{2,1,0:T(8,128)}, ...), condition=%wide.region_29.30_spmd.clone, body=%wide.region_28.29_spmd.clone.sunk | while | flops 6717773312 | bytes 69248592 | solution.py:166
  854.5 2.9 fusion.488
  860.5 4.3 fusion.489
  887.6 2.9 fusion.488
  893.6 4.3 fusion.489
  930.3 3.7 convolution_convert_fusion.4
  944.5 4.2 convolution_convert_fusion.1
  968.2 40.8 %psum.103 = f32[2,3]{1,0:T(2,128)S(1)} all-reduce(f32[2,3]{1,0:T(2,128)S(1)} %pad_maximum_fusion.36), channel_id=1, replica_groups=mesh['dp'=8,'tensor'=4] {'dp','tensor'}, use_global_device_ids=true, to_apply=%region_46.47 | all-reduce | flops 6 | bytes 48 | tf_op jit(solution)/shard_map/psum | solution.py:325
  1013.5 252.6 %all-reduce.3.cloned.1.call-done = (bf16[2,1024,704]{2,1,0:T(8,128)(2,1)}, bf16[2,1024,704]{2,1,0:T(8,128)(2,1)}, bf16[2,1024,256]{2,1,0:T(8,128)(2,1)}, bf16[2,...) async-done(((bf16[2,1024,704]{2,1,0:T(8,128)(2,1)}, ...) | async-done | bytes 13893648 | tf_op jit(solution)/shard_map/psum | solution.py:424
  1275.1 5.4 copy.104
  1280.4 3.4 copy.105
  1283.8 5.1 convert_element_type.266
  (655 shorter events, 286.6 us)
Async XLA Ops:
  7.2 42.2 %all-gather.9.cloned.1.call-start = ((), (), s32[]{:S(2)}) async-start(), calls=%async_computation.8 | async-start | bytes 2621440 | tf_op jit(solution)/shard_map/all_gather | solution.py:217
  11.2 132.8 %reduce-scatter.9.cloned.1.call-start = ((), (), s32[]{:S(2)}) async-start(), calls=%async_computation.9 | async-start | bytes 2621440 | tf_op jit(solution)/shard_map/reduce_scatter | solution.py:226
  14.5 49.6 %copy-start.63 = (f32[2,512,128]{1,2,0:T(8,128)}, f32[2,512,128]{1,2,0:T(8,128)S(1)}, u32[]{:S(2)}) copy-start(f32[2,512,128]{1,2,0:T(8,128)S(1)} %get-tuple-element.1113) | copy-start | bytes 1572868
  14.5 49.6 %copy-start.65 = (f32[2,512,128]{1,2,0:T(8,128)}, f32[2,512,128]{1,2,0:T(8,128)S(1)}, u32[]{:S(2)}) copy-start(f32[2,512,128]{1,2,0:T(8,128)S(1)} %get-tuple-element.1114) | copy-start | bytes 1572868
  17.2 32.2 %copy-start.113 = (bf16[1024,256]{1,0:T(8,128)(2,1)S(1)}, bf16[1024,256]{1,0:T(8,128)(2,1)}, u32[]{:S(2)}) copy-start(bf16[1024,256]{1,0:T(8,128)(2,1)} %get-tuple-element.1105) | copy-start | bytes 1572868
  17.2 32.2 %copy-start.115 = (bf16[1024,256]{1,0:T(8,128)(2,1)S(1)}, bf16[1024,256]{1,0:T(8,128)(2,1)}, u32[]{:S(2)}) copy-start(bf16[1024,256]{1,0:T(8,128)(2,1)} %get-tuple-element.1121) | copy-start | bytes 1572868
  18.3 31.1 %copy-start.117 = (bf16[1024,256]{1,0:T(8,128)(2,1)}, bf16[1024,256]{1,0:T(8,128)(2,1)S(1)}, u32[]{:S(2)}) copy-start(bf16[1024,256]{1,0:T(8,128)(2,1)S(1)} %get-tuple-element.1101) | copy-start | bytes 1572868
  18.3 31.1 %copy-start.119 = (bf16[1024,256]{1,0:T(8,128)(2,1)}, bf16[1024,256]{1,0:T(8,128)(2,1)S(1)}, u32[]{:S(2)}) copy-start(bf16[1024,256]{1,0:T(8,128)(2,1)S(1)} %get-tuple-element.1123) | copy-start | bytes 1572868
  95.2 9.1 copy-start.32
  95.2 11.3 copy-start.72
  106.5 37.5 %copy-start.26 = (bf16[256,1024]{1,0:T(8,128)(2,1)S(1)}, bf16[256,1024]{1,0:T(8,128)(2,1)}, u32[]{:S(2)}) copy-start(bf16[256,1024]{1,0:T(8,128)(2,1)} %param.19) | copy-start | bytes 1572868
  108.6 38.8 %copy-start.76 = (bf16[2,1024,704]{1,2,0:T(8,128)(2,1)S(1)}, bf16[2,1024,704]{1,2,0:T(8,128)(2,1)}, u32[]{:S(2)}) copy-start(bf16[2,1024,704]{1,2,0:T(8,128)(2,1)} %param.28) | copy-start | bytes 8650756
  108.6 74.2 %all-gather.11.cloned.1.call-start = ((), (), s32[]{:S(2)}) async-start(), calls=%async_computation.10 | async-start | bytes 2621440 | tf_op jit(solution)/shard_map/all_gather | solution.py:217
  147.3 83.9 %reduce-scatter.11.cloned.1.call-start = ((), (), s32[]{:S(2)}) async-start(), calls=%async_computation.11 | async-start | bytes 2621440 | tf_op jit(solution)/shard_map/reduce_scatter | solution.py:226
  195.9 35.4 %copy-start.29 = (bf16[256,1024]{1,0:T(8,128)(2,1)S(1)}, bf16[256,1024]{1,0:T(8,128)(2,1)}, u32[]{:S(2)}) copy-start(bf16[256,1024]{1,0:T(8,128)(2,1)} %reduce-scatter.9.cloned.1.call-done) | copy-start | bytes 1572868
  195.9 74.8 %copy-start.121 = (bf16[1024,256]{1,0:T(8,128)(2,1)S(1)}, bf16[1024,256]{1,0:T(8,128)(2,1)}, u32[]{:S(2)}) copy-start(bf16[1024,256]{1,0:T(8,128)(2,1)} %get-tuple-element.1104) | copy-start | bytes 1572868
  195.9 74.8 %copy-start.123 = (bf16[1024,256]{1,0:T(8,128)(2,1)S(1)}, bf16[1024,256]{1,0:T(8,128)(2,1)}, u32[]{:S(2)}) copy-start(bf16[1024,256]{1,0:T(8,128)(2,1)} %get-tuple-element.1122) | copy-start | bytes 1572868
  195.9 74.8 %copy-start.125 = (bf16[1024,256]{1,0:T(8,128)(2,1)S(1)}, bf16[1024,256]{1,0:T(8,128)(2,1)}, u32[]{:S(2)}) copy-start(bf16[1024,256]{1,0:T(8,128)(2,1)} %get-tuple-element.1100) | copy-start | bytes 1572868
  195.9 74.8 %copy-start.127 = (bf16[1024,256]{1,0:T(8,128)(2,1)S(1)}, bf16[1024,256]{1,0:T(8,128)(2,1)}, u32[]{:S(2)}) copy-start(bf16[1024,256]{1,0:T(8,128)(2,1)} %get-tuple-element.1124) | copy-start | bytes 1572868
  195.9 74.8 %all-gather.13.cloned.1.call-start = ((), (), s32[]{:S(2)}) async-start(), calls=%async_computation.12 | async-start | bytes 2621440 | tf_op jit(solution)/shard_map/all_gather | solution.py:217
  235.2 129.8 %reduce-scatter.13.cloned.1.call-start = ((), (), s32[]{:S(2)}) async-start(), calls=%async_computation.13 | async-start | bytes 2621440 | tf_op jit(solution)/shard_map/reduce_scatter | solution.py:226
  316.0 9.3 copy-start.34
  316.0 11.5 copy-start.73
  327.5 37.5 %copy-start.16 = (f32[256,1024]{1,0:T(8,128)S(1)}, f32[256,1024]{1,0:T(8,128)}, u32[]{:S(2)}) copy-start(f32[256,1024]{1,0:T(8,128)} %copy-done.15) | copy-start | bytes 3145732
  329.6 74.1 %all-gather.15.cloned.1.call-start = ((), (), s32[]{:S(2)}) async-start(), calls=%async_computation.14 | async-start | bytes 2621440 | tf_op jit(solution)/shard_map/all_gather | solution.py:217
  368.3 72.8 %all-gather.17.cloned.1.call-start = ((), (), s32[]{:S(2)}) async-start(), calls=%async_computation.16 | async-start | bytes 2621440 | tf_op jit(solution)/shard_map/all_gather | solution.py:223
  369.0 119.2 %reduce-scatter.15.cloned.1.call-start = ((), (), s32[]{:S(2)}) async-start(), calls=%async_computation.15 | async-start | bytes 2621440 | tf_op jit(solution)/shard_map/reduce_scatter | solution.py:226
  441.1 8.7 copy-start.137
  452.9 74.0 %reduce-scatter.17.cloned.1.call-start = ((), (), s32[]{:S(2)}) async-start(), calls=%async_computation.17 | async-start | bytes 2621440 | tf_op jit(solution)/shard_map/reduce_scatter | solution.py:235
  460.4 66.4 %copy-start.38 = (bf16[256,1024]{1,0:T(8,128)(2,1)S(1)}, bf16[256,1024]{1,0:T(8,128)(2,1)}, u32[]{:S(2)}) copy-start(bf16[256,1024]{1,0:T(8,128)(2,1)} %reduce-scatter.13.cloned.1.call-done) | copy-start | bytes 1572868
  460.5 70.0 %copy-start.69 = (bf16[256,1024]{1,0:T(8,128)(2,1)S(1)}, bf16[256,1024]{1,0:T(8,128)(2,1)}, u32[]{:S(2)}) copy-start(bf16[256,1024]{1,0:T(8,128)(2,1)} %param.20) | copy-start | bytes 1572868
  460.5 106.6 %all-gather.19.cloned.1.call-start = ((), (), s32[]{:S(2)}) async-start(), calls=%async_computation.18 | async-start | bytes 2621440 | tf_op jit(solution)/shard_map/all_gather | solution.py:223
  531.6 35.5 %copy-start.35 = (f32[32,8,2,512]{3,1,2,0:T(8,128)S(1)}, f32[32,8,2,512]{3,1,2,0:T(8,128)}, u32[]{:S(2)}) copy-start(f32[32,8,2,512]{3,1,2,0:T(8,128)} %copy-done.34) | copy-start | bytes 3145732
  531.6 176.9 %reduce-scatter.19.cloned.1.call-start = ((), (), s32[]{:S(2)}) async-start(), calls=%async_computation.19 | async-start | bytes 2621440 | tf_op jit(solution)/shard_map/reduce_scatter | solution.py:235
  531.7 39.1 %copy-start.67 = (bf16[2,512,2,128]{1,3,2,0:T(8,128)(2,1)}, bf16[2,512,2,128]{1,3,2,0:T(8,128)(2,1)S(1)}, u32[]{:S(2)}) copy-start(bf16[2,512,2,128]{1,3,2,0:T(8,128)(2,1)S(1)} %fusion.306) | copy-start | bytes 1572868
  589.1 13.3 %copy-start.9 = (bf16[2,512,2,256]{1,3,2,0:T(8,128)(2,1)}, bf16[2,512,2,256]{1,3,2,0:T(8,128)(2,1)S(1)}, u32[]{:S(2)}) copy-start(bf16[2,512,2,256]{1,3,2,0:T(8,128)(2,1)S(1)} %get-tuple-element.1582) | copy-start | bytes 3145732 | tf_op jit(solution)/shard_map/while
  589.1 13.3 %copy-start.24 = (f32[2,256,128]{2,1,0:T(8,128)}, f32[2,256,128]{2,1,0:T(8,128)S(1)}, u32[]{:S(2)}) copy-start(f32[2,256,128]{2,1,0:T(8,128)S(1)} %get-tuple-element.1557) | copy-start | bytes 786436 | tf_op jit(solution)/shard_map/while
  592.7 7.3 copy-start
  624.1 13.3 %copy-start.9 = (bf16[2,512,2,256]{1,3,2,0:T(8,128)(2,1)}, bf16[2,512,2,256]{1,3,2,0:T(8,128)(2,1)S(1)}, u32[]{:S(2)}) copy-start(bf16[2,512,2,256]{1,3,2,0:T(8,128)(2,1)S(1)} %get-tuple-element.1582) | copy-start | bytes 3145732 | tf_op jit(solution)/shard_map/while
  624.1 13.3 %copy-start.24 = (f32[2,256,128]{2,1,0:T(8,128)}, f32[2,256,128]{2,1,0:T(8,128)S(1)}, u32[]{:S(2)}) copy-start(f32[2,256,128]{2,1,0:T(8,128)S(1)} %get-tuple-element.1557) | copy-start | bytes 786436 | tf_op jit(solution)/shard_map/while
  627.7 7.3 copy-start
  673.2 35.4 %copy-start.17 = (f32[256,1024]{1,0:T(8,128)S(1)}, f32[256,1024]{1,0:T(8,128)}, u32[]{:S(2)}) copy-start(f32[256,1024]{1,0:T(8,128)} %copy-done.15) | copy-start | bytes 3145732
  673.2 36.7 %copy-start.39 = (bf16[256,1024]{1,0:T(8,128)(2,1)S(1)}, bf16[256,1024]{1,0:T(8,128)(2,1)}, u32[]{:S(2)}) copy-start(bf16[256,1024]{1,0:T(8,128)(2,1)} %reduce-scatter.13.cloned.1.call-done) | copy-start | bytes 1572868
  673.2 36.7 %copy-start.70 = (bf16[256,1024]{1,0:T(8,128)(2,1)S(1)}, bf16[256,1024]{1,0:T(8,128)(2,1)}, u32[]{:S(2)}) copy-start(bf16[256,1024]{1,0:T(8,128)(2,1)} %param.20) | copy-start | bytes 1572868
  673.2 74.8 %all-gather.21.cloned.1.call-start = ((), (), s32[]{:S(2)}) async-start(), calls=%async_computation.20 | async-start | bytes 2621440 | tf_op jit(solution)/shard_map/all_gather | solution.py:223
  712.5 85.1 %copy-start.48 = (f32[256,1024]{1,0:T(8,128)}, f32[256,1024]{1,0:T(8,128)S(1)}, u32[]{:S(2)}) copy-start(f32[256,1024]{1,0:T(8,128)S(1)} %get-tuple-element.1025) | copy-start | bytes 3145732
  712.5 42.9 %copy-start.86 = (bf16[1024,704]{0,1:T(8,128)(2,1)S(1)}, bf16[1024,704]{0,1:T(8,128)(2,1)}, u32[]{:S(2)}) copy-start(bf16[1024,704]{0,1:T(8,128)(2,1)} %get-tuple-element.1072) | copy-start | bytes 4325380
  712.5 83.0 %reduce-scatter.21.cloned.1.call-start = ((), (), s32[]{:S(2)}) async-start(), calls=%async_computation.21 | async-start | bytes 2621440 | tf_op jit(solution)/shard_map/reduce_scatter | solution.py:235
  748.0 7.5 copy-start.87
  760.1 35.4 %copy-start.27 = (bf16[256,1024]{1,0:T(8,128)(2,1)S(1)}, bf16[256,1024]{1,0:T(8,128)(2,1)}, u32[]{:S(2)}) copy-start(bf16[256,1024]{1,0:T(8,128)(2,1)} %param.19) | copy-start | bytes 1572868
  760.1 35.4 %copy-start.30 = (bf16[256,1024]{1,0:T(8,128)(2,1)S(1)}, bf16[256,1024]{1,0:T(8,128)(2,1)}, u32[]{:S(2)}) copy-start(bf16[256,1024]{1,0:T(8,128)(2,1)} %reduce-scatter.9.cloned.1.call-done) | copy-start | bytes 1572868
  760.1 35.4 %copy-start.132 = (f32[256]{0:T(256)S(1)}, f32[256]{0:T(256)}, u32[]{:S(2)}) copy-start(f32[256]{0:T(256)} %copy-done.131) | copy-start | bytes 3076
  760.2 75.1 %all-gather.23.cloned.1.call-start = ((), (), s32[]{:S(2)}) async-start(), calls=%async_computation.22 | async-start | bytes 2621440 | tf_op jit(solution)/shard_map/all_gather | solution.py:223
  799.8 209.8 %reduce-scatter.23.cloned.1.call-start = ((), (), s32[]{:S(2)}) async-start(), calls=%async_computation.23 | async-start | bytes 2621440 | tf_op jit(solution)/shard_map/reduce_scatter | solution.py:235
  812.3 23.0 %copy-start.33 = (f32[32,8,2,512]{3,1,2,0:T(8,128)S(1)}, f32[32,8,2,512]{3,1,2,0:T(8,128)}, u32[]{:S(2)}) copy-start(f32[32,8,2,512]{3,1,2,0:T(8,128)} %copy-done.32) | copy-start | bytes 3145732
  812.3 23.0 %copy-start.74 = (bf16[2,256,1024]{2,1,0:T(8,128)(2,1)S(1)}, bf16[2,256,1024]{2,1,0:T(8,128)(2,1)}, u32[]{:S(2)}) copy-start(bf16[2,256,1024]{2,1,0:T(8,128)(2,1)} %param.26) | copy-start | bytes 3145732
  812.3 23.0 %copy-start.130 = (f32[1024]{0:T(1024)S(1)}, f32[1024]{0:T(1024)}, u32[]{:S(2)}) copy-start(f32[1024]{0:T(1024)} %copy-done.129) | copy-start | bytes 12292
  890.7 7.3 copy-start.2
  934.0 332.1 %all-reduce.3.cloned.1.call-start = ((), (), s32[]{:S(2)}) async-start(), calls=%async_computation.24 | async-start | bytes 28835840 | tf_op jit(solution)/shard_map/psum | solution.py:424
  964.1 45.5 %copy-start.28 = (bf16[256,1024]{1,0:T(8,128)(2,1)S(1)}, bf16[256,1024]{1,0:T(8,128)(2,1)}, u32[]{:S(2)}) copy-start(bf16[256,1024]{1,0:T(8,128)(2,1)} %param.19) | copy-start | bytes 1572868
  964.1 45.5 %copy-start.134 = (f32[256]{0:T(256)S(1)}, f32[256]{0:T(256)}, u32[]{:S(2)}) copy-start(f32[256]{0:T(256)} %copy-done.133) | copy-start | bytes 3076
  964.1 46.9 %copy-start.31 = (bf16[256,1024]{1,0:T(8,128)(2,1)S(1)}, bf16[256,1024]{1,0:T(8,128)(2,1)}, u32[]{:S(2)}) copy-start(bf16[256,1024]{1,0:T(8,128)(2,1)} %reduce-scatter.9.cloned.1.call-done) | copy-start | bytes 1572868
  964.1 46.9 %copy-start.49 = (f32[256,1024]{1,0:T(8,128)S(1)}, f32[256,1024]{1,0:T(8,128)}, u32[]{:S(2)}) copy-start(f32[256,1024]{1,0:T(8,128)} %copy-done.48) | copy-start | bytes 3145732
  964.1 46.9 %copy-start.68 = (bf16[256,1024]{1,0:T(8,128)(2,1)S(1)}, bf16[256,1024]{1,0:T(8,128)(2,1)}, u32[]{:S(2)}) copy-start(bf16[256,1024]{1,0:T(8,128)(2,1)} %reduce-scatter.21.cloned.1.call-done) | copy-start | bytes 1572868
  (134 other events, 384.6 us)
Sparse Core Ops, SparseCore 0:
  11.3 38.0 all-gather.8
  108.7 35.1 reduce-scatter.8
  147.4 35.3 all-gather.10
  196.0 35.1 reduce-scatter.10
  235.3 35.2 all-gather.12
  329.7 35.1 reduce-scatter.12
  368.4 35.3 all-gather.14
  405.7 35.2 all-gather.16
  453.0 35.1 reduce-scatter.14
  491.6 35.1 reduce-scatter.16
  531.8 35.2 all-gather.18
  673.3 35.1 reduce-scatter.18
  712.6 35.2 all-gather.20
  760.3 35.1 reduce-scatter.20
  799.9 35.3 all-gather.22
  934.1 35.1 reduce-scatter.22
  973.3 292.7 all-reduce.2
where the time goes:
time: 1310 us; the launch traced here: 1300 us
  waiting for transfers between devices  743 us (57%)
  matrix products  201 us (15%)
  local copies, waits for them, and re-layouts  135 us (10%)
  other arithmetic  110 us (8%)
  blocking collectives  76.9 us (6%)
  between operations  15.3 us (1%)
    psum x1, waiting for transfers between devices, per_device(): lax.psum(stacked[5].astype(jnp.bfloat16), 'dp').astype(jnp.float32)  253 us
    reduce_scatter x4, waiting for transfers between devices, branch_sum(): lax.psum_scatter(jnp.dot(operand, matrix, preferred_element_type=jnp.floa...  134 us
    all_gather x4, waiting for transfers between devices, gather_normed(): return lax.all_gather(normed, 'tensor', axis=0, tiled=True)  132 us
    all_gather x4, waiting for transfers between devices, gather_grads(): return lax.all_gather(gradient, 'tensor', axis=0, tiled=True)  115 us
    reduce_scatter x4, waiting for transfers between devices, input_sum(): lax.psum_scatter(contract_last(operand, matrix).astype(jnp.bfloat16), 'te...  109 us
    psum x1, blocking collectives, per_device(): stat_sums = lax.psum(jnp.stack(stat_terms), ('dp', 'tensor'))  40.8 us
    dot_general x8, matrix products, contract_last(): lax.dot_general(left_part, right_part, (((1,), (1,)), ((), ())), preferre...  39.4 us
    unnamed x245, local copies, waits for them, and re-layouts  38.3 us
  transfers between devices with their start and end apart: 17, of which 16 were waited for; matrix products, arithmetic and copies ran while one was open for 6% of the time, Pallas kernels for 0%

commit v1 on v0

--- a/solution.py
+++ b/solution.py
@@ -1,8 +1,12 @@
+import functools
 import math
+import types
 
 import jax
 import jax.numpy as jnp
 from jax import lax
+from jax.experimental import pallas as pl
+from jax.experimental.pallas import tpu as pltpu
 from jax.sharding import PartitionSpec as P
 
 HEADS = 8
@@ -441,9 +445,788 @@
     )
 
 
+SQUARE_MESH = {"dp": 8, "tensor": 4}
+
+
+F32 = jnp.float32
+BF16 = jnp.bfloat16
+MESH = pl.DeviceIdType.MESH
+VMEM_LIMIT = 60 * 2**20
+SUPER = 2
+
+
+def nn(a, b):
+    return lax.dot_general(a, b, (((1,), (0,)), ((), ())), preferred_element_type=F32)
+
+
+def nt(a, b):
+    return lax.dot_general(a, b, (((1,), (1,)), ((), ())), preferred_element_type=F32)
+
+
+def tn(a, b):
+    return lax.dot_general(a, b, (((0,), (0,)), ((), ())), preferred_element_type=F32)
+
+
+def exact(a, b, dims):
+    return lax.dot_general(a, b, (dims, ((), ())), precision=highest, preferred_element_type=F32)
+
+
+def aligned(index, size):
+    return pl.ds(pl.multiple_of(index, size), size)
+
+
+class Place:
+    def __init__(self):
+        self.dp = lax.axis_index("dp")
+        self.me = lax.axis_index("tensor")
+        self.low = lax.rem(self.me, 2)
+        self.high = self.me // 2
+
+    def member(self, step):
+        low = lax.rem(self.low + lax.rem(step, 2), 2)
+        high = lax.rem(self.high + step // 2, 2)
+        return 2 * high + low
+
+    def device(self, step):
+        return (self.dp, self.member(step))
+
+    def greet(self):
+        barrier = pltpu.get_barrier_semaphore()
+        for step in (1, 2, 3):
+            pl.semaphore_signal(barrier, inc=1, device_id=self.device(step), device_id_type=MESH)
+        pl.semaphore_wait(barrier, 3)
+
+
+class Wire:
+    def __init__(self, place, step, send_sem, recv_sem, source, target, landing):
+        self.source, self.target, self.landing = source, target, landing
+        self.common = dict(
+            send_sem=send_sem, recv_sem=recv_sem, device_id=place.device(step), device_id_type=MESH
+        )
+
+    def out(self):
+        return pltpu.make_async_remote_copy(src_ref=self.source, dst_ref=self.target, **self.common)
+
+    def start(self):
+        self.out().start()
+
+    def wait_recv(self):
+        pltpu.make_async_remote_copy(src_ref=self.landing, dst_ref=self.landing, **self.common).wait_recv()
+
+    def wait_send(self):
+        self.out().wait_send()
+
+
+class Gather:
+    def __init__(self, place, buf, send, recv, block):
+        self.place, self.buf, self.block = place, buf, block
+        self.send, self.recv = send, recv
+        self.half = block // (2 * SUPER)
+
+    def rows(self, step, part, half):
+        start = self.place.member(step) * self.block + (2 * part + half) * self.half
+        return self.buf.at[aligned(start, self.half)]
+
+    def wire(self, part, number):
+        step, owner, half = ((1, 0, 0), (2, 0, 1), (1, 0, 1), (2, 0, 0), (2, 1, 0), (1, 2, 1))[number]
+        source = self.rows(owner, part, half)
+        landing = self.rows((0, 1, 2, 3)[owner ^ step], part, half)
+        return Wire(self.place, step, self.send.at[part, number], self.recv.at[part, number], source, source, landing)
+
+    def start(self, part):
+        for number in range(4):
+            self.wire(part, number).start()
+
+    def forward(self, part):
+        self.wire(part, 0).wait_recv()
+        self.wire(part, 4).start()
+        self.wire(part, 1).wait_recv()
+        self.wire(part, 5).start()
+
+    def finish(self, part, step):
+        for number in {0: (), 1: (2,), 2: (3,), 3: (4, 5)}[step]:
+            self.wire(part, number).wait_recv()
+
+    def drain(self):
+        for part in range(SUPER):
+            for number in range(6):
+                self.wire(part, number).wait_send()
+
+
+class Scatter:
+    def __init__(self, place, buf, land, send, recv, block):
+        self.place, self.buf, self.land, self.block = place, buf, land, block
+        self.send, self.recv = send, recv
+        self.half = block // (2 * SUPER)
+
+    def rows(self, step, part, half):
+        start = self.place.member(step) * self.block + (2 * part + half) * self.half
+        return aligned(start, self.half)
+
+    def wire(self, part, number):
+        step, owner, half = ((1, 3, 0), (1, 1, 0), (2, 3, 1), (2, 2, 1), (2, 2, 0), (1, 1, 1))[number]
+        target = self.land.at[part, number]
+        return Wire(
+            self.place, step, self.send.at[part, number], self.recv.at[part, number],
+            self.buf.at[self.rows(owner, part, half)], target, target,
+        )
+
+    def send_block(self, part, step):
+        for number in {0: (), 1: (1,), 2: (3,), 3: (0, 2)}[step]:
+            self.wire(part, number).start()
+
+    def middle(self, part):
+        for first, second, owner, half in ((0, 4, 2, 0), (2, 5, 1, 1)):
+            self.wire(part, first).wait_recv()
+            rows = self.rows(owner, part, half)
+            self.buf[rows, :] = (
+                self.buf[rows, :].astype(F32) + self.land[part, first].astype(F32)
+            ).astype(BF16)
+            self.wire(part, second).start()
+
+    def finish(self, part, half):
+        first, second = ((1, 4), (3, 5))[half]
+        self.wire(part, first).wait_recv()
+        self.wire(part, second).wait_recv()
+
+    def total(self, part, half, start, count):
+        first, second = ((1, 4), (3, 5))[half]
+        own = self.place.me * self.block + (2 * part + half) * self.half + start
+        rows = pl.ds(start, count)
+        return (
+            self.buf[aligned(own, count), :].astype(F32)
+            + self.land[part, first, rows, :].astype(F32)
+            + self.land[part, second, rows, :].astype(F32)
+        )
+
+    def drain(self):
+        for part in range(SUPER):
+            for number in range(6):
+                self.wire(part, number).wait_send()
+
+
+class Share:
+    def __init__(self, place, mine, land, send, recv):
+        self.wires = [
+            Wire(place, step, send.at[step - 1], recv.at[step - 1], mine, land.at[step - 1], land.at[step - 1])
+            for step in (1, 2, 3)
+        ]
+        self.mine, self.land = mine, land
+
+    def start(self):
+        for wire in self.wires:
+            wire.start()
+
+    def total(self):
+        for wire in self.wires:
+            wire.wait_recv()
+        return self.mine[...] + self.land[0] + self.land[1] + self.land[2]
+
+    def drain(self):
+        for wire in self.wires:
+            wire.wait_send()
+
+
+class Local:
+    def __init__(self, sems):
+        self.sems, self.used = sems, 0
+
+    def start(self, source, target):
+        copy = pltpu.make_async_copy(source, target, self.sems.at[self.used])
+        self.used += 1
+        copy.start()
+        return copy
+
+
+def row_sums(values, target, chunk):
+    sums = exact(jnp.ones((8, values.shape[1]), F32), values, ((1,), (1,)))
+    target[pl.ds(chunk, 1), :] = sums[0:1, :]
+
+
+def spread(sums, chunk):
+    picked = (lax.broadcasted_iota(jnp.int32, (8, 128), 0) == chunk).astype(F32)
+    return exact(sums, picked, ((0,), (0,)))
+
+
+def widen(columns, times):
+    return jnp.concatenate([columns] * times, axis=1)
+
+
+def decay_tiles(dec_ref, tiles, heads_here, size):
+    rows = lax.broadcasted_iota(jnp.int32, (size, size), 0)
+    cols = lax.broadcasted_iota(jnp.int32, (size, size), 1)
+    distance = (rows - cols).astype(F32)
+    for head in range(heads_here):
+        decay = dec_ref[head : head + 1, 0:1]
+        tiles[head, 0] = jnp.where(rows >= cols, jnp.exp(decay * jnp.maximum(distance, 0.0)), 0.0)
+        tiles[head, 1] = jnp.exp(decay * (distance + float(size)))
+
+
+def tile_weight(dec_ref, tiles, segc_ref, segr_ref, head, row_tile, col_tile, size):
+    gap = row_tile - col_tile
+    if gap == 0:
+        weight = tiles[head, 0]
+    else:
+        weight = tiles[head, 1]
+        if gap > 1:
+            weight = weight * jnp.exp(dec_ref[pl.ds(head, 1), 0:1] * float(size * (gap - 1)))
+    row_seg = widen(segc_ref[row_tile * size : (row_tile + 1) * size, :], size // 128)
+    col_seg = segr_ref[0:1, col_tile * size : (col_tile + 1) * size]
+    return jnp.where(row_seg == col_seg, weight, 0.0)
+
+
+def namespace(names, refs):
+    return types.SimpleNamespace(**dict(zip(names, refs)))
+
+
+def fwd_kernel(cfg, names, *refs):
+    r = namespace(names, refs)
+    layer, block, length, width, local = cfg.layer, cfg.block, cfg.length, cfg.width, cfg.local
+    heads_here, size = cfg.heads_here, cfg.block
+    place = Place()
+    copies = Local(r.local_sem)
+    w_in = [copies.start(h.at[layer], v) for h, v in (
+        (r.wq_h, r.wq), (r.wk_h, r.wk), (r.wv_h, r.wv), (r.wg_h, r.wg))]
+    w_out = copies.start(r.wo_h.at[layer], r.wo)
+    w_glu = [copies.start(h.at[layer], v) for h, v in ((r.wl_h, r.wl), (r.wr_h, r.wr), (r.wd_h, r.wd))]
+    saves = []
+    first = Gather(place, r.n1, r.ag1_send, r.ag1_recv, block)
+    mid_sum = Scatter(place, r.part1, r.land1, r.rs1_send, r.rs1_recv, block)
+    second = Gather(place, r.n2, r.ag2_send, r.ag2_recv, block)
+    out_sum = Scatter(place, r.part2, r.land2, r.rs2_send, r.rs2_recv, block)
+    share = Share(place, r.ss, r.ss_land, r.ss_send, r.ss_recv)
+    half, step_rows = first.half, 32
+    own_start = place.me * block
+
+    @pl.loop(0, block // step_rows)
+    def _(i):
+        rows = aligned(i * step_rows, step_rows)
+        v = r.x[rows, :]
+        scale = lax.rsqrt(jnp.mean(v * v, axis=1, keepdims=True) + epsilon)
+        r.n1[aligned(own_start + i * step_rows, step_rows), :] = (v * scale).astype(BF16)
+
+    place.greet()
+    for part in range(SUPER):
+        first.start(part)
+    decay_tiles(r.dec, r.tiles, heads_here, size)
+    for copy in w_in:
+        copy.wait()
+
+    @pl.loop(0, 4)
+    def _(step):
+        @pl.when(step == 1)
+        def _():
+            for part in range(SUPER):
+                first.forward(part)
+        for which in (1, 2, 3):
+            @pl.when(step == which)
+            def _():
+                for part in range(SUPER):
+                    first.finish(part, which)
+        rows = aligned(place.member(step) * block, block)
+        a = r.n1[rows, :]
+        cosine, sine = r.cos[rows, :], r.sin[rows, :]
+        for w, lin, rot in ((r.wq, r.ql, r.q), (r.wk, r.kl, r.k)):
+            v = nn(a, w[...])
+            lin[rows, :] = v.astype(BF16)
+            v = v / (1.0 + jnp.exp(-v))
+            for head in range(heads_here):
+                one = v[:, head * HDIM : (head + 1) * HDIM]
+                rot[rows, 2 * head * HDIM : (2 * head + 1) * HDIM] = (one * cosine).astype(BF16)
+                rot[rows, (2 * head + 1) * HDIM : (2 * head + 2) * HDIM] = (one * sine).astype(BF16)
+        r.v[rows, :] = nn(a, r.wv[...]).astype(BF16)
+        r.gate[rows, :] = nn(a, r.wg[...])
+
+    for v, h in ((r.n1, r.n1_h), (r.ql, r.ql_h), (r.kl, r.kl_h), (r.q, r.q_h), (r.k, r.k_h), (r.v, r.v_h), (r.gate, r.gate_h)):
+        saves.append(copies.start(v, h))
+
+    tiles_here = length // size
+
+    @pl.loop(0, heads_here)
+    def _(head):
+        wide = aligned(head * 2 * HDIM, 2 * HDIM)
+        thin = aligned(head * HDIM, HDIM)
+        for row_tile in range(tiles_here):
+            rows = slice(row_tile * size, (row_tile + 1) * size)
+            queries = r.q[rows, wide]
+            acc = None
+            for col_tile in range(row_tile + 1):
+                cols = slice(col_tile * size, (col_tile + 1) * size)
+                weight = tile_weight(r.dec, r.tiles, r.segc, r.segr, head, row_tile, col_tile, size)
+                scores = (nt(queries, r.k[cols, wide]) * weight).astype(BF16)
+                term = nn(scores, r.v[cols, thin])
+                acc = term if acc is None else acc + term
+            r.heads[rows, thin] = acc
+            r.u[rows, thin] = (acc * r.gate[rows, thin]).astype(BF16)
+
+    for chunk in range(length // 128):
+        v = r.heads[chunk * 128 : (chunk + 1) * 128, :]
+        row_sums(v * v, r.ss, chunk)
+    share.start()
+    saves.append(copies.start(r.heads, r.heads_h))
+    w_out.wait()
+
+    part_rows = 2 * half
+    for part in range(SUPER):
+        for step in (3, 1, 2, 0):
+            rows = aligned(place.member(step) * block + part * part_rows, part_rows)
+            r.part1[rows, :] = nn(r.u[rows, :], r.wo[...]).astype(BF16)
+            mid_sum.send_block(part, step)
+    for part in range(SUPER):
+        mid_sum.middle(part)
+    r.sstot[...] = share.total()
+    saves.append(copies.start(r.sstot, r.ss_h))
+    scaling = lax.rsqrt(r.sstot[...] / width + epsilon)
+    per_block = block // 128
+    for chunk in range(per_block):
+        r.scale[chunk * 128 : (chunk + 1) * 128, :] = spread(scaling, place.me * per_block + chunk)
+    r.stat[...] = jnp.zeros_like(r.stat)
+
+    def add_stat(row, v):
+        sums = jnp.sum(v * v, axis=0, keepdims=True)
+        r.stat[row : row + 1, :] += sums
+
+    step_rows = min(32, half)
+    for part in range(SUPER):
+        for h in range(2):
+            mid_sum.finish(part, h)
+            for i in range(half // step_rows):
+                offset = (2 * part + h) * half + i * step_rows
+                scale = widen(r.scale[offset : offset + step_rows, :], width // 128)
+                attn = mid_sum.total(part, h, i * step_rows, step_rows) * scale
+                middle = r.x[offset : offset + step_rows, :] + attn
+                r.mid[offset : offset + step_rows, :] = middle
+                add_stat(0, attn)
+                norm = lax.rsqrt(jnp.mean(middle * middle, axis=1, keepdims=True) + epsilon)
+                r.n2[aligned(own_start + offset, step_rows), :] = (middle * norm).astype(BF16)
+        second.start(part)
+    saves.append(copies.start(r.mid, r.mid_h))
+    for copy in w_glu:
+        copy.wait()
+    for part in range(SUPER):
+
+        def glu(step):
+            rows = aligned(place.member(step) * block + part * part_rows, part_rows)
+            a = r.n2[rows, :]
+            left = nn(a, r.wl[...])
+            right = nn(a, r.wr[...])
+            hidden = (left * right).astype(BF16)
+            r.left[rows, :] = left.astype(BF16)
+            r.right[rows, :] = right.astype(BF16)
+            r.hid[rows, :] = hidden
+            r.part2[rows, :] = nn(hidden, r.wd[...]).astype(BF16)
+
+        @pl.loop(0, 4)
+        def _(step):
+            if part == 0:
+                @pl.when(step == 1)
+                def _():
+                    for other in range(SUPER):
+                        second.forward(other)
+            for which in (1, 2, 3):
+                @pl.when(step == which)
+                def _():
+                    second.finish(part, which)
+            glu(step)
+            for which in (1, 2, 3):
+                @pl.when(step == which)
+                def _():
+                    out_sum.send_block(part, which)
+    for v, h in ((r.n2, r.n2_h), (r.left, r.left_h), (r.right, r.right_h), (r.hid, r.hid_h)):
+        saves.append(copies.start(v, h))
+    for part in range(SUPER):
+        out_sum.middle(part)
+    for part in range(SUPER):
+        for h in range(2):
+            out_sum.finish(part, h)
+            for i in range(half // step_rows):
+                offset = (2 * part + h) * half + i * step_rows
+                glu_rows = out_sum.total(part, h, i * step_rows, step_rows)
+                after = r.mid[offset : offset + step_rows, :] + glu_rows
+                r.xo[offset : offset + step_rows, :] = after
+                add_stat(1, glu_rows)
+                add_stat(2, after)
+    for copy in saves:
+        copy.wait()
+    for group in (first, mid_sum, second, out_sum, share):
+        group.drain()
+
+
+def bwd_kernel(cfg, names, *refs):
+    r = namespace(names, refs)
+    layer, block, length, width, local = cfg.layer, cfg.block, cfg.length, cfg.width, cfg.local
+    heads_here, size = cfg.heads_here, cfg.block
+    place = Place()
+    copies = Local(r.local_sem)
+    load_glu = [copies.start(s, v) for s, v in (
+        (r.wd_h.at[layer], r.wd), (r.left_h, r.left), (r.right_h, r.right),
+        (r.wl_h.at[layer], r.wl), (r.wr_h.at[layer], r.wr))]
+    load_glu_grad = [copies.start(r.hid_h, r.hid), copies.start(r.n2_h, r.n2)]
+    load_out = [copies.start(s, v) for s, v in (
+        (r.ss_h, r.sstot), (r.wo_h.at[layer], r.wo), (r.gate_h, r.gate), (r.heads_h, r.heads))]
+    load_attn = [copies.start(s, v) for s, v in (
+        (r.q_h, r.q), (r.k_h, r.k), (r.v_h, r.v), (r.ql_h, r.ql), (r.kl_h, r.kl))]
+    load_in = [copies.start(s, v) for s, v in (
+        (r.wq_h.at[layer], r.wq), (r.wk_h.at[layer], r.wk), (r.wv_h.at[layer], r.wv),
+        (r.wg_h.at[layer], r.wg))]
+    load_in_grad = [copies.start(r.n1_h, r.n1)]
+    saves = []
+    first = Gather(place, r.gd, r.ag1_send, r.ag1_recv, block)
+    mid_sum = Scatter(place, r.part1, r.land1, r.rs1_send, r.rs1_recv, block)
+    second = Gather(place, r.ga, r.ag2_send, r.ag2_recv, block)
+    in_sum = Scatter(place, r.part2, r.land2, r.rs2_send, r.rs2_recv, block)
+    share = Share(place, r.inner, r.inner_land, r.in_send, r.in_recv)
+    half = first.half
+    part_rows = 2 * half
+    own_start = place.me * block
+    step_rows = min(32, half)
+
+    @pl.loop(0, block // 32)
+    def _(i):
+        rows = aligned(i * 32, 32)
+        r.gd[aligned(own_start + i * 32, 32), :] = r.g[rows, :].astype(BF16)
+
+    place.greet()
+    for part in range(SUPER):
+        first.start(part)
+    decay_tiles(r.dec, r.tiles, heads_here, size)
+    for copy in load_glu:
+        copy.wait()
+    for copy in load_out:
+        copy.wait()
+    scaling = lax.rsqrt(r.sstot[...] / width + epsilon)
+    for chunk in range(length // 128):
+        r.scale[chunk * 128 : (chunk + 1) * 128, :] = spread(scaling, chunk)
+
+    for part in range(SUPER):
+        @pl.loop(0, 4)
+        def _(step):
+            if part == 0:
+                @pl.when(step == 1)
+                def _():
+                    for other in range(SUPER):
+                        first.forward(other)
+            for which in (1, 2, 3):
+                @pl.when(step == which)
+                def _():
+                    first.finish(part, which)
+            rows = aligned(place.member(step) * block + part * part_rows, part_rows)
+            grad_hidden = nt(r.gd[rows, :], r.wd[...])
+            grad_left = (grad_hidden * r.right[rows, :].astype(F32)).astype(BF16)
+            grad_right = (grad_hidden * r.left[rows, :].astype(F32)).astype(BF16)
+            r.dl[rows, :] = grad_left
+            r.dr[rows, :] = grad_right
+            r.part1[rows, :] = (nt(grad_left, r.wl[...]) + nt(grad_right, r.wr[...])).astype(BF16)
+            for which in (1, 2, 3):
+                @pl.when(step == which)
+                def _():
+                    mid_sum.send_block(part, which)
+
+    for copy in load_glu_grad:
+        copy.wait()
+    for n in range(width // 256):
+        cols = slice(n * 256, (n + 1) * 256)
+        r.down_g[:, cols] = tn(r.hid[...], r.gd[:, cols]).astype(BF16)
+    saves.append(copies.start(r.down_g, r.down_o))
+    for part in range(SUPER):
+        mid_sum.middle(part)
+    for n in range(width // 256):
+        cols = slice(n * 256, (n + 1) * 256)
+        r.left_g[cols, :] = tn(r.n2[:, cols], r.dl[...]).astype(BF16)
+    saves.append(copies.start(r.left_g, r.left_o))
+
+    def back_rows(total, values_ref, grad_ref, offset):
+        values = values_ref[offset : offset + step_rows, :]
+        norm = lax.rsqrt(jnp.mean(values * values, axis=1, keepdims=True) + epsilon)
+        m = values * norm
+        inner = jnp.mean(total * m, axis=1, keepdims=True)
+        return grad_ref[offset : offset + step_rows, :] + norm * (total - m * inner)
+
+    for part in range(SUPER):
+        for h in range(2):
+            mid_sum.finish(part, h)
+            for i in range(half // step_rows):
+                offset = (2 * part + h) * half + i * step_rows
+                total = mid_sum.total(part, h, i * step_rows, step_rows)
+                new = back_rows(total, r.mid, r.g, offset)
+                r.gm[offset : offset + step_rows, :] = new
+                r.ga[aligned(own_start + offset, step_rows), :] = new.astype(BF16)
+        second.start(part)
+    for n in range(width // 256):
+        cols = slice(n * 256, (n + 1) * 256)
+        r.right_g[cols, :] = tn(r.n2[:, cols], r.dr[...]).astype(BF16)
+    saves.append(copies.start(r.right_g, r.right_o))
+
+    per_block = block // 128
+
+    @pl.loop(0, 4)
+    def _(step):
+        @pl.when(step == 1)
+        def _():
+            for part in range(SUPER):
+                second.forward(part)
+        for which in (1, 2, 3):
+            @pl.when(step == which)
+            def _():
+                for part in range(SUPER):
+                    second.finish(part, which)
+        member = place.member(step)
+        for chunk in range(per_block):
+            rows = aligned(member * block + chunk * 128, 128)
+            grad_branch = nt(r.ga[rows, :], r.wo[...])
+            gate = r.gate[rows, :]
+            normed = r.heads[rows, :] * widen(r.scale[rows, :], local // 128)
+            grad_normed = grad_branch * gate
+            r.gn[rows, :] = grad_normed
+            r.dx[rows, 3 * local : 4 * local] = (grad_branch * normed).astype(BF16)
+            r.branch[rows, :] = (normed * gate).astype(BF16)
+            row_sums(grad_normed * normed, r.inner, member * per_block + chunk)
+    share.start()
+    r.out_g[...] = tn(r.branch[...], r.ga[...]).astype(BF16)
+    saves.append(copies.start(r.out_g, r.out_o))
+    for copy in load_attn:
+        copy.wait()
+    r.intot[...] = share.total() / width
+    for chunk in range(length // 128):
+        rows = slice(chunk * 128, (chunk + 1) * 128)
+        scale = widen(r.scale[rows, :], local // 128)
+        inner = widen(spread(r.intot[...], chunk), local // 128)
+        normed = r.heads[rows, :] * scale
+        r.dh[rows, :] = (scale * (r.gn[rows, :] - normed * inner)).astype(BF16)
+
+    tiles_here = length // size
+
+    @pl.loop(0, heads_here)
+    def _(head):
+        wide = aligned(head * 2 * HDIM, 2 * HDIM)
+        thin = aligned(head * HDIM, HDIM)
+        for col_tile in range(tiles_here):
+            cols = slice(col_tile * size, (col_tile + 1) * size)
+            keys = r.k[cols, wide]
+            values = r.v[cols, thin]
+            acc_key, acc_value = None, None
+            for row_tile in range(col_tile, tiles_here):
+                rows = slice(row_tile * size, (row_tile + 1) * size)
+                queries = r.q[rows, wide]
+                grads = r.dh[rows, thin]
+                weight = tile_weight(r.dec, r.tiles, r.segc, r.segr, head, row_tile, col_tile, size)
+                scores = (nt(queries, keys) * weight).astype(BF16)
+                pulled = (nt(grads, values) * weight).astype(BF16)
+                term = nn(pulled, keys)
+                if col_tile == 0:
+                    r.dq[rows, :] = term
+                else:
+                    r.dq[rows, :] += term
+                key_term = tn(pulled, queries)
+                value_term = tn(scores, grads)
+                acc_key = key_term if acc_key is None else acc_key + key_term
+                acc_value = value_term if acc_value is None else acc_value + value_term
+            r.dk[cols, :] = acc_key
+            r.dx[cols, aligned(2 * local + head * HDIM, HDIM)] = acc_value.astype(BF16)
+        for row_tile in range(tiles_here):
+            rows = slice(row_tile * size, (row_tile + 1) * size)
+            cosine, sine = r.cos[rows, :], r.sin[rows, :]
+            for grad, lin, base in ((r.dq, r.ql, 0), (r.dk, r.kl, local)):
+                v = lin[rows, thin].astype(F32)
+                gate = 1.0 / (1.0 + jnp.exp(-v))
+                back = grad[rows, :HDIM] * cosine + grad[rows, HDIM:] * sine
+                back = back * (gate + v * gate * (1.0 - gate))
+                r.dx[rows, aligned(base + head * HDIM, HDIM)] = back.astype(BF16)
+
+    for copy in load_in:
+        copy.wait()
+    weights = (r.wq, r.wk, r.wv, r.wg)
+    for part in range(SUPER):
+        for step in (3, 1, 2, 0):
+            rows = aligned(place.member(step) * block + part * part_rows, part_rows)
+            total = None
+            for n, w in enumerate(weights):
+                term = nt(r.dx[rows, n * local : (n + 1) * local], w[...])
+                total = term if total is None else total + term
+            r.part2[rows, :] = total.astype(BF16)
+            in_sum.send_block(part, step)
+    for copy in load_in_grad:
+        copy.wait()
+
+    def attn_grad(n):
+        cols = slice(n * local, (n + 1) * local)
+        r.attn_g[n] = tn(r.n1[...], r.dx[:, cols]).astype(BF16)
+        saves.append(copies.start(r.attn_g.at[n], r.attn_o.at[n]))
+
+    attn_grad(0)
+    attn_grad(1)
+    for part in range(SUPER):
+        in_sum.middle(part)
+    attn_grad(2)
+    attn_grad(3)
+    for part in range(SUPER):
+        for h in range(2):
+            in_sum.finish(part, h)
+            for i in range(half // step_rows):
+                offset = (2 * part + h) * half + i * step_rows
+                total = in_sum.total(part, h, i * step_rows, step_rows)
+                r.go[offset : offset + step_rows, :] = back_rows(total, r.x, r.gm, offset)
+    for copy in saves:
+        copy.wait()
+    for group in (first, mid_sum, second, in_sum, share):
+        group.drain()
+
+
+def call_kernel(body, cfg, inputs, outputs, scratch, collective_id, name):
+    vmem, anywhere = pl.BlockSpec(memory_space=pltpu.VMEM), pl.BlockSpec(memory_space=pl.ANY)
+    names = list(inputs) + list(outputs) + list(scratch)
+    result = pl.pallas_call(
+        functools.partial(body, cfg, names),
+        out_shape=[shape for shape, _ in outputs.values()],
+        in_specs=[vmem if placed else anywhere for _, placed in inputs.values()],
+        out_specs=[vmem if placed else anywhere for _, placed in outputs.values()],
+        scratch_shapes=list(scratch.values()),
+        compiler_params=pltpu.CompilerParams(
+            collective_id=collective_id, has_side_effects=True, vmem_limit_bytes=VMEM_LIMIT
+        ),
+        name=name,
+    )(*[array for array, _ in inputs.values()])
+    return dict(zip(outputs, result))
+
+
+def collective_scratch(cfg):
+    dma = pltpu.SemaphoreType.DMA
+    half = cfg.block // (2 * SUPER)
+    out = {}
+    for name in ("ag1", "ag2", "rs1", "rs2"):
+        out[name + "_send"] = dma((SUPER, 6))
+        out[name + "_recv"] = dma((SUPER, 6))
+    out["land1"] = pltpu.VMEM((SUPER, 6, half, cfg.width), BF16)
+    out["land2"] = pltpu.VMEM((SUPER, 6, half, cfg.width), BF16)
+    out["part1"] = pltpu.VMEM((cfg.length, cfg.width), BF16)
+    out["part2"] = pltpu.VMEM((cfg.length, cfg.width), BF16)
+    out["local_sem"] = dma((40,))
+    return out
+
+
+def weight_scratch(cfg):
+    v = pltpu.VMEM
+    return {
+        "wq": v((cfg.width, cfg.local), BF16), "wk": v((cfg.width, cfg.local), BF16),
+        "wv": v((cfg.width, cfg.local), BF16), "wg": v((cfg.width, cfg.local), BF16),
+        "wo": v((cfg.local, cfg.width), BF16), "wl": v((cfg.width, cfg.ff), BF16),
+        "wr": v((cfg.width, cfg.ff), BF16), "wd": v((cfg.ff, cfg.width), BF16),
+    }
+
+
+def run_forward(cfg, x, tables, weights):
+    v, dma, s = pltpu.VMEM, pltpu.SemaphoreType.DMA, jax.ShapeDtypeStruct
+    rows, wide, local, ff, block = cfg.length, cfg.width, cfg.local, cfg.ff, cfg.block
+    inputs = {"x": (x, True), **{k: (a, True) for k, a in tables.items()}, **{k + "_h": (a, False) for k, a in weights.items()}}
+    kept = {
+        "n1": ((rows, wide), BF16), "ql": ((rows, local), BF16), "kl": ((rows, local), BF16),
+        "q": ((rows, 2 * local), BF16), "k": ((rows, 2 * local), BF16), "v": ((rows, local), BF16),
+        "gate": ((rows, local), F32), "heads": ((rows, local), F32), "mid": ((block, wide), F32),
+        "n2": ((rows, wide), BF16), "left": ((rows, ff), BF16), "right": ((rows, ff), BF16), "hid": ((rows, ff), BF16),
+    }
+    outputs = {
+        "xo": (s((block, wide), F32), True), "stat": (s((8, wide), F32), True), "ss_h": (s((8, 128), F32), False),
+        **{k + "_h": (s(*a), False) for k, a in kept.items()},
+    }
+    scratch = {
+        **weight_scratch(cfg), **collective_scratch(cfg), **{k: v(*a) for k, a in kept.items()},
+        "tiles": v((cfg.heads_here, 2, block, block), F32), "u": v((rows, local), BF16),
+        "ss": v((8, 128), F32), "sstot": v((8, 128), F32), "scale": v((block, 128), F32),
+        "ss_land": v((3, 8, 128), F32), "ss_send": dma((3,)), "ss_recv": dma((3,)),
+    }
+    return call_kernel(fwd_kernel, cfg, inputs, outputs, scratch, 2 * cfg.layer, "layer_forward")
+
+
+def run_backward(cfg, g, x, saved, tables, weights):
+    v, dma, s = pltpu.VMEM, pltpu.SemaphoreType.DMA, jax.ShapeDtypeStruct
+    rows, wide, local, ff, block = cfg.length, cfg.width, cfg.local, cfg.ff, cfg.block
+    inputs = {
+        "g": (g, True), "x": (x, True), "mid": (saved["mid_h"], True),
+        **{k: (a, True) for k, a in tables.items()}, **{k + "_h": (a, False) for k, a in weights.items()},
+        **{k: (saved[k], False) for k in ("ss_h", "n1_h", "ql_h", "kl_h", "q_h", "k_h", "v_h", "gate_h", "heads_h", "n2_h", "left_h", "right_h", "hid_h")},
+    }
+    outputs = {
+        "go": (s((block, wide), F32), True), "attn_o": (s((4, wide, local), BF16), False),
+        "out_o": (s((local, wide), BF16), False), "left_o": (s((wide, ff), BF16), False),
+        "right_o": (s((wide, ff), BF16), False), "down_o": (s((ff, wide), BF16), False),
+    }
+    scratch = {
+        **weight_scratch(cfg), **collective_scratch(cfg),
+        "n1": v((rows, wide), BF16), "ql": v((rows, local), BF16), "kl": v((rows, local), BF16),
+        "q": v((rows, 2 * local), BF16), "k": v((rows, 2 * local), BF16), "v": v((rows, local), BF16),
+        "gate": v((rows, local), F32), "heads": v((rows, local), F32), "n2": v((rows, wide), BF16),
+        "left": v((rows, ff), BF16), "right": v((rows, ff), BF16), "hid": v((rows, ff), BF16),
+        "gd": v((rows, wide), BF16), "ga": v((rows, wide), BF16), "gm": v((block, wide), F32),
+        "dl": v((rows, ff), BF16), "dr": v((rows, ff), BF16), "gn": v((rows, local), F32),
+        "dh": v((rows, local), BF16), "branch": v((rows, local), BF16), "dx": v((rows, 4 * local), BF16),
+        "dq": v((rows, 2 * HDIM), F32), "dk": v((rows, 2 * HDIM), F32),
+        "attn_g": v((4, wide, local), BF16), "out_g": v((local, wide), BF16), "left_g": v((wide, ff), BF16),
+        "right_g": v((wide, ff), BF16), "down_g": v((ff, wide), BF16),
+        "tiles": v((cfg.heads_here, 2, block, block), F32), "scale": v((rows, 128), F32),
+        "sstot": v((8, 128), F32), "inner": v((8, 128), F32), "intot": v((8, 128), F32),
+        "inner_land": v((3, 8, 128), F32), "in_send": dma((3,)), "in_recv": dma((3,)),
+    }
+    return call_kernel(bwd_kernel, cfg, inputs, outputs, scratch, 2 * cfg.layer + 1, "layer_backward")
+
+
+def per_device_square(
+    tokens, upstream, segment_ids, query_proj, key_proj, value_proj, gate_proj, output_proj, left_proj, right_proj, down_proj
+):
+    layers = query_proj.shape[0]
+    block, width = tokens.shape
+    length = segment_ids.shape[0]
+    local, ff = query_proj.shape[2], left_proj.shape[2]
+    heads_here = local // HDIM
+    positions = jnp.arange(length, dtype=F32)
+    frequency = jnp.exp(-math.log(10000.0) * jnp.arange(HDIM, dtype=F32) / HDIM)
+    angles = positions[:, None] * frequency[None, :]
+    head_index = (lax.axis_index("tensor") * heads_here + jnp.arange(heads_here)).astype(F32)
+    slopes = jnp.exp2(-8.0 * (head_index + 1.0) / HEADS)
+    fixed = {
+        "cos": jnp.cos(angles), "sin": jnp.sin(angles),
+        "segc": jnp.broadcast_to(segment_ids[:, None], (length, 128)),
+        "segr": jnp.broadcast_to(segment_ids[None, :], (8, length)),
+    }
+    weights = {
+        "wq": query_proj, "wk": key_proj, "wv": value_proj, "wg": gate_proj,
+        "wo": output_proj, "wl": left_proj, "wr": right_proj, "wd": down_proj,
+    }
+    current = tokens.astype(F32)
+    runs = []
+    for layer in range(layers):
+        cfg = types.SimpleNamespace(
+            layer=layer, block=block, length=length, width=width, local=local, ff=ff, heads_here=heads_here
+        )
+        decay = -slopes * (1.0 - depth_start - depth_step * layer)
+        decay = jnp.concatenate([decay, jnp.zeros((8 - heads_here,), F32)])
+        tables = {**fixed, "dec": jnp.broadcast_to(decay[:, None], (8, 128))}
+        saved = run_forward(cfg, current, tables, weights)
+        runs.append((cfg, current, tables, saved))
+        current = saved["xo"]
+    stats = jnp.stack([jnp.sum(run[3]["stat"][:3], axis=1) for run in runs])
+    stat_sums = lax.psum(stats, ("dp", "tensor"))
+    rms_stats = jnp.sqrt(stat_sums / (length * lax.axis_size("dp") * width))
+    final_rows = current.astype(BF16)
+    gradient = upstream.astype(F32)
+    grads = [None] * layers
+    for layer in reversed(range(layers)):
+        cfg, x, tables, saved = runs[layer]
+        back = run_backward(cfg, gradient, x, saved, tables, weights)
+        gradient = back["go"]
+        grads[layer] = [back["attn_o"][0], back["attn_o"][1], back["attn_o"][2], back["attn_o"][3],
+                        back["out_o"], back["left_o"], back["right_o"], back["down_o"]]
+    totals = []
+    for member in range(8):
+        stacked = jnp.stack([grads[layer][member] for layer in range(layers)])
+        totals.append(lax.psum(stacked, "dp").astype(F32))
+    return (final_rows, gradient.astype(BF16), *totals, rms_stats)
+
+
 def solution(mesh):
+    square = dict(mesh.shape) == SQUARE_MESH
+    body = per_device_square if square else per_device
     return jax.shard_map(
-        per_device,
+        body,
         mesh=mesh,
         in_specs=(
             P(("dp", "tensor"), None),

time: 1310 us -> 697 us (0.53)
  waiting for transfers between devices: 743 us -> 249 us
  Pallas kernels: 0 us -> 324 us
  matrix products: 201 us -> 0 us
  local copies, waits for them, and re-layouts: 135 us -> 25.5 us
  other arithmetic: 110 us -> 33.5 us
  blocking collectives: 76.9 us -> 40.6 us
    pallas_call x0 -> x4, Pallas kernels: none -> 324 us  [call_kernel(): pl.pallas_call(functools.partial(body, cfg, names), out_shape=[shape for...]
    all_gather x8 -> x0, waiting for transfers between devices: 247 us -> none  [the longest x4 132 us: gather_normed(): return lax.all_gather(normed, 'tensor', axis=0, tiled=True)]
    reduce_scatter x8 -> x0, waiting for transfers between devices: 243 us -> none  [the longest x4 134 us: branch_sum(): lax.psum_scatter(jnp.dot(operand, matrix, preferred_element_type=jnp.floa...]
    dot_general x76 -> x0, matrix products: 201 us -> none  [the longest x8 39.4 us: contract_last(): lax.dot_general(left_part, right_part, (((1,), (1,)), ((), ())), preferre...]
    psum x5 -> x1, blocking collectives: 76.9 us -> 40.6 us  [per_device_square(): stat_sums = lax.psum(stats, ('dp', 'tensor'))]
    dynamic_update_slice x12 -> x0, local copies, waits for them, and re-layouts: 26.9 us -> none  [attend_backward(): lax.scan(retreat, zero_state, (split_blocks(queries, block_count), split_...]
    another operation x16 -> x0, local copies, waits for them, and re-layouts: 21.1 us -> none  [the longest x4 9.43 us: split_blocks(): return array.reshape((block_count, BLK) + array.shape[1:])]
    convert_element_type x19 -> x10, other arithmetic: 37.9 us -> 18.8 us  [the longest x6 13.9 us: per_device_square(): totals.append(lax.psum(stacked, 'dp').astype(F32))]
  transfers between devices with their start and end apart: 17 -> 1, of which waited for: 16 -> 1; matrix products, arithmetic and copies ran while one was open for 6% -> 0% of each run, Pallas kernels for 0% -> 0%
where the time goes in v1:
time: 697 us; the launch traced here: 688 us
  Pallas kernels  324 us (46%)
  waiting for transfers between devices  249 us (36%)
  blocking collectives  40.6 us (6%)
  other arithmetic  33.5 us (5%)
  local copies, waits for them, and re-layouts  25.5 us (4%)
  between operations  14.6 us (2%)
    pallas_call x4, Pallas kernels, call_kernel(): pl.pallas_call(functools.partial(body, cfg, names), out_shape=[shape for...  324 us
    psum x1, waiting for transfers between devices, per_device_square(): totals.append(lax.psum(stacked, 'dp').astype(F32))  249 us
    psum x1, blocking collectives, per_device_square(): stat_sums = lax.psum(stats, ('dp', 'tensor'))  40.6 us
    unnamed x46, local copies, waits for them, and re-layouts  20.6 us
  transfers between devices with their start and end apart: 1, of which 1 were waited for; matrix products, arithmetic and copies ran while one was open for 0% of the time, Pallas kernels for 0%

profile of v1, /device:TPU:0, one launch (start us, length us, event | category | flops | bytes accessed | tf_op | source)
XLA Modules:
  0.0 687.9 jit_solution(12456993633679394594)
XLA Ops:
  7.2 0.0 copy-start.15
  7.2 0.0 all-reduce.5.cloned.1.call-start
  7.3 0.0 copy-start.1
  7.3 2.8 fusion
  10.1 2.1 convert_element_type.39.refs_0_.refs_1_
  12.2 0.0 copy-done.15
  12.2 1.1 convert_element_type.42.refs_0_
  13.3 0.0 copy-done.1
  13.3 2.8 copy.22.refs_11_.refs_13_
  16.1 4.6 copy.23.refs_12_.refs_14_
  20.7 0.7 broadcast_in_dim.10.refs_5_.refs_7_
  21.3 0.0 copy-done.18
  21.3 0.6 broadcast_in_dim.9.refs_4_.refs_6_
  22.0 1.0 broadcast_in_dim.8.refs_3_.refs_5_
  23.0 83.7 %layer_forward.2 = (f32[256,1024]{1,0:T(8,128)}, f32[8,1024]{1,0:T(8,128)}, f32[8,128]{1,0:T(8,128)}, bf16[1024,1024]{1,0:T(8,128)(2,1)}, bf16[1024,256]{1,0:T(8...) custom-call(f32[256,1024]{1,0:T(8,128)} %convert_element_type.39.ref, ...), custom_call_target="tpu_custom_call" | custom-call | tf_op jit(solution)/shard_map/layer_forward/pallas_call | solution.py:1078
  106.6 0.7 broadcast_in_dim.11.refs_5_.refs_7_
  107.3 78.9 %layer_forward.3 = (f32[256,1024]{1,0:T(8,128)}, f32[8,1024]{1,0:T(8,128)}, f32[8,128]{1,0:T(8,128)}, bf16[1024,1024]{1,0:T(8,128)(2,1)}, bf16[1024,256]{1,0:T(8...) custom-call(f32[256,1024]{1,0:T(8,128)} %get-tuple-element.55.refs_0, ...), custom_call_target="tpu_custom_call" | custom-call | tf_op jit(solution)/shard_map/layer_forward/pallas_call | solution.py:1078
  186.1 81.7 %layer_backward.2 = (f32[256,1024]{1,0:T(8,128)}, bf16[4,1024,256]{2,1,0:T(8,128)(2,1)}, bf16[256,1024]{1,0:T(8,128)(2,1)}, bf16[1024,704]{1,0:T(8,128)(2,1)}, b...) custom-call(f32[256,1024]{1,0:T(8,128)} %convert_element_type.42.refs_0_, ...), custom_call_target="tpu_custom_call" | custom-call | tf_op jit(solution)/shard_map/layer_backward/pallas_call | solution.py:1078
  267.9 80.1 %layer_backward.3 = (f32[256,1024]{1,0:T(8,128)}, bf16[4,1024,256]{2,1,0:T(8,128)(2,1)}, bf16[256,1024]{1,0:T(8,128)(2,1)}, bf16[1024,704]{1,0:T(8,128)(2,1)}, b...) custom-call(f32[256,1024]{1,0:T(8,128)} %get-tuple-element.71.refs_0_, ...), custom_call_target="tpu_custom_call" | custom-call | tf_op jit(solution)/shard_map/layer_backward/pallas_call | solution.py:1078
  348.0 0.0 copy-start.2
  348.0 1.8 fusion.2
  349.8 0.4 copy-done.2
  350.2 0.1 fusion.3
  350.4 0.0 copy-start.7
  350.4 0.9 copy-done.16
  351.3 0.2 copy-done.17
  351.4 1.1 pad_maximum_fusion.7
  352.5 0.0 copy-done.8
  352.5 0.0 copy-done.7
  352.5 1.8 pad_maximum_fusion.2
  354.3 0.1 copy-done.4
  354.4 1.0 copy-done.6
  355.4 2.0 pad_maximum_fusion
  357.4 0.0 copy-done.3
  357.4 1.0 copy-done.5
  358.4 2.0 pad_maximum_fusion.1
  360.4 1.1 pad_maximum_fusion.6
  361.4 1.1 pad_maximum_fusion.5
  362.5 1.1 pad_maximum_fusion.4
  363.6 1.1 pad_maximum_fusion.3
  364.6 0.0 all-reduce.5.cloned.1.call-update
  364.7 0.0 copy-start.14
  364.7 0.7 copy-done.19
  365.4 0.1 slice_reduce_fusion.1
  365.5 0.0 copy-done.20
  365.5 0.1 slice_reduce_fusion
  365.6 40.6 %psum.71 = f32[2,3]{1,0:T(2,128)S(1)} all-reduce(f32[2,3]{1,0:T(2,128)S(1)} %pad_maximum_fusion.8), channel_id=1, replica_groups=mesh['dp'=8,'tensor'=4] {'dp','tensor'}, use_global_device_ids=true, to_apply=%region_10.0 | all-reduce | flops 6 | bytes 48 | tf_op jit(solution)/shard_map/psum | solution.py:1207
  406.2 0.0 copy-done.13
  406.2 0.9 convert_element_type.41
  407.1 0.0 copy-done.14
  407.1 0.9 convert_element_type.43
  408.0 0.6 multiply_sqrt_fusion
  408.5 249.3 %all-reduce.5.cloned.1.call-done = (bf16[2,1024,704]{2,1,0:T(8,128)(2,1)}, bf16[2,1024,704]{2,1,0:T(8,128)(2,1)}, bf16[2,1024,256]{2,1,0:T(8,128)(2,1)}, bf16[2,...) async-done(((bf16[2,1024,704]{2,1,0:T(8,128)(2,1)}, ...) | async-done | bytes 13893648 | tf_op jit(solution)/shard_map/psum | solution.py:1221
  657.8 2.8 convert_element_type.44
  660.6 0.0 copy-done.12
  660.6 1.5 convert_element_type.45
  662.1 0.1 copy-done.11
  662.2 1.5 convert_element_type.46
  663.7 1.5 convert_element_type.47
  665.2 0.1 copy-done.9
  665.2 1.6 convert_element_type.48
  666.8 5.4 copy.30
  672.2 3.4 copy.31
  675.5 5.1 convert_element_type.51
  (23 shorter events, 0.1 us)
Async XLA Ops:
  7.2 5.1 copy-start.15
  7.2 650.6 %all-reduce.5.cloned.1.call-start = ((), (), s32[]{:S(2)}) async-start(), calls=%async_computation | async-start | bytes 28835840 | tf_op jit(solution)/shard_map/psum | solution.py:1221
  7.3 6.0 copy-start.1
  16.1 5.3 copy-start.18
  348.0 2.2 copy-start.2
  350.2 1.0 copy-start.16
  350.2 1.2 copy-start.17
  350.2 2.3 copy-start.8
  350.4 2.1 copy-start.7
  352.5 1.9 copy-start.4
  352.5 2.9 copy-start.6
  355.4 2.0 copy-start.3
  355.4 3.0 copy-start.5
  364.6 0.8 copy-start.19
  364.6 0.9 copy-start.20
  364.6 41.6 %copy-start.13 = (f32[256,1024]{1,0:T(8,128)S(1)}, f32[256,1024]{1,0:T(8,128)}, u32[]{:S(2)}) copy-start(f32[256,1024]{1,0:T(8,128)} %get-tuple-element.56) | copy-start | bytes 3145732
  364.7 42.4 %copy-start.14 = (f32[256,1024]{1,0:T(8,128)S(1)}, f32[256,1024]{1,0:T(8,128)}, u32[]{:S(2)}) copy-start(f32[256,1024]{1,0:T(8,128)} %get-tuple-element.86) | copy-start | bytes 3145732
  657.8 2.8 copy-start.12
  660.6 1.6 copy-start.11
  662.1 1.6 copy-start.10
  663.7 1.6 copy-start.9
  666.8 5.4 copy-start
Sparse Core Ops, SparseCore 0:
  364.8 293.0 all-reduce.4

commit v2 on v1

--- a/solution.py
+++ b/solution.py
@@ -4,6 +4,7 @@
 
 import jax
 import jax.numpy as jnp
+import numpy as np
 from jax import lax
 from jax.experimental import pallas as pl
 from jax.experimental.pallas import tpu as pltpu
@@ -453,6 +454,9 @@
 MESH = pl.DeviceIdType.MESH
 VMEM_LIMIT = 60 * 2**20
 SUPER = 2
+CHUNK = 128
+HOP = 2
+SLOTS = 12
 
 
 def nn(a, b):
@@ -476,11 +480,14 @@
 
 
 class Place:
-    def __init__(self):
+    def __init__(self, pairs):
         self.dp = lax.axis_index("dp")
         self.me = lax.axis_index("tensor")
         self.low = lax.rem(self.me, 2)
         self.high = self.me // 2
+        self.core = lax.rem(self.dp, 2)
+        self.at = self.dp // 2
+        self.last = pairs - 1
 
     def member(self, step):
         low = lax.rem(self.low + lax.rem(step, 2), 2)
@@ -490,19 +497,43 @@
     def device(self, step):
         return (self.dp, self.member(step))
 
-    def greet(self):
+    def partner(self):
+        return (self.dp + 1 - 2 * self.core, self.me)
+
+    def right(self):
+        return (self.dp + 2, self.me)
+
+    def left(self):
+        return (self.dp - 2, self.me)
+
+    def greet(self, line):
         barrier = pltpu.get_barrier_semaphore()
+
+        def signal(device):
+            pl.semaphore_signal(barrier, inc=1, device_id=device, device_id_type=MESH)
+
         for step in (1, 2, 3):
-            pl.semaphore_signal(barrier, inc=1, device_id=self.device(step), device_id_type=MESH)
-        pl.semaphore_wait(barrier, 3)
+            signal(self.device(step))
+        if not line:
+            pl.semaphore_wait(barrier, 3)
+            return
+        signal(self.partner())
+
+        @pl.when(self.at < self.last)
+        def _():
+            signal(self.right())
+
+        @pl.when(self.at > 0)
+        def _():
+            signal(self.left())
+
+        pl.semaphore_wait(barrier, 4 + jnp.minimum(self.at, 1) + jnp.minimum(self.last - self.at, 1))
 
 
 class Wire:
-    def __init__(self, place, step, send_sem, recv_sem, source, target, landing):
+    def __init__(self, device, send_sem, recv_sem, source, target, landing):
         self.source, self.target, self.landing = source, target, landing
-        self.common = dict(
-            send_sem=send_sem, recv_sem=recv_sem, device_id=place.device(step), device_id_type=MESH
-        )
+        self.common = dict(send_sem=send_sem, recv_sem=recv_sem, device_id=device, device_id_type=MESH)
 
     def out(self):
         return pltpu.make_async_remote_copy(src_ref=self.source, dst_ref=self.target, **self.common)
@@ -531,7 +562,7 @@
         step, owner, half = ((1, 0, 0), (2, 0, 1), (1, 0, 1), (2, 0, 0), (2, 1, 0), (1, 2, 1))[number]
         source = self.rows(owner, part, half)
         landing = self.rows((0, 1, 2, 3)[owner ^ step], part, half)
-        return Wire(self.place, step, self.send.at[part, number], self.recv.at[part, number], source, source, landing)
+        return Wire(self.place.device(step), self.send.at[part, number], self.recv.at[part, number], source, source, landing)
 
     def start(self, part):
         for number in range(4):
@@ -567,7 +598,7 @@
         step, owner, half = ((1, 3, 0), (1, 1, 0), (2, 3, 1), (2, 2, 1), (2, 2, 0), (1, 1, 1))[number]
         target = self.land.at[part, number]
         return Wire(
-            self.place, step, self.send.at[part, number], self.recv.at[part, number],
+            self.place.device(step), self.send.at[part, number], self.recv.at[part, number],
             self.buf.at[self.rows(owner, part, half)], target, target,
         )
 
@@ -608,7 +639,7 @@
 class Share:
     def __init__(self, place, mine, land, send, recv):
         self.wires = [
-            Wire(place, step, send.at[step - 1], recv.at[step - 1], mine, land.at[step - 1], land.at[step - 1])
+            Wire(place.device(step), send.at[step - 1], recv.at[step - 1], mine, land.at[step - 1], land.at[step - 1])
             for step in (1, 2, 3)
         ]
         self.mine, self.land = mine, land
@@ -652,26 +683,34 @@
     return jnp.concatenate([columns] * times, axis=1)
 
 
-def decay_tiles(dec_ref, tiles, heads_here, size):
+def decay_tiles(dec_ref, first_head, tiles, heads_here, size):
     rows = lax.broadcasted_iota(jnp.int32, (size, size), 0)
     cols = lax.broadcasted_iota(jnp.int32, (size, size), 1)
     distance = (rows - cols).astype(F32)
     for head in range(heads_here):
-        decay = dec_ref[head : head + 1, 0:1]
+        decay = dec_ref[pl.ds(first_head + head, 1), 0:1]
         tiles[head, 0] = jnp.where(rows >= cols, jnp.exp(decay * jnp.maximum(distance, 0.0)), 0.0)
         tiles[head, 1] = jnp.exp(decay * (distance + float(size)))
 
 
-def tile_weight(dec_ref, tiles, segc_ref, segr_ref, head, row_tile, col_tile, size):
+def spread_segments(r, length):
+    r.segf[...] = r.seg[...].astype(F32)
+    for chunk in range(length // 128):
+        r.segc[chunk * 128 : (chunk + 1) * 128, :] = spread(r.segf[...], chunk)
+
+
+def tile_weight(r, first_head, head, row_tile, col_tile, size):
     gap = row_tile - col_tile
     if gap == 0:
-        weight = tiles[head, 0]
+        weight = r.tiles[head, 0]
     else:
-        weight = tiles[head, 1]
+        weight = r.tiles[head, 1]
         if gap > 1:
-            weight = weight * jnp.exp(dec_ref[pl.ds(head, 1), 0:1] * float(size * (gap - 1)))
-    row_seg = widen(segc_ref[row_tile * size : (row_tile + 1) * size, :], size // 128)
-    col_seg = segr_ref[0:1, col_tile * size : (col_tile + 1) * size]
+            decay = r.dec[pl.ds(first_head + head, 1), 0:1]
+            weight = weight * jnp.exp(decay * float(size * (gap - 1)))
+    row_seg = widen(r.segc[row_tile * size : (row_tile + 1) * size, :], size // 128)
+    per = size // 128
+    col_seg = jnp.concatenate([r.segf[per * col_tile + i : per * col_tile + i + 1, :] for i in range(per)], axis=1)
     return jnp.where(row_seg == col_seg, weight, 0.0)
 
 
@@ -683,7 +722,8 @@
     r = namespace(names, refs)
     layer, block, length, width, local = cfg.layer, cfg.block, cfg.length, cfg.width, cfg.local
     heads_here, size = cfg.heads_here, cfg.block
-    place = Place()
+    place = Place(cfg.pairs)
+    first_head = layer * HEADS + place.me * heads_here
     copies = Local(r.local_sem)
     w_in = [copies.start(h.at[layer], v) for h, v in (
         (r.wq_h, r.wq), (r.wk_h, r.wk), (r.wv_h, r.wv), (r.wg_h, r.wg))]
@@ -701,14 +741,15 @@
     @pl.loop(0, block // step_rows)
     def _(i):
         rows = aligned(i * step_rows, step_rows)
-        v = r.x[rows, :]
+        v = r.x[rows, :].astype(F32)
         scale = lax.rsqrt(jnp.mean(v * v, axis=1, keepdims=True) + epsilon)
         r.n1[aligned(own_start + i * step_rows, step_rows), :] = (v * scale).astype(BF16)
 
-    place.greet()
+    place.greet(False)
     for part in range(SUPER):
         first.start(part)
-    decay_tiles(r.dec, r.tiles, heads_here, size)
+    decay_tiles(r.dec, first_head, r.tiles, heads_here, size)
+    spread_segments(r, length)
     for copy in w_in:
         copy.wait()
 
@@ -752,7 +793,7 @@
             acc = None
             for col_tile in range(row_tile + 1):
                 cols = slice(col_tile * size, (col_tile + 1) * size)
-                weight = tile_weight(r.dec, r.tiles, r.segc, r.segr, head, row_tile, col_tile, size)
+                weight = tile_weight(r, first_head, head, row_tile, col_tile, size)
                 scores = (nt(queries, r.k[cols, wide]) * weight).astype(BF16)
                 term = nn(scores, r.v[cols, thin])
                 acc = term if acc is None else acc + term
@@ -780,11 +821,11 @@
     per_block = block // 128
     for chunk in range(per_block):
         r.scale[chunk * 128 : (chunk + 1) * 128, :] = spread(scaling, place.me * per_block + chunk)
-    r.stat[...] = jnp.zeros_like(r.stat)
+    r.stat_wide[...] = jnp.zeros_like(r.stat_wide)
 
     def add_stat(row, v):
         sums = jnp.sum(v * v, axis=0, keepdims=True)
-        r.stat[row : row + 1, :] += sums
+        r.stat_wide[row : row + 1, :] += sums
 
     step_rows = min(32, half)
     for part in range(SUPER):
@@ -794,7 +835,7 @@
                 offset = (2 * part + h) * half + i * step_rows
                 scale = widen(r.scale[offset : offset + step_rows, :], width // 128)
                 attn = mid_sum.total(part, h, i * step_rows, step_rows) * scale
-                middle = r.x[offset : offset + step_rows, :] + attn
+                middle = r.x[offset : offset + step_rows, :].astype(F32) + attn
                 r.mid[offset : offset + step_rows, :] = middle
                 add_stat(0, attn)
                 norm = lax.rsqrt(jnp.mean(middle * middle, axis=1, keepdims=True) + epsilon)
@@ -808,8 +849,8 @@
         def glu(step):
             rows = aligned(place.member(step) * block + part * part_rows, part_rows)
             a = r.n2[rows, :]
-            left = nn(a, r.wl[...])
-            right = nn(a, r.wr[...])
+            left = nt(a, r.wl[...])
+            right = nt(a, r.wr[...])
             hidden = (left * right).astype(BF16)
             r.left[rows, :] = left.astype(BF16)
             r.right[rows, :] = right.astype(BF16)
@@ -846,230 +887,515 @@
                 r.xo[offset : offset + step_rows, :] = after
                 add_stat(1, glu_rows)
                 add_stat(2, after)
+    folded = r.stat_wide[:, :128]
+    for n in range(1, width // 128):
+        folded = folded + r.stat_wide[:, n * 128 : (n + 1) * 128]
+    r.stat[...] = folded
     for copy in saves:
         copy.wait()
     for group in (first, mid_sum, second, out_sum, share):
         group.drain()
 
 
+class Line:
+    def __init__(self, cfg, place, r):
+        self.place, self.r = place, r
+        self.per, self.count = cfg.chunks, cfg.chunks * cfg.layers
+        self.layers, self.rows_each = cfg.layers, cfg.chunks * CHUNK
+        self.half = CHUNK // 2
+        self.ticks = self.count + 3 + HOP * place.last
+        self.done = 0
+
+    def rows(self, k, core):
+        return aligned(lax.rem(k, self.per) * CHUNK + core * self.half, self.half)
+
+    def own(self, k):
+        return self.rows(k, self.place.core)
+
+    def out_rows(self, k, core):
+        layer = self.layers - 1 - k // self.per
+        start = layer * self.rows_each + lax.rem(k, self.per) * CHUNK + core * self.half
+        return aligned(start, self.half)
+
+    def pair(self, k):
+        slot = lax.rem(k, SLOTS)
+        r = self.r
+        return Wire(self.place.partner(), r.pair_send.at[slot], r.pair_recv.at[slot],
+                    r.grads.at[self.rows(k, 1 - self.place.core)], r.pair_land.at[slot], r.pair_land.at[slot])
+
+    def hop(self, k, land, send, recv, device):
+        slot = lax.rem(k, SLOTS)
+        return Wire(device, send.at[slot], recv.at[slot], land.at[slot], land.at[slot], land.at[slot])
+
+    def going_right(self, k):
+        return self.hop(k, self.r.right_land, self.r.right_send, self.r.right_recv, self.place.right())
+
+    def going_left(self, k):
+        return self.hop(k, self.r.left_land, self.r.left_send, self.r.left_recv, self.place.left())
+
+    def coming_right(self, k):
+        return self.hop(k, self.r.right_land, self.r.right_send, self.r.right_recv, self.place.left())
+
+    def coming_left(self, k):
+        return self.hop(k, self.r.left_land, self.r.left_send, self.r.left_recv, self.place.right())
+
+    def result(self, k):
+        slot, r = lax.rem(k, SLOTS), self.r
+        return Wire(self.place.partner(), r.give_send.at[slot], r.give_recv.at[slot],
+                    r.grads.at[self.own(k)], r.out_h.at[self.out_rows(k, self.place.core)],
+                    r.out_h.at[self.out_rows(k, 1 - self.place.core)])
+
+    def keep(self, k):
+        slot, r = lax.rem(k, SLOTS), self.r
+        return pltpu.make_async_copy(
+            r.grads.at[self.own(k)], r.out_h.at[self.out_rows(k, self.place.core)], r.keep_sem.at[slot]
+        )
+
+    def one_way(self, k, land, start_here, coming, ends_here, going):
+        slot = lax.rem(k, SLOTS)
+
+        @pl.when(start_here)
+        def _():
+            land[slot] = self.r.grads[self.own(k), :]
+
+        @pl.when(jnp.logical_not(start_here))
+        def _():
+            coming(k).wait_recv()
+            land[slot] = (land[slot].astype(F32) + self.r.grads[self.own(k), :].astype(F32)).astype(BF16)
+
+        @pl.when(jnp.logical_not(ends_here))
+        def _():
+            going(k).start()
+
+    def tick(self, n):
+        place, r, last = self.place, self.r, self.place.last
+        at_left, at_right = place.at == 0, place.at == last
+
+        @pl.when(n < self.count)
+        def _():
+            self.pair(n).start()
+
+        k = n - 1
+
+        @pl.when(jnp.logical_and(k >= 0, k < self.count))
+        def _():
+            wire = self.pair(k)
+            wire.wait_recv()
+            wire.wait_send()
+            slot = lax.rem(k, SLOTS)
+            r.grads[self.own(k), :] = (
+                r.grads[self.own(k), :].astype(F32) + r.pair_land[slot].astype(F32)
+            ).astype(BF16)
+
+        left_k = n - 1 - HOP * (last - place.at)
+
+        @pl.when(jnp.logical_and(left_k >= 0, left_k < self.count))
+        def _():
+            self.one_way(left_k, r.left_land, at_right, self.coming_left, at_left, self.going_left)
+
+        right_k = n - 1 - HOP * place.at
+
+        @pl.when(jnp.logical_and(right_k >= 0, right_k < self.count))
+        def _():
+            self.one_way(right_k, r.right_land, at_left, self.coming_right, at_right, self.going_right)
+
+        full_k = n - 1 - HOP * last
+
+        @pl.when(jnp.logical_and(full_k >= 0, full_k < self.count))
+        def _():
+            @pl.when(jnp.logical_not(at_right))
+            def _():
+                self.going_right(full_k).wait_send()
+
+            @pl.when(jnp.logical_not(at_left))
+            def _():
+                self.going_left(full_k).wait_send()
+
+            slot = lax.rem(full_k, SLOTS)
+            own = self.own(full_k)
+            total = r.right_land[slot].astype(F32) + r.left_land[slot].astype(F32) - r.grads[own, :].astype(F32)
+            r.grads[own, :] = total.astype(BF16)
+            self.result(full_k).start()
+            self.keep(full_k).start()
+
+        old_k = full_k - 2
+
+        @pl.when(jnp.logical_and(old_k >= 0, old_k < self.count))
+        def _():
+            wire = self.result(old_k)
+            wire.wait_recv()
+            wire.wait_send()
+            self.keep(old_k).wait()
+
+    def pump(self, ready, most):
+        stop = min(self.done + most, ready)
+        if stop > self.done:
+            start, self.done = self.done, stop
+
+            @pl.loop(start, stop)
+            def _(n):
+                self.tick(n)
+
+    def finish(self):
+        start, self.done = self.done, self.ticks
+
+        @pl.loop(start, self.ticks)
+        def _(n):
+            self.tick(n)
+
+
+class StatLine:
+    def __init__(self, place, r):
+        self.place, self.r = place, r
+        self.share = Share(place, r.stat_mine, r.stat_land, r.st_send, r.st_recv)
+
+    def square(self):
+        self.share.start()
+
+    def pair(self):
+        r = self.r
+        r.stat_square[...] = self.share.total()
+        self.wire(0, self.place.partner(), r.stat_square).start()
+
+    def wire(self, number, device, source):
+        r = self.r
+        return Wire(device, r.line_send.at[number], r.line_recv.at[number], source, r.line_land.at[number], r.line_land.at[number])
+
+    def stage(self, number):
+        place, r = self.place, self.r
+        if number == 0:
+            self.wire(0, place.partner(), r.stat_square).wait_recv()
+            r.stat_pair[...] = r.stat_square[...] + r.line_land[0]
+            r.stat_right[...] = r.stat_pair[...]
+            r.stat_left[...] = r.stat_pair[...]
+        else:
+            @pl.when(place.at == number)
+            def _():
+                self.wire(1, place.left(), r.stat_right).wait_recv()
+                r.stat_right[...] = r.stat_pair[...] + r.line_land[1]
+
+            @pl.when(place.last - place.at == number)
+            def _():
+                self.wire(2, place.right(), r.stat_left).wait_recv()
+                r.stat_left[...] = r.stat_pair[...] + r.line_land[2]
+        if number < place.last:
+            @pl.when(place.at == number)
+            def _():
+                self.wire(1, place.right(), r.stat_right).start()
+
+            @pl.when(place.last - place.at == number)
+            def _():
+                self.wire(2, place.left(), r.stat_left).start()
+
+    def finish(self):
+        place, r = self.place, self.r
+        r.stat_total[...] = r.stat_right[...] + r.stat_left[...] - r.stat_pair[...]
+        self.share.drain()
+        self.wire(0, place.partner(), r.stat_square).wait_send()
+
+        @pl.when(place.at < place.last)
+        def _():
+            self.wire(1, place.right(), r.stat_right).wait_send()
+
+        @pl.when(place.at > 0)
+        def _():
+            self.wire(2, place.left(), r.stat_left).wait_send()
+
+
 def bwd_kernel(cfg, names, *refs):
     r = namespace(names, refs)
-    layer, block, length, width, local = cfg.layer, cfg.block, cfg.length, cfg.width, cfg.local
-    heads_here, size = cfg.heads_here, cfg.block
-    place = Place()
+    block, length, width, local, ff = cfg.block, cfg.length, cfg.width, cfg.local, cfg.ff
+    heads_here, size, layers = cfg.heads_here, cfg.block, cfg.layers
+    place = Place(cfg.pairs)
     copies = Local(r.local_sem)
-    load_glu = [copies.start(s, v) for s, v in (
-        (r.wd_h.at[layer], r.wd), (r.left_h, r.left), (r.right_h, r.right),
-        (r.wl_h.at[layer], r.wl), (r.wr_h.at[layer], r.wr))]
-    load_glu_grad = [copies.start(r.hid_h, r.hid), copies.start(r.n2_h, r.n2)]
-    load_out = [copies.start(s, v) for s, v in (
-        (r.ss_h, r.sstot), (r.wo_h.at[layer], r.wo), (r.gate_h, r.gate), (r.heads_h, r.heads))]
-    load_attn = [copies.start(s, v) for s, v in (
-        (r.q_h, r.q), (r.k_h, r.k), (r.v_h, r.v), (r.ql_h, r.ql), (r.kl_h, r.kl))]
-    load_in = [copies.start(s, v) for s, v in (
-        (r.wq_h.at[layer], r.wq), (r.wk_h.at[layer], r.wk), (r.wv_h.at[layer], r.wv),
-        (r.wg_h.at[layer], r.wg))]
-    load_in_grad = [copies.start(r.n1_h, r.n1)]
-    saves = []
-    first = Gather(place, r.gd, r.ag1_send, r.ag1_recv, block)
-    mid_sum = Scatter(place, r.part1, r.land1, r.rs1_send, r.rs1_recv, block)
-    second = Gather(place, r.ga, r.ag2_send, r.ag2_recv, block)
-    in_sum = Scatter(place, r.part2, r.land2, r.rs2_send, r.rs2_recv, block)
-    share = Share(place, r.inner, r.inner_land, r.in_send, r.in_recv)
-    half = first.half
+    line = Line(cfg, place, r)
+    stats = StatLine(place, r)
+    loads = {}
+    base_down, base_left, base_right, base_out, base_gate, base_qkv, base_end = cfg.bases
+    half = block // (2 * SUPER)
     part_rows = 2 * half
     own_start = place.me * block
     step_rows = min(32, half)
+    per_block = block // 128
+    tiles_here = length // size
+
+    def load(layer, *keys):
+        for key in keys:
+            if key in SAVED:
+                source = getattr(r, key + str(layer) + "_h")
+            else:
+                source = getattr(r, key + "_h").at[layer]
+            loads[key] = copies.start(source, getattr(r, key))
+
+    def await_loads(*keys):
+        for key in keys:
+            loads[key].wait()
+
+    glu_in = ("wd", "left", "right", "wl", "wr")
+    glu_grad = ("hid", "n2", "mid")
+    out_in = ("ss", "wo", "gate", "heads")
+    attn_in = ("q", "k", "v", "ql", "kl")
+    in_in = ("wq", "wk", "wv", "wg")
+    load(layers - 1, *glu_in, *glu_grad, *out_in, *attn_in, *in_in, "n1")
+
+    def gather_one(layer):
+        return Gather(place, r.gd, r.ag1_send.at[layer], r.ag1_recv.at[layer], block)
+
+    firsts = [gather_one(layer) for layer in range(layers)]
 
     @pl.loop(0, block // 32)
     def _(i):
         rows = aligned(i * 32, 32)
-        r.gd[aligned(own_start + i * 32, 32), :] = r.g[rows, :].astype(BF16)
-
-    place.greet()
+        v = r.up[rows, :]
+        r.g[rows, :] = v.astype(F32)
+        r.gd[aligned(own_start + i * 32, 32), :] = v
+
+    r.stat_mine[...] = jnp.zeros_like(r.stat_mine)
+    for layer in range(layers):
+        r.stat_mine[3 * layer : 3 * layer + 3, :] = getattr(r, "stat%d" % layer)[0:3, :]
+    place.greet(True)
     for part in range(SUPER):
-        first.start(part)
-    decay_tiles(r.dec, r.tiles, heads_here, size)
-    for copy in load_glu:
-        copy.wait()
-    for copy in load_out:
-        copy.wait()
-    scaling = lax.rsqrt(r.sstot[...] / width + epsilon)
-    for chunk in range(length // 128):
-        r.scale[chunk * 128 : (chunk + 1) * 128, :] = spread(scaling, chunk)
-
-    for part in range(SUPER):
+        firsts[layers - 1].start(part)
+    stats.square()
+    spread_segments(r, length)
+    r.grads[base_end : cfg.chunks * CHUNK, :] = jnp.zeros((cfg.chunks * CHUNK - base_end, width), BF16)
+    stats.pair()
+
+    def back_rows(total, values, grad):
+        norm = lax.rsqrt(jnp.mean(values * values, axis=1, keepdims=True) + epsilon)
+        m = values * norm
+        inner = jnp.mean(total * m, axis=1, keepdims=True)
+        return grad + norm * (total - m * inner)
+
+    for turn, layer in enumerate(reversed(range(layers))):
+        first = firsts[layer]
+        mid_sum = Scatter(place, r.part, r.land, r.rs1_send.at[layer], r.rs1_recv.at[layer], block)
+        second = Gather(place, r.ga, r.ag2_send.at[layer], r.ag2_recv.at[layer], block)
+        in_sum = Scatter(place, r.part, r.land, r.rs2_send.at[layer], r.rs2_recv.at[layer], block)
+        share = Share(place, r.inner, r.inner_land.at[layer], r.in_send.at[layer], r.in_recv.at[layer])
+        first_head = layer * HEADS + place.me * heads_here
+
+        def ready(rows):
+            return turn * cfg.chunks + rows // CHUNK
+
+        decay_tiles(r.dec, first_head, r.tiles, heads_here, size)
+        await_loads(*glu_in)
+        await_loads(*out_in)
+        scaling = lax.rsqrt(r.ss[...] / width + epsilon)
+        for chunk in range(length // 128):
+            r.scale[chunk * 128 : (chunk + 1) * 128, :] = spread(scaling, chunk)
+        if turn == 0:
+            stats.stage(0)
+
+        for part in range(SUPER):
+            start = line.done
+            beside = min(4, ready(0) - start)
+            line.done = start + max(beside, 0)
+
+            @pl.loop(0, 4)
+            def _(step):
+                if beside > 0:
+                    @pl.when(step < beside)
+                    def _():
+                        line.tick(start + step)
+                if part == 0:
+                    @pl.when(step == 1)
+                    def _():
+                        for other in range(SUPER):
+                            first.forward(other)
+                for which in (1, 2, 3):
+                    @pl.when(step == which)
+                    def _():
+                        first.finish(part, which)
+                rows = aligned(place.member(step) * block + part * part_rows, part_rows)
+                grad_hidden = nt(r.gd[rows, :], r.wd[...])
+                grad_left = (grad_hidden * r.right[rows, :].astype(F32)).astype(BF16)
+                grad_right = (grad_hidden * r.left[rows, :].astype(F32)).astype(BF16)
+                r.right[rows, :] = grad_left
+                r.left[rows, :] = grad_right
+                r.part[rows, :] = (nn(grad_left, r.wl[...]) + nn(grad_right, r.wr[...])).astype(BF16)
+                for which in (1, 2, 3):
+                    @pl.when(step == which)
+                    def _():
+                        mid_sum.send_block(part, which)
+        first.drain()
+        grad_left_ref, grad_right_ref = r.right, r.left
+
+        def glu_grad_rows(base, a_ref, b_ref, limit):
+            for n in range(width // 256):
+                cols = slice(n * 256, (n + 1) * 256)
+                r.grads[base : base + ff, cols] = tn(a_ref[...], b_ref[:, cols]).astype(BF16)
+                if n % 2 == 1:
+                    line.pump(ready(limit), 1)
+
+        await_loads(*glu_grad)
+        glu_grad_rows(base_down, r.hid, r.gd, 0)
+        if turn == 0:
+            stats.stage(1)
+        for part in range(SUPER):
+            line.pump(ready(base_left), 1)
+            mid_sum.middle(part)
+        glu_grad_rows(base_left, grad_left_ref, r.n2, base_left)
+        for part in range(SUPER):
+            for h in range(2):
+                line.pump(ready(base_right), 1)
+                mid_sum.finish(part, h)
+                for i in range(half // step_rows):
+                    offset = (2 * part + h) * half + i * step_rows
+                    rows = slice(offset, offset + step_rows)
+                    total = mid_sum.total(part, h, i * step_rows, step_rows)
+                    new = back_rows(total, r.mid[rows, :], r.g[rows, :])
+                    r.gm[rows, :] = new
+                    r.ga[aligned(own_start + offset, step_rows), :] = new.astype(BF16)
+            second.start(part)
+        mid_sum.drain()
+        if turn == 0:
+            stats.stage(2)
+        glu_grad_rows(base_right, grad_right_ref, r.n2, base_right)
+        if turn + 1 < layers:
+            load(layer - 1, *glu_in, *glu_grad)
+        if turn == 0:
+            stats.stage(3)
+        start = line.done
+        beside = max(min(4, ready(base_out) - start), 0)
+        line.done = start + beside
+
         @pl.loop(0, 4)
         def _(step):
-            if part == 0:
-                @pl.when(step == 1)
+            if beside > 0:
+                @pl.when(step < beside)
                 def _():
-                    for other in range(SUPER):
-                        first.forward(other)
+                    line.tick(start + step)
+            @pl.when(step == 1)
+            def _():
+                for part in range(SUPER):
+                    second.forward(part)
             for which in (1, 2, 3):
                 @pl.when(step == which)
                 def _():
-                    first.finish(part, which)
-            rows = aligned(place.member(step) * block + part * part_rows, part_rows)
-            grad_hidden = nt(r.gd[rows, :], r.wd[...])
-            grad_left = (grad_hidden * r.right[rows, :].astype(F32)).astype(BF16)
-            grad_right = (grad_hidden * r.left[rows, :].astype(F32)).astype(BF16)
-            r.dl[rows, :] = grad_left
-            r.dr[rows, :] = grad_right
-            r.part1[rows, :] = (nt(grad_left, r.wl[...]) + nt(grad_right, r.wr[...])).astype(BF16)
-            for which in (1, 2, 3):
-                @pl.when(step == which)
+                    for part in range(SUPER):
+                        second.finish(part, which)
+            member = place.member(step)
+            for chunk in range(per_block):
+                rows = aligned(member * block + chunk * 128, 128)
+                grad_branch = nt(r.ga[rows, :], r.wo[...])
+                gate = r.gate[rows, :]
+                normed = r.heads[rows, :] * widen(r.scale[rows, :], local // 128)
+                grad_normed = grad_branch * gate
+                r.dx[rows, 3 * local : 4 * local] = (grad_branch * normed).astype(BF16)
+                r.branch[rows, :] = (normed * gate).astype(BF16)
+                r.gate[rows, :] = grad_normed
+                row_sums(grad_normed * normed, r.inner, member * per_block + chunk)
+        share.start()
+        r.grads[base_out : base_out + local, :] = tn(r.branch[...], r.ga[...]).astype(BF16)
+        line.pump(ready(base_gate), 1)
+
+        def in_grad_rows(number, base):
+            cols = slice(number * local, (number + 1) * local)
+            for n in range(width // local):
+                part_grad = tn(r.n1[:, n * local : (n + 1) * local], r.dx[:, cols])
+                r.grads[base : base + local, n * local : (n + 1) * local] = part_grad.astype(BF16)
+
+        await_loads("n1")
+        in_grad_rows(3, base_gate)
+        line.pump(ready(base_qkv), 1)
+        await_loads(*attn_in)
+        r.intot[...] = share.total() / width
+        for chunk in range(length // 128):
+            rows = slice(chunk * 128, (chunk + 1) * 128)
+            scale = widen(r.scale[rows, :], local // 128)
+            inner = widen(spread(r.intot[...], chunk), local // 128)
+            normed = r.heads[rows, :] * scale
+            r.dh[rows, :] = (scale * (r.gate[rows, :] - normed * inner)).astype(BF16)
+        share.drain()
+        second.drain()
+        if turn + 1 < layers:
+            load(layer - 1, *out_in)
+        start = line.done
+        beside = max(min(heads_here, ready(base_qkv) - start), 0)
+        line.done = start + beside
+
+        @pl.loop(0, heads_here)
+        def _(head):
+            if beside > 0:
+                @pl.when(head < beside)
                 def _():
-                    mid_sum.send_block(part, which)
-
-    for copy in load_glu_grad:
-        copy.wait()
-    for n in range(width // 256):
-        cols = slice(n * 256, (n + 1) * 256)
-        r.down_g[:, cols] = tn(r.hid[...], r.gd[:, cols]).astype(BF16)
-    saves.append(copies.start(r.down_g, r.down_o))
-    for part in range(SUPER):
-        mid_sum.middle(part)
-    for n in range(width // 256):
-        cols = slice(n * 256, (n + 1) * 256)
-        r.left_g[cols, :] = tn(r.n2[:, cols], r.dl[...]).astype(BF16)
-    saves.append(copies.start(r.left_g, r.left_o))
-
-    def back_rows(total, values_ref, grad_ref, offset):
-        values = values_ref[offset : offset + step_rows, :]
-        norm = lax.rsqrt(jnp.mean(values * values, axis=1, keepdims=True) + epsilon)
-        m = values * norm
-        inner = jnp.mean(total * m, axis=1, keepdims=True)
-        return grad_ref[offset : offset + step_rows, :] + norm * (total - m * inner)
-
-    for part in range(SUPER):
-        for h in range(2):
-            mid_sum.finish(part, h)
-            for i in range(half // step_rows):
-                offset = (2 * part + h) * half + i * step_rows
-                total = mid_sum.total(part, h, i * step_rows, step_rows)
-                new = back_rows(total, r.mid, r.g, offset)
-                r.gm[offset : offset + step_rows, :] = new
-                r.ga[aligned(own_start + offset, step_rows), :] = new.astype(BF16)
-        second.start(part)
-    for n in range(width // 256):
-        cols = slice(n * 256, (n + 1) * 256)
-        r.right_g[cols, :] = tn(r.n2[:, cols], r.dr[...]).astype(BF16)
-    saves.append(copies.start(r.right_g, r.right_o))
-
-    per_block = block // 128
-
-    @pl.loop(0, 4)
-    def _(step):
-        @pl.when(step == 1)
-        def _():
-            for part in range(SUPER):
-                second.forward(part)
-        for which in (1, 2, 3):
-            @pl.when(step == which)
-            def _():
-                for part in range(SUPER):
-                    second.finish(part, which)
-        member = place.member(step)
-        for chunk in range(per_block):
-            rows = aligned(member * block + chunk * 128, 128)
-            grad_branch = nt(r.ga[rows, :], r.wo[...])
-            gate = r.gate[rows, :]
-            normed = r.heads[rows, :] * widen(r.scale[rows, :], local // 128)
-            grad_normed = grad_branch * gate
-            r.gn[rows, :] = grad_normed
-            r.dx[rows, 3 * local : 4 * local] = (grad_branch * normed).astype(BF16)
-            r.branch[rows, :] = (normed * gate).astype(BF16)
-            row_sums(grad_normed * normed, r.inner, member * per_block + chunk)
-    share.start()
-    r.out_g[...] = tn(r.branch[...], r.ga[...]).astype(BF16)
-    saves.append(copies.start(r.out_g, r.out_o))
-    for copy in load_attn:
-        copy.wait()
-    r.intot[...] = share.total() / width
-    for chunk in range(length // 128):
-        rows = slice(chunk * 128, (chunk + 1) * 128)
-        scale = widen(r.scale[rows, :], local // 128)
-        inner = widen(spread(r.intot[...], chunk), local // 128)
-        normed = r.heads[rows, :] * scale
-        r.dh[rows, :] = (scale * (r.gn[rows, :] - normed * inner)).astype(BF16)
-
-    tiles_here = length // size
-
-    @pl.loop(0, heads_here)
-    def _(head):
-        wide = aligned(head * 2 * HDIM, 2 * HDIM)
-        thin = aligned(head * HDIM, HDIM)
-        for col_tile in range(tiles_here):
-            cols = slice(col_tile * size, (col_tile + 1) * size)
-            keys = r.k[cols, wide]
-            values = r.v[cols, thin]
-            acc_key, acc_value = None, None
-            for row_tile in range(col_tile, tiles_here):
+                    line.tick(start + head)
+            wide = aligned(head * 2 * HDIM, 2 * HDIM)
+            thin = aligned(head * HDIM, HDIM)
+            for col_tile in range(tiles_here):
+                cols = slice(col_tile * size, (col_tile + 1) * size)
+                keys = r.k[cols, wide]
+                values = r.v[cols, thin]
+                acc_key, acc_value = None, None
+                for row_tile in range(col_tile, tiles_here):
+                    rows = slice(row_tile * size, (row_tile + 1) * size)
+                    queries = r.q[rows, wide]
+                    grads = r.dh[rows, thin]
+                    weight = tile_weight(r, first_head, head, row_tile, col_tile, size)
+                    scores = (nt(queries, keys) * weight).astype(BF16)
+                    pulled = (nt(grads, values) * weight).astype(BF16)
+                    term = nn(pulled, keys)
+                    if col_tile == 0:
+                        r.dq[rows, :] = term
+                    else:
+                        r.dq[rows, :] += term
+                    key_term = tn(pulled, queries)
+                    value_term = tn(scores, grads)
+                    acc_key = key_term if acc_key is None else acc_key + key_term
+                    acc_value = value_term if acc_value is None else acc_value + value_term
+                r.dk[cols, :] = acc_key
+                r.dx[cols, aligned(2 * local + head * HDIM, HDIM)] = acc_value.astype(BF16)
+            for row_tile in range(tiles_here):
                 rows = slice(row_tile * size, (row_tile + 1) * size)
-                queries = r.q[rows, wide]
-                grads = r.dh[rows, thin]
-                weight = tile_weight(r.dec, r.tiles, r.segc, r.segr, head, row_tile, col_tile, size)
-                scores = (nt(queries, keys) * weight).astype(BF16)
-                pulled = (nt(grads, values) * weight).astype(BF16)
-                term = nn(pulled, keys)
-                if col_tile == 0:
-                    r.dq[rows, :] = term
-                else:
-                    r.dq[rows, :] += term
-                key_term = tn(pulled, queries)
-                value_term = tn(scores, grads)
-                acc_key = key_term if acc_key is None else acc_key + key_term
-                acc_value = value_term if acc_value is None else acc_value + value_term
-            r.dk[cols, :] = acc_key
-            r.dx[cols, aligned(2 * local + head * HDIM, HDIM)] = acc_value.astype(BF16)
-        for row_tile in range(tiles_here):
-            rows = slice(row_tile * size, (row_tile + 1) * size)
-            cosine, sine = r.cos[rows, :], r.sin[rows, :]
-            for grad, lin, base in ((r.dq, r.ql, 0), (r.dk, r.kl, local)):
-                v = lin[rows, thin].astype(F32)
-                gate = 1.0 / (1.0 + jnp.exp(-v))
-                back = grad[rows, :HDIM] * cosine + grad[rows, HDIM:] * sine
-                back = back * (gate + v * gate * (1.0 - gate))
-                r.dx[rows, aligned(base + head * HDIM, HDIM)] = back.astype(BF16)
-
-    for copy in load_in:
-        copy.wait()
-    weights = (r.wq, r.wk, r.wv, r.wg)
-    for part in range(SUPER):
-        for step in (3, 1, 2, 0):
-            rows = aligned(place.member(step) * block + part * part_rows, part_rows)
-            total = None
-            for n, w in enumerate(weights):
-                term = nt(r.dx[rows, n * local : (n + 1) * local], w[...])
-                total = term if total is None else total + term
-            r.part2[rows, :] = total.astype(BF16)
-            in_sum.send_block(part, step)
-    for copy in load_in_grad:
-        copy.wait()
-
-    def attn_grad(n):
-        cols = slice(n * local, (n + 1) * local)
-        r.attn_g[n] = tn(r.n1[...], r.dx[:, cols]).astype(BF16)
-        saves.append(copies.start(r.attn_g.at[n], r.attn_o.at[n]))
-
-    attn_grad(0)
-    attn_grad(1)
-    for part in range(SUPER):
-        in_sum.middle(part)
-    attn_grad(2)
-    attn_grad(3)
-    for part in range(SUPER):
-        for h in range(2):
-            in_sum.finish(part, h)
-            for i in range(half // step_rows):
-                offset = (2 * part + h) * half + i * step_rows
-                total = in_sum.total(part, h, i * step_rows, step_rows)
-                r.go[offset : offset + step_rows, :] = back_rows(total, r.x, r.gm, offset)
-    for copy in saves:
-        copy.wait()
-    for group in (first, mid_sum, second, in_sum, share):
-        group.drain()
+                cosine, sine = r.cos[rows, :], r.sin[rows, :]
+                for grad, lin, base in ((r.dq, r.ql, 0), (r.dk, r.kl, local)):
+                    v = lin[rows, thin].astype(F32)
+                    gate = 1.0 / (1.0 + jnp.exp(-v))
+                    back = grad[rows, :HDIM] * cosine + grad[rows, HDIM:] * sine
+                    back = back * (gate + v * gate * (1.0 - gate))
+                    r.dx[rows, aligned(base + head * HDIM, HDIM)] = back.astype(BF16)
+
+        if turn + 1 < layers:
+            load(layer - 1, *attn_in)
+        await_loads(*in_in)
+        for part in range(SUPER):
+            for step in (3, 1, 2, 0):
+                rows = aligned(place.member(step) * block + part * part_rows, part_rows)
+                total = None
+                for n, w in enumerate((r.wq, r.wk, r.wv, r.wg)):
+                    term = nt(r.dx[rows, n * local : (n + 1) * local], w[...])
+                    total = term if total is None else total + term
+                r.part[rows, :] = total.astype(BF16)
+                in_sum.send_block(part, step)
+            line.pump(ready(base_qkv), 1)
+        for number in range(3):
+            in_grad_rows(number, base_qkv + number * local)
+            if number < SUPER:
+                in_sum.middle(number)
+            line.pump(ready(base_qkv + (number + 1) * local), 1)
+        if turn + 1 < layers:
+            load(layer - 1, *in_in, "n1")
+        for part in range(SUPER):
+            for h in range(2):
+                line.pump(ready(cfg.chunks * CHUNK), 1)
+                in_sum.finish(part, h)
+                for i in range(half // step_rows):
+                    offset = (2 * part + h) * half + i * step_rows
+                    rows = slice(offset, offset + step_rows)
+                    total = in_sum.total(part, h, i * step_rows, step_rows)
+                    values = getattr(r, "x%d" % layer)[rows, :].astype(F32)
+                    new = back_rows(total, values, r.gm[rows, :])
+                    if layer > 0:
+                        r.g[rows, :] = new
+                        r.gd[aligned(own_start + offset, step_rows), :] = new.astype(BF16)
+                    else:
+                        r.go[rows, :] = new.astype(BF16)
+            if layer > 0:
+                firsts[layer - 1].start(part)
+        in_sum.drain()
+    stats.finish()
+    line.finish()
 
 
 def call_kernel(body, cfg, inputs, outputs, scratch, collective_id, name):
@@ -1089,84 +1415,100 @@
     return dict(zip(outputs, result))
 
 
-def collective_scratch(cfg):
+def collective_scratch(cfg, copies, lead):
     dma = pltpu.SemaphoreType.DMA
     half = cfg.block // (2 * SUPER)
     out = {}
     for name in ("ag1", "ag2", "rs1", "rs2"):
-        out[name + "_send"] = dma((SUPER, 6))
-        out[name + "_recv"] = dma((SUPER, 6))
-    out["land1"] = pltpu.VMEM((SUPER, 6, half, cfg.width), BF16)
-    out["land2"] = pltpu.VMEM((SUPER, 6, half, cfg.width), BF16)
-    out["part1"] = pltpu.VMEM((cfg.length, cfg.width), BF16)
-    out["part2"] = pltpu.VMEM((cfg.length, cfg.width), BF16)
-    out["local_sem"] = dma((40,))
+        out[name + "_send"] = dma((*lead, SUPER, 6))
+        out[name + "_recv"] = dma((*lead, SUPER, 6))
+    for name in copies:
+        out["land" + name] = pltpu.VMEM((SUPER, 6, half, cfg.width), BF16)
+        out["part" + name] = pltpu.VMEM((cfg.length, cfg.width), BF16)
+    out["local_sem"] = dma((64,))
     return out
 
 
 def weight_scratch(cfg):
     v = pltpu.VMEM
-    return {
-        "wq": v((cfg.width, cfg.local), BF16), "wk": v((cfg.width, cfg.local), BF16),
-        "wv": v((cfg.width, cfg.local), BF16), "wg": v((cfg.width, cfg.local), BF16),
-        "wo": v((cfg.local, cfg.width), BF16), "wl": v((cfg.width, cfg.ff), BF16),
-        "wr": v((cfg.width, cfg.ff), BF16), "wd": v((cfg.ff, cfg.width), BF16),
-    }
+    return dict(
+        wq=v((cfg.width, cfg.local), BF16), wk=v((cfg.width, cfg.local), BF16),
+        wv=v((cfg.width, cfg.local), BF16), wg=v((cfg.width, cfg.local), BF16),
+        wo=v((cfg.local, cfg.width), BF16), wl=v((cfg.ff, cfg.width), BF16),
+        wr=v((cfg.ff, cfg.width), BF16), wd=v((cfg.ff, cfg.width), BF16),
+    )
+
+
+def table_scratch(cfg):
+    v = pltpu.VMEM
+    return dict(
+        segc=v((cfg.length, 128), F32), segf=v((8, 128), F32),
+        tiles=v((cfg.heads_here, 2, cfg.block, cfg.block), F32),
+    )
 
 
 def run_forward(cfg, x, tables, weights):
     v, dma, s = pltpu.VMEM, pltpu.SemaphoreType.DMA, jax.ShapeDtypeStruct
     rows, wide, local, ff, block = cfg.length, cfg.width, cfg.local, cfg.ff, cfg.block
-    inputs = {"x": (x, True), **{k: (a, True) for k, a in tables.items()}, **{k + "_h": (a, False) for k, a in weights.items()}}
-    kept = {
-        "n1": ((rows, wide), BF16), "ql": ((rows, local), BF16), "kl": ((rows, local), BF16),
-        "q": ((rows, 2 * local), BF16), "k": ((rows, 2 * local), BF16), "v": ((rows, local), BF16),
-        "gate": ((rows, local), F32), "heads": ((rows, local), F32), "mid": ((block, wide), F32),
-        "n2": ((rows, wide), BF16), "left": ((rows, ff), BF16), "right": ((rows, ff), BF16), "hid": ((rows, ff), BF16),
-    }
-    outputs = {
-        "xo": (s((block, wide), F32), True), "stat": (s((8, wide), F32), True), "ss_h": (s((8, 128), F32), False),
+    inputs = dict(x=(x, True), **{k: (a, True) for k, a in tables.items()}, **{k + "_h": (a, False) for k, a in weights.items()})
+    kept = dict(
+        n1=((rows, wide), BF16), ql=((rows, local), BF16), kl=((rows, local), BF16),
+        q=((rows, 2 * local), BF16), k=((rows, 2 * local), BF16), v=((rows, local), BF16),
+        gate=((rows, local), F32), heads=((rows, local), F32), mid=((block, wide), F32),
+        n2=((rows, wide), BF16), left=((rows, ff), BF16), right=((rows, ff), BF16), hid=((rows, ff), BF16),
+    )
+    outputs = dict(
+        xo=(s((block, wide), F32), True), stat=(s((8, 128), F32), True), ss_h=(s((8, 128), F32), False),
         **{k + "_h": (s(*a), False) for k, a in kept.items()},
-    }
-    scratch = {
-        **weight_scratch(cfg), **collective_scratch(cfg), **{k: v(*a) for k, a in kept.items()},
-        "tiles": v((cfg.heads_here, 2, block, block), F32), "u": v((rows, local), BF16),
-        "ss": v((8, 128), F32), "sstot": v((8, 128), F32), "scale": v((block, 128), F32),
-        "ss_land": v((3, 8, 128), F32), "ss_send": dma((3,)), "ss_recv": dma((3,)),
-    }
-    return call_kernel(fwd_kernel, cfg, inputs, outputs, scratch, 2 * cfg.layer, "layer_forward")
-
-
-def run_backward(cfg, g, x, saved, tables, weights):
+    )
+    scratch = dict(
+        **weight_scratch(cfg), **collective_scratch(cfg, ("1", "2"), ()), **table_scratch(cfg),
+        **{k: v(*a) for k, a in kept.items()}, u=v((rows, local), BF16), stat_wide=v((8, wide), F32),
+        ss=v((8, 128), F32), sstot=v((8, 128), F32), scale=v((block, 128), F32),
+        ss_land=v((3, 8, 128), F32), ss_send=dma((3,)), ss_recv=dma((3,)),
+    )
+    return call_kernel(fwd_kernel, cfg, inputs, outputs, scratch, cfg.layer, "layer_forward")
+
+
+SAVED = ("ss", "mid", "n1", "ql", "kl", "q", "k", "v", "gate", "heads", "n2", "left", "right", "hid")
+
+
+def run_backward(cfg, upstream, xs, saved, tables, weights):
     v, dma, s = pltpu.VMEM, pltpu.SemaphoreType.DMA, jax.ShapeDtypeStruct
     rows, wide, local, ff, block = cfg.length, cfg.width, cfg.local, cfg.ff, cfg.block
-    inputs = {
-        "g": (g, True), "x": (x, True), "mid": (saved["mid_h"], True),
-        **{k: (a, True) for k, a in tables.items()}, **{k + "_h": (a, False) for k, a in weights.items()},
-        **{k: (saved[k], False) for k in ("ss_h", "n1_h", "ql_h", "kl_h", "q_h", "k_h", "v_h", "gate_h", "heads_h", "n2_h", "left_h", "right_h", "hid_h")},
-    }
-    outputs = {
-        "go": (s((block, wide), F32), True), "attn_o": (s((4, wide, local), BF16), False),
-        "out_o": (s((local, wide), BF16), False), "left_o": (s((wide, ff), BF16), False),
-        "right_o": (s((wide, ff), BF16), False), "down_o": (s((ff, wide), BF16), False),
-    }
-    scratch = {
-        **weight_scratch(cfg), **collective_scratch(cfg),
-        "n1": v((rows, wide), BF16), "ql": v((rows, local), BF16), "kl": v((rows, local), BF16),
-        "q": v((rows, 2 * local), BF16), "k": v((rows, 2 * local), BF16), "v": v((rows, local), BF16),
-        "gate": v((rows, local), F32), "heads": v((rows, local), F32), "n2": v((rows, wide), BF16),
-        "left": v((rows, ff), BF16), "right": v((rows, ff), BF16), "hid": v((rows, ff), BF16),
-        "gd": v((rows, wide), BF16), "ga": v((rows, wide), BF16), "gm": v((block, wide), F32),
-        "dl": v((rows, ff), BF16), "dr": v((rows, ff), BF16), "gn": v((rows, local), F32),
-        "dh": v((rows, local), BF16), "branch": v((rows, local), BF16), "dx": v((rows, 4 * local), BF16),
-        "dq": v((rows, 2 * HDIM), F32), "dk": v((rows, 2 * HDIM), F32),
-        "attn_g": v((4, wide, local), BF16), "out_g": v((local, wide), BF16), "left_g": v((wide, ff), BF16),
-        "right_g": v((wide, ff), BF16), "down_g": v((ff, wide), BF16),
-        "tiles": v((cfg.heads_here, 2, block, block), F32), "scale": v((rows, 128), F32),
-        "sstot": v((8, 128), F32), "inner": v((8, 128), F32), "intot": v((8, 128), F32),
-        "inner_land": v((3, 8, 128), F32), "in_send": dma((3,)), "in_recv": dma((3,)),
-    }
-    return call_kernel(bwd_kernel, cfg, inputs, outputs, scratch, 2 * cfg.layer + 1, "layer_backward")
+    inputs = dict(up=(upstream, True), **{k: (a, True) for k, a in tables.items()}, **{k + "_h": (a, False) for k, a in weights.items()})
+    for layer in range(cfg.layers):
+        inputs["x%d" % layer] = (xs[layer], True)
+        inputs["stat%d" % layer] = (saved[layer]["stat"], True)
+        for key in SAVED:
+            inputs["%s%d_h" % (key, layer)] = (saved[layer][key + "_h"], False)
+    total_rows = cfg.chunks * CHUNK
+    outputs = dict(
+        go=(s((block, wide), BF16), True), stat_total=(s((8, 128), F32), True),
+        out_h=(s((cfg.layers * total_rows, wide), BF16), False),
+    )
+    small, ring, ring_sem = v((8, 128), F32), v((SLOTS, CHUNK // 2, wide), BF16), dma((SLOTS,))
+    scratch = dict(
+        **weight_scratch(cfg), **collective_scratch(cfg, ("",), (cfg.layers,)), **table_scratch(cfg),
+        n1=v((rows, wide), BF16), ql=v((rows, local), BF16), kl=v((rows, local), BF16),
+        q=v((rows, 2 * local), BF16), k=v((rows, 2 * local), BF16), v=v((rows, local), BF16),
+        gate=v((rows, local), F32), heads=v((rows, local), F32), n2=v((rows, wide), BF16),
+        left=v((rows, ff), BF16), right=v((rows, ff), BF16), hid=v((rows, ff), BF16),
+        gd=v((rows, wide), BF16), ga=v((rows, wide), BF16),
+        g=v((block, wide), F32), gm=v((block, wide), F32), mid=v((block, wide), F32),
+        dh=v((rows, local), BF16), branch=v((rows, local), BF16), dx=v((rows, 4 * local), BF16),
+        dq=v((rows, 2 * HDIM), F32), dk=v((rows, 2 * HDIM), F32),
+        grads=v((total_rows, wide), BF16), scale=v((rows, 128), F32),
+        ss=small, inner=small, intot=small,
+        inner_land=v((cfg.layers, 3, 8, 128), F32), in_send=dma((cfg.layers, 3)), in_recv=dma((cfg.layers, 3)),
+        pair_land=ring, right_land=ring, left_land=ring,
+        pair_send=ring_sem, pair_recv=ring_sem, right_send=ring_sem, right_recv=ring_sem, left_send=ring_sem,
+        left_recv=ring_sem, give_send=ring_sem, give_recv=ring_sem, keep_sem=ring_sem,
+        stat_mine=small, stat_square=small, stat_pair=small, stat_right=small, stat_left=small,
+        stat_land=v((3, 8, 128), F32), st_send=dma((3,)), st_recv=dma((3,)),
+        line_land=v((3, 8, 128), F32), line_send=dma((3,)), line_recv=dma((3,)),
+    )
+    return call_kernel(bwd_kernel, cfg, inputs, outputs, scratch, cfg.layers, "layers_backward")
 
 
 def per_device_square(
@@ -1177,49 +1519,54 @@
     length = segment_ids.shape[0]
     local, ff = query_proj.shape[2], left_proj.shape[2]
     heads_here = local // HDIM
-    positions = jnp.arange(length, dtype=F32)
-    frequency = jnp.exp(-math.log(10000.0) * jnp.arange(HDIM, dtype=F32) / HDIM)
+    positions = np.arange(length, dtype=np.float32)
+    frequency = np.exp(np.float32(-math.log(10000.0)) * np.arange(HDIM, dtype=np.float32) / np.float32(HDIM))
     angles = positions[:, None] * frequency[None, :]
-    head_index = (lax.axis_index("tensor") * heads_here + jnp.arange(heads_here)).astype(F32)
-    slopes = jnp.exp2(-8.0 * (head_index + 1.0) / HEADS)
-    fixed = {
-        "cos": jnp.cos(angles), "sin": jnp.sin(angles),
-        "segc": jnp.broadcast_to(segment_ids[:, None], (length, 128)),
-        "segr": jnp.broadcast_to(segment_ids[None, :], (8, length)),
-    }
-    weights = {
-        "wq": query_proj, "wk": key_proj, "wv": value_proj, "wg": gate_proj,
-        "wo": output_proj, "wl": left_proj, "wr": right_proj, "wd": down_proj,
-    }
-    current = tokens.astype(F32)
-    runs = []
+    slopes = np.exp2(-8.0 * (np.arange(HEADS) + 1.0) / HEADS)
+    decays = np.concatenate([-slopes * (1.0 - depth_start - depth_step * layer) for layer in range(layers)])
+    tables = dict(
+        cos=jnp.asarray(np.cos(angles)), sin=jnp.asarray(np.sin(angles)),
+        dec=jnp.asarray(np.broadcast_to(decays[:, None], (layers * HEADS, 128)).astype(np.float32)),
+        seg=segment_ids.reshape(8, length // 8),
+    )
+    weights = dict(
+        wq=query_proj, wk=key_proj, wv=value_proj, wg=gate_proj, wo=output_proj,
+        wl=jnp.swapaxes(left_proj, 1, 2), wr=jnp.swapaxes(right_proj, 1, 2), wd=down_proj,
+    )
+    ends = np.cumsum([0, ff, ff, ff, local, local, 3 * local]).tolist()
+    common = dict(
+        layers=layers, block=block, length=length, width=width, local=local, ff=ff, heads_here=heads_here,
+        pairs=lax.axis_size("dp") // 2, bases=ends, chunks=-(-ends[-1] // CHUNK),
+    )
+    current, xs, saved = tokens, [], []
     for layer in range(layers):
-        cfg = types.SimpleNamespace(
-            layer=layer, block=block, length=length, width=width, local=local, ff=ff, heads_here=heads_here
-        )
-        decay = -slopes * (1.0 - depth_start - depth_step * layer)
-        decay = jnp.concatenate([decay, jnp.zeros((8 - heads_here,), F32)])
-        tables = {**fixed, "dec": jnp.broadcast_to(decay[:, None], (8, 128))}
-        saved = run_forward(cfg, current, tables, weights)
-        runs.append((cfg, current, tables, saved))
-        current = saved["xo"]
-    stats = jnp.stack([jnp.sum(run[3]["stat"][:3], axis=1) for run in runs])
-    stat_sums = lax.psum(stats, ("dp", "tensor"))
-    rms_stats = jnp.sqrt(stat_sums / (length * lax.axis_size("dp") * width))
+        xs.append(current)
+        saved.append(run_forward(types.SimpleNamespace(layer=layer, **common), current, tables, weights))
+        current = saved[-1]["xo"]
     final_rows = current.astype(BF16)
-    gradient = upstream.astype(F32)
-    grads = [None] * layers
-    for layer in reversed(range(layers)):
-        cfg, x, tables, saved = runs[layer]
-        back = run_backward(cfg, gradient, x, saved, tables, weights)
-        gradient = back["go"]
-        grads[layer] = [back["attn_o"][0], back["attn_o"][1], back["attn_o"][2], back["attn_o"][3],
-                        back["out_o"], back["left_o"], back["right_o"], back["down_o"]]
-    totals = []
-    for member in range(8):
-        stacked = jnp.stack([grads[layer][member] for layer in range(layers)])
-        totals.append(lax.psum(stacked, "dp").astype(F32))
-    return (final_rows, gradient.astype(BF16), *totals, rms_stats)
+    back = run_backward(types.SimpleNamespace(**common), upstream, xs, saved, tables, weights)
+    stats = jnp.sum(back["stat_total"][: 3 * layers], axis=1).reshape(layers, 3)
+    rms_stats = jnp.sqrt(stats / (length * lax.axis_size("dp") * width))
+    grads = back["out_h"].reshape(layers, -1, width)
+
+    def rows(number):
+        return grads[:, ends[number] : ends[number + 1]]
+
+    def unfold(start):
+        piece = grads[:, start : start + local].reshape(layers, local, width // local, local)
+        return piece.transpose(0, 2, 1, 3).reshape(layers, width, local).astype(F32)
+
+    return (
+        final_rows,
+        back["go"],
+        *[unfold(ends[5] + number * local) for number in range(3)],
+        unfold(ends[4]),
+        rows(3).astype(F32),
+        jnp.swapaxes(rows(1).astype(F32), 1, 2),
+        jnp.swapaxes(rows(2).astype(F32), 1, 2),
+        rows(0).astype(F32),
+        rms_stats,
+    )
 
 
 def solution(mesh):

time: 697 us -> 452 us (0.65)
  waiting for transfers between devices: 249 us -> 0 us
  Pallas kernels: 324 us -> 397 us
  blocking collectives: 40.6 us -> 0 us
  other arithmetic: 33.5 us -> 19.1 us
  between operations: 14.6 us -> 1.12 us
    psum x1 -> x0, waiting for transfers between devices: 249 us -> none  [per_device_square(): totals.append(lax.psum(stacked, 'dp').astype(F32))]
    pallas_call x4 -> x3, Pallas kernels: 324 us -> 397 us  [call_kernel(): pl.pallas_call(functools.partial(body, cfg, names), out_shape=[shape for...]
    psum x1 -> x0, blocking collectives: 40.6 us -> none  [per_device_square(): stat_sums = lax.psum(stats, ('dp', 'tensor'))]
    convert_element_type x0 -> x8, local copies, waits for them, and re-layouts: none -> 24.7 us  [unfold(): return piece.transpose(0, 2, 1, 3).reshape(layers, width, local).astype(F32)]
    unnamed x46 -> x5, local copies, waits for them, and re-layouts: 20.6 us -> 0.8 us
    another operation x9 -> x0, other arithmetic: 11.1 us -> none  [the longest x8 11.1 us: per_device_square(): stacked = jnp.stack([grads[layer][member] for layer in range(layers)])]
    convert_element_type x9 -> x2, other arithmetic: 17.9 us -> 16.9 us  [the longest x1 10.5 us: per_device_square(): rows(0).astype(F32)]
  transfers between devices with their start and end apart: 1 -> 0, of which waited for: 1 -> 0; matrix products, arithmetic and copies ran while one was open for 0% -> 0% of each run, Pallas kernels for 0% -> 0%
where the time goes in v2:
time: 452 us; the launch traced here: 443 us
  Pallas kernels  397 us (88%)
  local copies, waits for them, and re-layouts  26.1 us (6%)
  other arithmetic  19.1 us (4%)
    pallas_call x3, Pallas kernels, call_kernel(): pl.pallas_call(functools.partial(body, cfg, names), out_shape=[shape for...  397 us
    convert_element_type x8, local copies, waits for them, and re-layouts, unfold(): return piece.transpose(0, 2, 1, 3).reshape(layers, width, local).astype(F32)  24.7 us
    convert_element_type x1, other arithmetic, per_device_square(): rows(0).astype(F32)  10.5 us

profile of v2, /device:TPU:0, one launch (start us, length us, event | category | flops | bytes accessed | tf_op | source)
XLA Modules:
  0.0 443.4 jit_solution(18394454024913728207)
XLA Ops:
  0.6 83.7 %layer_forward.2 = (f32[256,1024]{1,0:T(8,128)}, f32[8,128]{1,0:T(8,128)}, f32[8,128]{1,0:T(8,128)}, bf16[1024,1024]{1,0:T(8,128)(2,1)}, bf16[1024,256]{1,0:T(8,...) custom-call(bf16[256,1024]{1,0:T(8,128)(2,1)} %refs_13_.1, ...), custom_call_target="tpu_custom_call" | custom-call | tf_op jit(solution)/shard_map/layer_forward/pallas_call | solution.py:1404
  84.4 78.9 %layer_forward.3 = (f32[256,1024]{1,0:T(8,128)}, f32[8,128]{1,0:T(8,128)}, f32[8,128]{1,0:T(8,128)}, bf16[1024,1024]{1,0:T(8,128)(2,1)}, bf16[1024,256]{1,0:T(8,...) custom-call(f32[256,1024]{1,0:T(8,128)} %get-tuple-element.46.refs_0, ...), custom_call_target="tpu_custom_call" | custom-call | tf_op jit(solution)/shard_map/layer_forward/pallas_call | solution.py:1404
  163.2 2.1 convert_element_type.59
  165.3 234.4 %layers_backward.1 = (bf16[256,1024]{1,0:T(8,128)(2,1)}, f32[8,128]{1,0:T(8,128)}, bf16[6912,1024]{1,0:T(8,128)(2,1)}) custom-call(bf16[256,1024]{1,0:T(8,128)(2,1)} %refs_0_.3, f32[1024,128]{1,0:T(8,128)} %constant.11.clone.refs_1_, f32[1024,128]{1,0:T(8,128)} %constant.12.clone.refs_2_, f32[16,128]{1,0:T(8,128)} %constant.13.clone.refs_3_, ...), custom_call_target="tpu_custom_call" | custom-call | tf_op jit(solution)/shard_map/layers_backward/pallas_call | solution.py:1404
  399.8 6.5 %slice_convert_fusion.1 = (f32[2,256,1024]{2,1,0:T(8,128)}, f32[2,256,1024]{2,1,0:T(8,128)S(1)}, f32[2,256,1024]{2,1,0:T(8,128)}, f32[2,256,1024]{2,1,0:T(8,128)}, f32[2,256,1024]{2,1,0:T(8,128)}) fusion(bf16[2,3456,1024]{2,1,0:T(8,128)(2,1)} %bitcast.22), kind=kLoop, calls=%fused_computation.3 | loop fusion | flops 2621440 | bytes 15728640 | tf_op jit(solution)/shard_map/convert_element_type | solution.py:1564
  406.2 3.2 reshape.62
  409.4 3.3 copy.25
  412.7 3.2 reshape.63
  415.9 3.3 copy.26
  419.2 3.2 reshape.64
  422.3 3.3 copy.27
  425.6 2.0 reshape.65
  427.6 3.3 copy.28
  430.9 0.0 copy-start.1
  430.9 0.0 copy-start
  430.9 10.5 %slice_convert_fusion = (f32[2,704,1024]{2,1,0:T(8,128)}, f32[2,1024,704]{1,2,0:T(8,128)}, f32[2,1024,704]{1,2,0:T(8,128)}) fusion(bf16[2,3456,1024]{2,1,0:T(8,128)(2,1)} %bitcast.23), kind=kLoop, calls=%fused_computation.2 | loop fusion | flops 4325376 | bytes 25952256 | tf_op jit(solution)/shard_map/convert_element_type | solution.py:1567
  441.4 0.0 copy-done.1
  441.4 0.1 slice_reduce_fusion
  441.5 0.7 sqrt.7
  442.2 0.0 copy-done
  442.2 0.8 copy.30
  (1 shorter events, 0.0 us)
Async XLA Ops:
  430.9 10.5 %copy-start.1 = (f32[8,128]{1,0:T(8,128)S(1)}, f32[8,128]{1,0:T(8,128)}, u32[]{:S(2)}) copy-start(f32[8,128]{1,0:T(8,128)} %get-tuple-element.80) | copy-start | bytes 12292
  430.9 11.2 %copy-start = (bf16[256,1024]{1,0:T(8,128)(2,1)S(1)}, bf16[256,1024]{1,0:T(8,128)(2,1)}, u32[]{:S(2)}) copy-start(bf16[256,1024]{1,0:T(8,128)(2,1)} %get-tuple-element.101) | copy-start | bytes 1572868

commit v3 on v2

--- a/solution.py
+++ b/solution.py
@@ -455,8 +455,8 @@
 VMEM_LIMIT = 60 * 2**20
 SUPER = 2
 CHUNK = 128
-HOP = 2
-SLOTS = 12
+HOP = 4
+SLOTS = 20
 
 
 def nn(a, b):
@@ -584,6 +584,30 @@
                 self.wire(part, number).wait_send()
 
 
+def gather_stage(gather, block_fn, beside):
+    @pl.loop(0, 4 * SUPER)
+    def _(i):
+        mixed = i - SUPER
+        part = jnp.where(i < SUPER, i, jnp.where(i < 3 * SUPER, mixed // 2, i - 3 * SUPER))
+        step = jnp.where(i < SUPER, 0, jnp.where(i < 3 * SUPER, 1 + lax.rem(mixed, 2), 3))
+
+        @pl.when(i == SUPER)
+        def _():
+            for one in range(SUPER):
+                beside(one)
+                gather.forward(one)
+
+        @pl.when(i == 3 * SUPER)
+        def _():
+            beside(SUPER)
+
+        for which in (1, 2, 3):
+            @pl.when(step == which)
+            def _():
+                gather.finish(part, which)
+        block_fn(part, step)
+
+
 class Scatter:
     def __init__(self, place, buf, land, send, recv, block):
         self.place, self.buf, self.land, self.block = place, buf, land, block
@@ -610,9 +634,7 @@
         for first, second, owner, half in ((0, 4, 2, 0), (2, 5, 1, 1)):
             self.wire(part, first).wait_recv()
             rows = self.rows(owner, part, half)
-            self.buf[rows, :] = (
-                self.buf[rows, :].astype(F32) + self.land[part, first].astype(F32)
-            ).astype(BF16)
+            self.buf[rows, :] = self.buf[rows, :] + self.land[part, first]
             self.wire(part, second).start()
 
     def finish(self, part, half):
@@ -735,6 +757,9 @@
     second = Gather(place, r.n2, r.ag2_send, r.ag2_recv, block)
     out_sum = Scatter(place, r.part2, r.land2, r.rs2_send, r.rs2_recv, block)
     share = Share(place, r.ss, r.ss_land, r.ss_send, r.ss_recv)
+    third = Gather(place, r.gd, r.ag3_send, r.ag3_recv, block) if cfg.last else None
+    if cfg.last:
+        load_up = copies.start(r.up_h, r.gd.at[aligned(place.me * block, block), :])
     half, step_rows = first.half, 32
     own_start = place.me * block
 
@@ -781,6 +806,10 @@
     for v, h in ((r.n1, r.n1_h), (r.ql, r.ql_h), (r.kl, r.kl_h), (r.q, r.q_h), (r.k, r.k_h), (r.v, r.v_h), (r.gate, r.gate_h)):
         saves.append(copies.start(v, h))
 
+    if cfg.last:
+        load_up.wait()
+        for part in range(SUPER):
+            third.start(part)
     tiles_here = length // size
 
     @pl.loop(0, heads_here)
@@ -805,6 +834,9 @@
         row_sums(v * v, r.ss, chunk)
     share.start()
     saves.append(copies.start(r.heads, r.heads_h))
+    if cfg.last:
+        for part in range(SUPER):
+            third.forward(part)
     w_out.wait()
 
     part_rows = 2 * half
@@ -844,39 +876,31 @@
     saves.append(copies.start(r.mid, r.mid_h))
     for copy in w_glu:
         copy.wait()
-    for part in range(SUPER):
-
-        def glu(step):
-            rows = aligned(place.member(step) * block + part * part_rows, part_rows)
-            a = r.n2[rows, :]
-            left = nt(a, r.wl[...])
-            right = nt(a, r.wr[...])
-            hidden = (left * right).astype(BF16)
-            r.left[rows, :] = left.astype(BF16)
-            r.right[rows, :] = right.astype(BF16)
-            r.hid[rows, :] = hidden
-            r.part2[rows, :] = nn(hidden, r.wd[...]).astype(BF16)
-
-        @pl.loop(0, 4)
-        def _(step):
-            if part == 0:
-                @pl.when(step == 1)
-                def _():
-                    for other in range(SUPER):
-                        second.forward(other)
-            for which in (1, 2, 3):
-                @pl.when(step == which)
-                def _():
-                    second.finish(part, which)
-            glu(step)
-            for which in (1, 2, 3):
-                @pl.when(step == which)
-                def _():
-                    out_sum.send_block(part, which)
+    def glu(part, step):
+        rows = aligned(place.member(step) * block + part * part_rows, part_rows)
+        a = r.n2[rows, :]
+        left = nt(a, r.wl[...])
+        right = nt(a, r.wr[...])
+        hidden = (left * right).astype(BF16)
+        r.left[rows, :] = left.astype(BF16)
+        r.right[rows, :] = right.astype(BF16)
+        r.hid[rows, :] = hidden
+        r.part2[rows, :] = nn(hidden, r.wd[...]).astype(BF16)
+        for which in (1, 2, 3):
+            @pl.when(step == which)
+            def _():
+                out_sum.send_block(part, which)
+
+    gather_stage(second, glu, lambda i: None)
     for v, h in ((r.n2, r.n2_h), (r.left, r.left_h), (r.right, r.right_h), (r.hid, r.hid_h)):
         saves.append(copies.start(v, h))
     for part in range(SUPER):
         out_sum.middle(part)
+    if cfg.last:
+        for part in range(SUPER):
+            for which in (1, 2, 3):
+                third.finish(part, which)
+        saves.append(copies.start(r.gd, r.gd_h))
     for part in range(SUPER):
         for h in range(2):
             out_sum.finish(part, h)
@@ -893,7 +917,7 @@
     r.stat[...] = folded
     for copy in saves:
         copy.wait()
-    for group in (first, mid_sum, second, out_sum, share):
+    for group in (first, mid_sum, second, out_sum, share) + ((third,) if cfg.last else ()):
         group.drain()
 
 
@@ -961,7 +985,7 @@
         @pl.when(jnp.logical_not(start_here))
         def _():
             coming(k).wait_recv()
-            land[slot] = (land[slot].astype(F32) + self.r.grads[self.own(k), :].astype(F32)).astype(BF16)
+            land[slot] = land[slot] + self.r.grads[self.own(k), :]
 
         @pl.when(jnp.logical_not(ends_here))
         def _():
@@ -983,9 +1007,7 @@
             wire.wait_recv()
             wire.wait_send()
             slot = lax.rem(k, SLOTS)
-            r.grads[self.own(k), :] = (
-                r.grads[self.own(k), :].astype(F32) + r.pair_land[slot].astype(F32)
-            ).astype(BF16)
+            r.grads[self.own(k), :] = r.grads[self.own(k), :] + r.pair_land[slot]
 
         left_k = n - 1 - HOP * (last - place.at)
 
@@ -1035,6 +1057,12 @@
             @pl.loop(start, stop)
             def _(n):
                 self.tick(n)
+
+    def release(self, turn, rows):
+        needed = (turn - 1) * self.per + -(-rows // CHUNK) + 3 + HOP * self.place.last
+        if turn > 0 and needed > self.done:
+            self.pump(turn * self.per, needed - self.done)
+            assert self.done >= needed
 
     def finish(self):
         start, self.done = self.done, self.ticks
@@ -1131,6 +1159,7 @@
         for key in keys:
             loads[key].wait()
 
+    loads["gd"] = copies.start(r.gd_h, r.gd)
     glu_in = ("wd", "left", "right", "wl", "wr")
     glu_grad = ("hid", "n2", "mid")
     out_in = ("ss", "wo", "gate", "heads")
@@ -1146,16 +1175,12 @@
     @pl.loop(0, block // 32)
     def _(i):
         rows = aligned(i * 32, 32)
-        v = r.up[rows, :]
-        r.g[rows, :] = v.astype(F32)
-        r.gd[aligned(own_start + i * 32, 32), :] = v
+        r.g[rows, :] = r.up[rows, :].astype(F32)
 
     r.stat_mine[...] = jnp.zeros_like(r.stat_mine)
     for layer in range(layers):
         r.stat_mine[3 * layer : 3 * layer + 3, :] = getattr(r, "stat%d" % layer)[0:3, :]
     place.greet(True)
-    for part in range(SUPER):
-        firsts[layers - 1].start(part)
     stats.square()
     spread_segments(r, length)
     r.grads[base_end : cfg.chunks * CHUNK, :] = jnp.zeros((cfg.chunks * CHUNK - base_end, width), BF16)
@@ -1187,55 +1212,44 @@
         if turn == 0:
             stats.stage(0)
 
-        for part in range(SUPER):
-            start = line.done
-            beside = min(4, ready(0) - start)
-            line.done = start + max(beside, 0)
-
-            @pl.loop(0, 4)
-            def _(step):
-                if beside > 0:
-                    @pl.when(step < beside)
-                    def _():
-                        line.tick(start + step)
-                if part == 0:
-                    @pl.when(step == 1)
-                    def _():
-                        for other in range(SUPER):
-                            first.forward(other)
-                for which in (1, 2, 3):
-                    @pl.when(step == which)
-                    def _():
-                        first.finish(part, which)
-                rows = aligned(place.member(step) * block + part * part_rows, part_rows)
-                grad_hidden = nt(r.gd[rows, :], r.wd[...])
-                grad_left = (grad_hidden * r.right[rows, :].astype(F32)).astype(BF16)
-                grad_right = (grad_hidden * r.left[rows, :].astype(F32)).astype(BF16)
-                r.right[rows, :] = grad_left
-                r.left[rows, :] = grad_right
-                r.part[rows, :] = (nn(grad_left, r.wl[...]) + nn(grad_right, r.wr[...])).astype(BF16)
-                for which in (1, 2, 3):
-                    @pl.when(step == which)
-                    def _():
-                        mid_sum.send_block(part, which)
-        first.drain()
+        def glu_back(part, step):
+            rows = aligned(place.member(step) * block + part * part_rows, part_rows)
+            grad_hidden = nt(r.gd[rows, :], r.wd[...])
+            grad_left = (grad_hidden * r.right[rows, :].astype(F32)).astype(BF16)
+            grad_right = (grad_hidden * r.left[rows, :].astype(F32)).astype(BF16)
+            r.right[rows, :] = grad_left
+            r.left[rows, :] = grad_right
+            r.part[rows, :] = (nn(grad_left, r.wl[...]) + nn(grad_right, r.wr[...])).astype(BF16)
+            for which in (1, 2, 3):
+                @pl.when(step == which)
+                def _():
+                    mid_sum.send_block(part, which)
+
+        if turn == 0:
+            await_loads("gd")
+            for part in range(SUPER):
+                @pl.loop(0, 4)
+                def _(i):
+                    glu_back(part, 3 - i)
+        else:
+            gather_stage(first, glu_back, lambda i: line.pump(ready(0), 2))
+            first.drain()
         grad_left_ref, grad_right_ref = r.right, r.left
 
-        def glu_grad_rows(base, a_ref, b_ref, limit):
+        def glu_grad_rows(base, a_ref, b_ref):
+            line.release(turn, base + ff)
             for n in range(width // 256):
                 cols = slice(n * 256, (n + 1) * 256)
                 r.grads[base : base + ff, cols] = tn(a_ref[...], b_ref[:, cols]).astype(BF16)
-                if n % 2 == 1:
-                    line.pump(ready(limit), 1)
 
         await_loads(*glu_grad)
-        glu_grad_rows(base_down, r.hid, r.gd, 0)
+        glu_grad_rows(base_down, r.hid, r.gd)
         if turn == 0:
             stats.stage(1)
         for part in range(SUPER):
-            line.pump(ready(base_left), 1)
+            line.pump(ready(base_left), 2)
             mid_sum.middle(part)
-        glu_grad_rows(base_left, grad_left_ref, r.n2, base_left)
+        glu_grad_rows(base_left, grad_left_ref, r.n2)
         for part in range(SUPER):
             for h in range(2):
                 line.pump(ready(base_right), 1)
@@ -1251,33 +1265,16 @@
         mid_sum.drain()
         if turn == 0:
             stats.stage(2)
-        glu_grad_rows(base_right, grad_right_ref, r.n2, base_right)
+        glu_grad_rows(base_right, grad_right_ref, r.n2)
         if turn + 1 < layers:
             load(layer - 1, *glu_in, *glu_grad)
         if turn == 0:
             stats.stage(3)
-        start = line.done
-        beside = max(min(4, ready(base_out) - start), 0)
-        line.done = start + beside
-
-        @pl.loop(0, 4)
-        def _(step):
-            if beside > 0:
-                @pl.when(step < beside)
-                def _():
-                    line.tick(start + step)
-            @pl.when(step == 1)
-            def _():
-                for part in range(SUPER):
-                    second.forward(part)
-            for which in (1, 2, 3):
-                @pl.when(step == which)
-                def _():
-                    for part in range(SUPER):
-                        second.finish(part, which)
+        def out_back(part, step):
             member = place.member(step)
-            for chunk in range(per_block):
-                rows = aligned(member * block + chunk * 128, 128)
+            for chunk in range(part_rows // 128):
+                number = part * (part_rows // 128) + chunk
+                rows = aligned(member * block + number * 128, 128)
                 grad_branch = nt(r.ga[rows, :], r.wo[...])
                 gate = r.gate[rows, :]
                 normed = r.heads[rows, :] * widen(r.scale[rows, :], local // 128)
@@ -1285,13 +1282,17 @@
                 r.dx[rows, 3 * local : 4 * local] = (grad_branch * normed).astype(BF16)
                 r.branch[rows, :] = (normed * gate).astype(BF16)
                 r.gate[rows, :] = grad_normed
-                row_sums(grad_normed * normed, r.inner, member * per_block + chunk)
+                row_sums(grad_normed * normed, r.inner, member * per_block + number)
+
+        gather_stage(second, out_back, lambda i: line.pump(ready(base_out), 2))
         share.start()
+        line.release(turn, base_gate)
         r.grads[base_out : base_out + local, :] = tn(r.branch[...], r.ga[...]).astype(BF16)
         line.pump(ready(base_gate), 1)
 
         def in_grad_rows(number, base):
             cols = slice(number * local, (number + 1) * local)
+            line.release(turn, base + local)
             for n in range(width // local):
                 part_grad = tn(r.n1[:, n * local : (n + 1) * local], r.dx[:, cols])
                 r.grads[base : base + local, n * local : (n + 1) * local] = part_grad.astype(BF16)
@@ -1311,16 +1312,8 @@
         second.drain()
         if turn + 1 < layers:
             load(layer - 1, *out_in)
-        start = line.done
-        beside = max(min(heads_here, ready(base_qkv) - start), 0)
-        line.done = start + beside
-
         @pl.loop(0, heads_here)
         def _(head):
-            if beside > 0:
-                @pl.when(head < beside)
-                def _():
-                    line.tick(start + head)
             wide = aligned(head * 2 * HDIM, 2 * HDIM)
             thin = aligned(head * HDIM, HDIM)
             for col_tile in range(tiles_here):
@@ -1359,6 +1352,10 @@
         if turn + 1 < layers:
             load(layer - 1, *attn_in)
         await_loads(*in_in)
+        last = turn == layers - 1
+        if last:
+            for number in range(3):
+                in_grad_rows(number, base_qkv + number * local)
         for part in range(SUPER):
             for step in (3, 1, 2, 0):
                 rows = aligned(place.member(step) * block + part * part_rows, part_rows)
@@ -1368,12 +1365,14 @@
                     total = term if total is None else total + term
                 r.part[rows, :] = total.astype(BF16)
                 in_sum.send_block(part, step)
-            line.pump(ready(base_qkv), 1)
+            if last:
+                line.pump(ready(cfg.chunks * CHUNK), 2)
         for number in range(3):
-            in_grad_rows(number, base_qkv + number * local)
+            if not last:
+                in_grad_rows(number, base_qkv + number * local)
+            line.pump(ready(base_qkv + (number + 1) * local), 2)
             if number < SUPER:
                 in_sum.middle(number)
-            line.pump(ready(base_qkv + (number + 1) * local), 1)
         if turn + 1 < layers:
             load(layer - 1, *in_in, "n1")
         for part in range(SUPER):
@@ -1408,7 +1407,7 @@
         out_specs=[vmem if placed else anywhere for _, placed in outputs.values()],
         scratch_shapes=list(scratch.values()),
         compiler_params=pltpu.CompilerParams(
-            collective_id=collective_id, has_side_effects=True, vmem_limit_bytes=VMEM_LIMIT
+            collective_id=collective_id, has_side_effects=collective_id is not None, vmem_limit_bytes=VMEM_LIMIT
         ),
         name=name,
     )(*[array for array, _ in inputs.values()])
@@ -1447,7 +1446,7 @@
     )
 
 
-def run_forward(cfg, x, tables, weights):
+def run_forward(cfg, x, upstream, tables, weights):
     v, dma, s = pltpu.VMEM, pltpu.SemaphoreType.DMA, jax.ShapeDtypeStruct
     rows, wide, local, ff, block = cfg.length, cfg.width, cfg.local, cfg.ff, cfg.block
     inputs = dict(x=(x, True), **{k: (a, True) for k, a in tables.items()}, **{k + "_h": (a, False) for k, a in weights.items()})
@@ -1467,6 +1466,10 @@
         ss=v((8, 128), F32), sstot=v((8, 128), F32), scale=v((block, 128), F32),
         ss_land=v((3, 8, 128), F32), ss_send=dma((3,)), ss_recv=dma((3,)),
     )
+    if cfg.last:
+        inputs.update(up_h=(upstream, False))
+        outputs.update(gd_h=(s((rows, wide), BF16), False))
+        scratch.update(gd=v((rows, wide), BF16), ag3_send=dma((SUPER, 6)), ag3_recv=dma((SUPER, 6)))
     return call_kernel(fwd_kernel, cfg, inputs, outputs, scratch, cfg.layer, "layer_forward")
 
 
@@ -1476,7 +1479,7 @@
 def run_backward(cfg, upstream, xs, saved, tables, weights):
     v, dma, s = pltpu.VMEM, pltpu.SemaphoreType.DMA, jax.ShapeDtypeStruct
     rows, wide, local, ff, block = cfg.length, cfg.width, cfg.local, cfg.ff, cfg.block
-    inputs = dict(up=(upstream, True), **{k: (a, True) for k, a in tables.items()}, **{k + "_h": (a, False) for k, a in weights.items()})
+    inputs = dict(up=(upstream, True), gd_h=(saved[-1]["gd_h"], False), **{k: (a, True) for k, a in tables.items()}, **{k + "_h": (a, False) for k, a in weights.items()})
     for layer in range(cfg.layers):
         inputs["x%d" % layer] = (xs[layer], True)
         inputs["stat%d" % layer] = (saved[layer]["stat"], True)
@@ -1511,6 +1514,75 @@
     return call_kernel(bwd_kernel, cfg, inputs, outputs, scratch, cfg.layers, "layers_backward")
 
 
+def widen_kernel(cfg, names, *refs):
+    r = namespace(names, refs)
+    tasks = []
+    for layer in range(cfg.layers):
+        for number, target in enumerate((r.down, r.left, r.right, r.out)):
+            start, stop = cfg.bases[number], cfg.bases[number + 1]
+            rows = (stop - start) // 2 if stop - start > 512 else stop - start
+            for first in range(start, stop, rows):
+                tasks.append((layer, first, rows, [(target.at[layer, pl.ds(first - start, rows), :], slice(None))]))
+        for number, target in enumerate((r.gate, r.query, r.key, r.value)):
+            pieces = [
+                (target.at[layer, pl.ds(n * cfg.local, cfg.local), :], slice(n * cfg.local, (n + 1) * cfg.local))
+                for n in range(cfg.width // cfg.local)
+            ]
+            tasks.append((layer, cfg.bases[4] + number * cfg.local, cfg.local, pieces))
+    depth = 3
+
+    def fetch(task):
+        layer, first, rows, _ = tasks[task]
+        start = layer * cfg.chunks * CHUNK + first
+        slot = task % depth
+        return pltpu.make_async_copy(r.grads.at[pl.ds(start, rows), :], r.narrow.at[slot, pl.ds(0, rows), :], r.in_sem.at[slot])
+
+    def store(task):
+        _, _, rows, pieces = tasks[task]
+        slot = task % depth
+        return [
+            pltpu.make_async_copy(r.wide.at[slot, pl.ds(0, rows), lanes], target, r.out_sem.at[slot, n])
+            for n, (target, lanes) in enumerate(pieces)
+        ]
+
+    for task in range(min(depth, len(tasks))):
+        fetch(task).start()
+    for task in range(len(tasks)):
+        slot, rows = task % depth, tasks[task][2]
+        fetch(task).wait()
+        if task >= depth:
+            for copy in store(task - depth):
+                copy.wait()
+
+        @pl.loop(0, rows // 32)
+        def _(i):
+            part = aligned(i * 32, 32)
+            r.wide[slot, part, :] = r.narrow[slot, part, :].astype(F32)
+
+        for copy in store(task):
+            copy.start()
+        if task + depth < len(tasks):
+            fetch(task + depth).start()
+    for task in range(max(len(tasks) - depth, 0), len(tasks)):
+        for copy in store(task):
+            copy.wait()
+
+
+def run_widen(cfg, grads):
+    v, dma, s = pltpu.VMEM, pltpu.SemaphoreType.DMA, jax.ShapeDtypeStruct
+    thin, flat = s((cfg.layers, cfg.width, cfg.local), F32), s((cfg.layers, cfg.ff, cfg.width), F32)
+    outputs = dict(
+        down=(flat, False), left=(flat, False), right=(flat, False), out=(s((cfg.layers, cfg.local, cfg.width), F32), False),
+        gate=(thin, False), query=(thin, False), key=(thin, False), value=(thin, False),
+    )
+    rows = max(cfg.ff // 2, cfg.local, 512)
+    scratch = dict(
+        narrow=v((3, rows, cfg.width), BF16), wide=v((3, rows, cfg.width), F32),
+        in_sem=dma((3,)), out_sem=dma((3, cfg.width // cfg.local)),
+    )
+    return call_kernel(widen_kernel, cfg, dict(grads=(grads, False)), outputs, scratch, None, "widen_gradients")
+
+
 def per_device_square(
     tokens, upstream, segment_ids, query_proj, key_proj, value_proj, gate_proj, output_proj, left_proj, right_proj, down_proj
 ):
@@ -1541,31 +1613,17 @@
     current, xs, saved = tokens, [], []
     for layer in range(layers):
         xs.append(current)
-        saved.append(run_forward(types.SimpleNamespace(layer=layer, **common), current, tables, weights))
+        cfg = types.SimpleNamespace(layer=layer, last=layer == layers - 1, **common)
+        saved.append(run_forward(cfg, current, upstream, tables, weights))
         current = saved[-1]["xo"]
     final_rows = current.astype(BF16)
     back = run_backward(types.SimpleNamespace(**common), upstream, xs, saved, tables, weights)
     stats = jnp.sum(back["stat_total"][: 3 * layers], axis=1).reshape(layers, 3)
     rms_stats = jnp.sqrt(stats / (length * lax.axis_size("dp") * width))
-    grads = back["out_h"].reshape(layers, -1, width)
-
-    def rows(number):
-        return grads[:, ends[number] : ends[number + 1]]
-
-    def unfold(start):
-        piece = grads[:, start : start + local].reshape(layers, local, width // local, local)
-        return piece.transpose(0, 2, 1, 3).reshape(layers, width, local).astype(F32)
-
+    wide = run_widen(types.SimpleNamespace(**common), back["out_h"])
     return (
-        final_rows,
-        back["go"],
-        *[unfold(ends[5] + number * local) for number in range(3)],
-        unfold(ends[4]),
-        rows(3).astype(F32),
-        jnp.swapaxes(rows(1).astype(F32), 1, 2),
-        jnp.swapaxes(rows(2).astype(F32), 1, 2),
-        rows(0).astype(F32),
-        rms_stats,
+        final_rows, back["go"], wide["query"], wide["key"], wide["value"], wide["gate"], wide["out"],
+        jnp.swapaxes(wide["left"], 1, 2), jnp.swapaxes(wide["right"], 1, 2), wide["down"], rms_stats,
     )
 
 

time: 452 us -> 422 us (0.934)
  local copies, waits for them, and re-layouts: 26.1 us -> 1.45 us
  other arithmetic: 19.1 us -> 2.22 us
  Pallas kernels: 397 us -> 410 us
    convert_element_type x8 -> x0, local copies, waits for them, and re-layouts: 24.7 us -> none  [unfold(): return piece.transpose(0, 2, 1, 3).reshape(layers, width, local).astype(F32)]
    convert_element_type x2 -> x0, other arithmetic: 16.9 us -> none  [the longest x1 10.5 us: per_device_square(): rows(0).astype(F32)]
    pallas_call x3 -> x4, Pallas kernels: 397 us -> 410 us  [call_kernel(): pl.pallas_call(functools.partial(body, cfg, names), out_shape=[shape for...]
where the time goes in v3:
time: 422 us; the launch traced here: 415 us
  Pallas kernels  410 us (97%)
    pallas_call x4, Pallas kernels, call_kernel(): pl.pallas_call(functools.partial(body, cfg, names), out_shape=[shape for...  410 us

profile of v3, /device:TPU:0, one launch (start us, length us, event | category | flops | bytes accessed | tf_op | source)
XLA Modules:
  0.0 414.8 jit_solution(1970249129309801516)
XLA Ops:
  0.6 83.7 %layer_forward.2 = (f32[256,1024]{1,0:T(8,128)}, f32[8,128]{1,0:T(8,128)}, f32[8,128]{1,0:T(8,128)}, bf16[1024,1024]{1,0:T(8,128)(2,1)}, bf16[1024,256]{1,0:T(8,...) custom-call(bf16[256,1024]{1,0:T(8,128)(2,1)} %refs_14_.1, ...), custom_call_target="tpu_custom_call" | custom-call | tf_op jit(solution)/shard_map/layer_forward/pallas_call | solution.py:1403
  84.4 92.6 %layer_forward.3 = (f32[256,1024]{1,0:T(8,128)}, f32[8,128]{1,0:T(8,128)}, f32[8,128]{1,0:T(8,128)}, bf16[1024,1024]{1,0:T(8,128)(2,1)}, bf16[1024,256]{1,0:T(8,...) custom-call(f32[256,1024]{1,0:T(8,128)} %get-tuple-element.55.refs_0, ...), custom_call_target="tpu_custom_call" | custom-call | tf_op jit(solution)/shard_map/layer_forward/pallas_call | solution.py:1403
  177.0 2.1 convert_element_type.3
  179.1 218.6 %layers_backward.1 = (bf16[256,1024]{1,0:T(8,128)(2,1)}, f32[8,128]{1,0:T(8,128)}, bf16[6912,1024]{1,0:T(8,128)(2,1)}) custom-call(bf16[256,1024]{1,0:T(8,128)(2,1)} %refs_0_.3, bf16[1024,1024]{1,0:T(8,128)(2,1)} %get-tuple-element.57.refs_1_, f32[1024,128]{1,0:T(8,128)} %constant.11.clone.refs_1_.refs_2_, f32[1024,128]{1,0:T(8,128)} %constant.12.clone.refs_2_.refs_3_, ...), custom_call_target="tpu_custom_call" | custom-call | tf_op jit(solution)/shard_map/layers_backward/pallas_call | solution.py:1403
  397.6 0.0 copy-start.1
  397.6 0.0 copy-start
  397.7 15.1 %widen_gradients.1 = (f32[2,704,1024]{2,1,0:T(8,128)}, f32[2,704,1024]{2,1,0:T(8,128)}, f32[2,704,1024]{2,1,0:T(8,128)}, f32[2,256,1024]{2,1,0:T(8,128)}, f32[2,...) custom-call(bf16[6912,1024]{1,0:T(8,128)(2,1)} %get-tuple-element.89.refs_0_), custom_call_target="tpu_custom_call" | custom-call | tf_op jit(solution)/shard_map/widen_gradients/pallas_call | solution.py:1403
  412.8 0.0 copy-done.1
  412.8 0.1 slice_reduce_fusion
  412.9 0.7 sqrt.7
  413.6 0.0 copy-done
  413.6 0.8 copy.26
  (1 shorter events, 0.0 us)
Async XLA Ops:
  397.6 15.2 %copy-start.1 = (f32[8,128]{1,0:T(8,128)S(1)}, f32[8,128]{1,0:T(8,128)}, u32[]{:S(2)}) copy-start(f32[8,128]{1,0:T(8,128)} %get-tuple-element.98) | copy-start | bytes 12292
  397.6 15.9 %copy-start = (bf16[256,1024]{1,0:T(8,128)(2,1)S(1)}, bf16[256,1024]{1,0:T(8,128)(2,1)}, u32[]{:S(2)}) copy-start(bf16[256,1024]{1,0:T(8,128)(2,1)} %get-tuple-element.111) | copy-start | bytes 1572868

commit v4 on v3

--- a/solution.py
+++ b/solution.py
@@ -455,8 +455,8 @@
 VMEM_LIMIT = 60 * 2**20
 SUPER = 2
 CHUNK = 128
-HOP = 4
-SLOTS = 20
+HOP = 3
+SLOTS = 16
 
 
 def nn(a, b):
@@ -908,7 +908,7 @@
                 offset = (2 * part + h) * half + i * step_rows
                 glu_rows = out_sum.total(part, h, i * step_rows, step_rows)
                 after = r.mid[offset : offset + step_rows, :] + glu_rows
-                r.xo[offset : offset + step_rows, :] = after
+                r.xo[offset : offset + step_rows, :] = after.astype(r.xo.dtype)
                 add_stat(1, glu_rows)
                 add_stat(2, after)
     folded = r.stat_wide[:, :128]
@@ -921,6 +921,10 @@
         group.drain()
 
 
+def turns_of(k, size, count):
+    return sum(((k >= size * n).astype(jnp.int32) for n in range(1, -(-count // size))), jnp.int32(0))
+
+
 class Line:
     def __init__(self, cfg, place, r):
         self.place, self.r = place, r
@@ -930,25 +934,30 @@
         self.ticks = self.count + 3 + HOP * place.last
         self.done = 0
 
+    def slot(self, k):
+        return k - SLOTS * turns_of(k, SLOTS, self.count)
+
     def rows(self, k, core):
-        return aligned(lax.rem(k, self.per) * CHUNK + core * self.half, self.half)
+        place = k - self.per * turns_of(k, self.per, self.count)
+        return aligned(place * CHUNK + core * self.half, self.half)
 
     def own(self, k):
         return self.rows(k, self.place.core)
 
     def out_rows(self, k, core):
-        layer = self.layers - 1 - k // self.per
-        start = layer * self.rows_each + lax.rem(k, self.per) * CHUNK + core * self.half
+        turn = turns_of(k, self.per, self.count)
+        place = (self.layers - 1 - turn) * self.per + k - turn * self.per
+        start = place * CHUNK + core * self.half
         return aligned(start, self.half)
 
     def pair(self, k):
-        slot = lax.rem(k, SLOTS)
+        slot = self.slot(k)
         r = self.r
         return Wire(self.place.partner(), r.pair_send.at[slot], r.pair_recv.at[slot],
                     r.grads.at[self.rows(k, 1 - self.place.core)], r.pair_land.at[slot], r.pair_land.at[slot])
 
     def hop(self, k, land, send, recv, device):
-        slot = lax.rem(k, SLOTS)
+        slot = self.slot(k)
         return Wire(device, send.at[slot], recv.at[slot], land.at[slot], land.at[slot], land.at[slot])
 
     def going_right(self, k):
@@ -964,19 +973,19 @@
         return self.hop(k, self.r.left_land, self.r.left_send, self.r.left_recv, self.place.right())
 
     def result(self, k):
-        slot, r = lax.rem(k, SLOTS), self.r
+        slot, r = self.slot(k), self.r
         return Wire(self.place.partner(), r.give_send.at[slot], r.give_recv.at[slot],
                     r.grads.at[self.own(k)], r.out_h.at[self.out_rows(k, self.place.core)],
                     r.out_h.at[self.out_rows(k, 1 - self.place.core)])
 
     def keep(self, k):
-        slot, r = lax.rem(k, SLOTS), self.r
+        slot, r = self.slot(k), self.r
         return pltpu.make_async_copy(
             r.grads.at[self.own(k)], r.out_h.at[self.out_rows(k, self.place.core)], r.keep_sem.at[slot]
         )
 
     def one_way(self, k, land, start_here, coming, ends_here, going):
-        slot = lax.rem(k, SLOTS)
+        slot = self.slot(k)
 
         @pl.when(start_here)
         def _():
@@ -1006,7 +1015,7 @@
             wire = self.pair(k)
             wire.wait_recv()
             wire.wait_send()
-            slot = lax.rem(k, SLOTS)
+            slot = self.slot(k)
             r.grads[self.own(k), :] = r.grads[self.own(k), :] + r.pair_land[slot]
 
         left_k = n - 1 - HOP * (last - place.at)
@@ -1033,7 +1042,7 @@
             def _():
                 self.going_left(full_k).wait_send()
 
-            slot = lax.rem(full_k, SLOTS)
+            slot = self.slot(full_k)
             own = self.own(full_k)
             total = r.right_land[slot].astype(F32) + r.left_land[slot].astype(F32) - r.grads[own, :].astype(F32)
             r.grads[own, :] = total.astype(BF16)
@@ -1246,13 +1255,16 @@
         glu_grad_rows(base_down, r.hid, r.gd)
         if turn == 0:
             stats.stage(1)
+        line.pump(ready(base_left), 1)
+        mid_sum.middle(0)
+        glu_grad_rows(base_left, grad_left_ref, r.n2)
+        line.pump(ready(base_right), 1)
+        for part in range(1, SUPER):
+            mid_sum.middle(part)
+        glu_grad_rows(base_right, grad_right_ref, r.n2)
         for part in range(SUPER):
-            line.pump(ready(base_left), 2)
-            mid_sum.middle(part)
-        glu_grad_rows(base_left, grad_left_ref, r.n2)
-        for part in range(SUPER):
+            line.pump(ready(base_out), 2 - part)
             for h in range(2):
-                line.pump(ready(base_right), 1)
                 mid_sum.finish(part, h)
                 for i in range(half // step_rows):
                     offset = (2 * part + h) * half + i * step_rows
@@ -1265,7 +1277,6 @@
         mid_sum.drain()
         if turn == 0:
             stats.stage(2)
-        glu_grad_rows(base_right, grad_right_ref, r.n2)
         if turn + 1 < layers:
             load(layer - 1, *glu_in, *glu_grad)
         if turn == 0:
@@ -1312,6 +1323,8 @@
         second.drain()
         if turn + 1 < layers:
             load(layer - 1, *out_in)
+        line.pump(ready(base_qkv), 1)
+
         @pl.loop(0, heads_here)
         def _(head):
             wide = aligned(head * 2 * HDIM, 2 * HDIM)
@@ -1365,19 +1378,18 @@
                     total = term if total is None else total + term
                 r.part[rows, :] = total.astype(BF16)
                 in_sum.send_block(part, step)
-            if last:
-                line.pump(ready(cfg.chunks * CHUNK), 2)
+            line.pump(ready(cfg.chunks * CHUNK if last else base_qkv), 2 if last else 1)
         for number in range(3):
             if not last:
                 in_grad_rows(number, base_qkv + number * local)
-            line.pump(ready(base_qkv + (number + 1) * local), 2)
+            line.pump(ready(base_qkv + (number + 1) * local), 2 if last else 1)
             if number < SUPER:
                 in_sum.middle(number)
         if turn + 1 < layers:
             load(layer - 1, *in_in, "n1")
         for part in range(SUPER):
+            line.pump(ready(cfg.chunks * CHUNK), 2)
             for h in range(2):
-                line.pump(ready(cfg.chunks * CHUNK), 1)
                 in_sum.finish(part, h)
                 for i in range(half // step_rows):
                     offset = (2 * part + h) * half + i * step_rows
@@ -1457,7 +1469,7 @@
         n2=((rows, wide), BF16), left=((rows, ff), BF16), right=((rows, ff), BF16), hid=((rows, ff), BF16),
     )
     outputs = dict(
-        xo=(s((block, wide), F32), True), stat=(s((8, 128), F32), True), ss_h=(s((8, 128), F32), False),
+        xo=(s((block, wide), BF16 if cfg.last else F32), True), stat=(s((8, 128), F32), True), ss_h=(s((8, 128), F32), False),
         **{k + "_h": (s(*a), False) for k, a in kept.items()},
     )
     scratch = dict(
@@ -1616,13 +1628,12 @@
         cfg = types.SimpleNamespace(layer=layer, last=layer == layers - 1, **common)
         saved.append(run_forward(cfg, current, upstream, tables, weights))
         current = saved[-1]["xo"]
-    final_rows = current.astype(BF16)
     back = run_backward(types.SimpleNamespace(**common), upstream, xs, saved, tables, weights)
     stats = jnp.sum(back["stat_total"][: 3 * layers], axis=1).reshape(layers, 3)
     rms_stats = jnp.sqrt(stats / (length * lax.axis_size("dp") * width))
     wide = run_widen(types.SimpleNamespace(**common), back["out_h"])
     return (
-        final_rows, back["go"], wide["query"], wide["key"], wide["value"], wide["gate"], wide["out"],
+        current, back["go"], wide["query"], wide["key"], wide["value"], wide["gate"], wide["out"],
         jnp.swapaxes(wide["left"], 1, 2), jnp.swapaxes(wide["right"], 1, 2), wide["down"], rms_stats,
     )
 

time: 422 us -> 418 us (level)
  no operation moved by 1% of the time
where the time goes in v4:
time: 418 us; the launch traced here: 411 us
  Pallas kernels  407 us (97%)
    pallas_call x4, Pallas kernels, call_kernel(): pl.pallas_call(functools.partial(body, cfg, names), out_shape=[shape for...  407 us

profile of v4, /device:TPU:0, one launch (start us, length us, event | category | flops | bytes accessed | tf_op | source)
XLA Modules:
  0.0 410.8 jit_solution(16723546663499540078)
XLA Ops:
  0.6 83.7 %layer_forward.2 = (f32[256,1024]{1,0:T(8,128)}, f32[8,128]{1,0:T(8,128)}, f32[8,128]{1,0:T(8,128)}, bf16[1024,1024]{1,0:T(8,128)(2,1)}, bf16[1024,256]{1,0:T(8,...) custom-call(bf16[256,1024]{1,0:T(8,128)(2,1)} %refs_14_.1, ...), custom_call_target="tpu_custom_call" | custom-call | tf_op jit(solution)/shard_map/layer_forward/pallas_call | solution.py:1415
  84.3 92.4 %layer_forward.3 = (bf16[256,1024]{1,0:T(8,128)(2,1)}, f32[8,128]{1,0:T(8,128)}, f32[8,128]{1,0:T(8,128)}, bf16[1024,1024]{1,0:T(8,128)(2,1)}, bf16[1024,256]{1,...) custom-call(f32[256,1024]{1,0:T(8,128)} %get-tuple-element.55.refs_0, ...), custom_call_target="tpu_custom_call" | custom-call | tf_op jit(solution)/shard_map/layer_forward/pallas_call | solution.py:1415
  176.7 216.1 %layers_backward.1 = (bf16[256,1024]{1,0:T(8,128)(2,1)}, f32[8,128]{1,0:T(8,128)}, bf16[6912,1024]{1,0:T(8,128)(2,1)}) custom-call(bf16[256,1024]{1,0:T(8,128)(2,1)} %refs_0_.3, bf16[1024,1024]{1,0:T(8,128)(2,1)} %get-tuple-element.57.refs_1_, f32[1024,128]{1,0:T(8,128)} %constant.11.clone.refs_1_.refs_2_, f32[1024,128]{1,0:T(8,128)} %constant.12.clone.refs_2_.refs_3_, ...), custom_call_target="tpu_custom_call" | custom-call | tf_op jit(solution)/shard_map/layers_backward/pallas_call | solution.py:1415
  392.9 0.0 copy-start.2
  392.9 0.0 copy-start
  392.9 0.0 copy-start.1
  392.9 15.2 %widen_gradients.1 = (f32[2,704,1024]{2,1,0:T(8,128)}, f32[2,704,1024]{2,1,0:T(8,128)}, f32[2,704,1024]{2,1,0:T(8,128)}, f32[2,256,1024]{2,1,0:T(8,128)}, f32[2,...) custom-call(bf16[6912,1024]{1,0:T(8,128)(2,1)} %get-tuple-element.89.refs_0_), custom_call_target="tpu_custom_call" | custom-call | tf_op jit(solution)/shard_map/widen_gradients/pallas_call | solution.py:1415
  408.1 0.0 copy-done.2
  408.1 0.1 slice_reduce_fusion
  408.2 0.7 sqrt.7
  408.9 0.0 copy-done
  408.9 0.8 copy.27
  409.7 0.0 copy-done.1
  409.7 0.8 copy.28
  (1 shorter events, 0.0 us)
Async XLA Ops:
  392.9 15.2 %copy-start.2 = (f32[8,128]{1,0:T(8,128)S(1)}, f32[8,128]{1,0:T(8,128)}, u32[]{:S(2)}) copy-start(f32[8,128]{1,0:T(8,128)} %get-tuple-element.98) | copy-start | bytes 12292
  392.9 16.0 %copy-start = (bf16[256,1024]{1,0:T(8,128)(2,1)S(1)}, bf16[256,1024]{1,0:T(8,128)(2,1)}, u32[]{:S(2)}) copy-start(bf16[256,1024]{1,0:T(8,128)(2,1)} %get-tuple-element.110) | copy-start | bytes 1572868
  392.9 16.8 %copy-start.1 = (bf16[256,1024]{1,0:T(8,128)(2,1)S(1)}, bf16[256,1024]{1,0:T(8,128)(2,1)}, u32[]{:S(2)}) copy-start(bf16[256,1024]{1,0:T(8,128)(2,1)} %get-tuple-element.111) | copy-start | bytes 1572868

commit v5 on v4

--- a/solution.py
+++ b/solution.py
@@ -1148,7 +1148,7 @@
     line = Line(cfg, place, r)
     stats = StatLine(place, r)
     loads = {}
-    base_down, base_left, base_right, base_out, base_gate, base_qkv, base_end = cfg.bases
+    base_down, base_left, base_right, base_out, base_gate, gate_end, base_qkv, _ = cfg.bases
     half = block // (2 * SUPER)
     part_rows = 2 * half
     own_start = place.me * block
@@ -1192,7 +1192,9 @@
     place.greet(True)
     stats.square()
     spread_segments(r, length)
-    r.grads[base_end : cfg.chunks * CHUNK, :] = jnp.zeros((cfg.chunks * CHUNK - base_end, width), BF16)
+    for start, stop in ((gate_end, base_qkv), (base_qkv + 3 * local, cfg.chunks * CHUNK)):
+        if stop > start:
+            r.grads[start:stop, :] = jnp.zeros((stop - start, width), BF16)
     stats.pair()
 
     def back_rows(total, values, grad):
@@ -1255,15 +1257,15 @@
         glu_grad_rows(base_down, r.hid, r.gd)
         if turn == 0:
             stats.stage(1)
-        line.pump(ready(base_left), 1)
+        line.pump(ready(base_left), 1 + turn)
         mid_sum.middle(0)
         glu_grad_rows(base_left, grad_left_ref, r.n2)
-        line.pump(ready(base_right), 1)
+        line.pump(ready(base_right), 1 + turn)
         for part in range(1, SUPER):
             mid_sum.middle(part)
         glu_grad_rows(base_right, grad_right_ref, r.n2)
         for part in range(SUPER):
-            line.pump(ready(base_out), 2 - part)
+            line.pump(ready(base_out), 2 if part == 0 else 1)
             for h in range(2):
                 mid_sum.finish(part, h)
                 for i in range(half // step_rows):
@@ -1295,7 +1297,7 @@
                 r.gate[rows, :] = grad_normed
                 row_sums(grad_normed * normed, r.inner, member * per_block + number)
 
-        gather_stage(second, out_back, lambda i: line.pump(ready(base_out), 2))
+        gather_stage(second, out_back, lambda i: line.pump(ready(base_out), 3 if i == SUPER else 2))
         share.start()
         line.release(turn, base_gate)
         r.grads[base_out : base_out + local, :] = tn(r.branch[...], r.ga[...]).astype(BF16)
@@ -1324,9 +1326,16 @@
         if turn + 1 < layers:
             load(layer - 1, *out_in)
         line.pump(ready(base_qkv), 1)
+        between = line.done
+        line.done += 1
+        assert line.done <= ready(base_qkv)
 
         @pl.loop(0, heads_here)
         def _(head):
+            @pl.when(head == 1)
+            def _():
+                line.tick(between + head - 1)
+
             wide = aligned(head * 2 * HDIM, 2 * HDIM)
             thin = aligned(head * HDIM, HDIM)
             for col_tile in range(tiles_here):
@@ -1540,7 +1549,8 @@
                 (target.at[layer, pl.ds(n * cfg.local, cfg.local), :], slice(n * cfg.local, (n + 1) * cfg.local))
                 for n in range(cfg.width // cfg.local)
             ]
-            tasks.append((layer, cfg.bases[4] + number * cfg.local, cfg.local, pieces))
+            start = cfg.bases[6] + (number - 1) * cfg.local if number > 0 else cfg.bases[4]
+            tasks.append((layer, start, cfg.local, pieces))
     depth = 3
 
     def fetch(task):
@@ -1617,10 +1627,12 @@
         wq=query_proj, wk=key_proj, wv=value_proj, wg=gate_proj, wo=output_proj,
         wl=jnp.swapaxes(left_proj, 1, 2), wr=jnp.swapaxes(right_proj, 1, 2), wd=down_proj,
     )
-    ends = np.cumsum([0, ff, ff, ff, local, local, 3 * local]).tolist()
+    ends = np.cumsum([0, ff, ff, ff, local, local]).tolist()
+    ends += [-(-ends[-1] // CHUNK) * CHUNK]
+    ends += [-(-(ends[-1] + 3 * local) // CHUNK) * CHUNK]
     common = dict(
         layers=layers, block=block, length=length, width=width, local=local, ff=ff, heads_here=heads_here,
-        pairs=lax.axis_size("dp") // 2, bases=ends, chunks=-(-ends[-1] // CHUNK),
+        pairs=lax.axis_size("dp") // 2, bases=ends, chunks=ends[-1] // CHUNK,
     )
     current, xs, saved = tokens, [], []
     for layer in range(layers):

time: 418 us -> 413 us (0.988)
  Pallas kernels: 407 us -> 402 us
    pallas_call x4, Pallas kernels: 407 us -> 402 us  [call_kernel(): pl.pallas_call(functools.partial(body, cfg, names), out_shape=[shape for...]
where the time goes in v5:
time: 413 us; the launch traced here: 405 us
  Pallas kernels  402 us (97%)
    pallas_call x4, Pallas kernels, call_kernel(): pl.pallas_call(functools.partial(body, cfg, names), out_shape=[shape for...  402 us

profile of v5, /device:TPU:0, one launch (start us, length us, event | category | flops | bytes accessed | tf_op | source)
XLA Modules:
  0.0 405.1 jit_solution(16059516073654816363)
XLA Ops:
  0.6 83.7 %layer_forward.2 = (f32[256,1024]{1,0:T(8,128)}, f32[8,128]{1,0:T(8,128)}, f32[8,128]{1,0:T(8,128)}, bf16[1024,1024]{1,0:T(8,128)(2,1)}, bf16[1024,256]{1,0:T(8,...) custom-call(bf16[256,1024]{1,0:T(8,128)(2,1)} %refs_14_.1, ...), custom_call_target="tpu_custom_call" | custom-call | tf_op jit(solution)/shard_map/layer_forward/pallas_call | solution.py:1424
  84.3 92.4 %layer_forward.3 = (bf16[256,1024]{1,0:T(8,128)(2,1)}, f32[8,128]{1,0:T(8,128)}, f32[8,128]{1,0:T(8,128)}, bf16[1024,1024]{1,0:T(8,128)(2,1)}, bf16[1024,256]{1,...) custom-call(f32[256,1024]{1,0:T(8,128)} %get-tuple-element.55.refs_0, ...), custom_call_target="tpu_custom_call" | custom-call | tf_op jit(solution)/shard_map/layer_forward/pallas_call | solution.py:1424
  176.8 210.6 %layers_backward.1 = (bf16[256,1024]{1,0:T(8,128)(2,1)}, f32[8,128]{1,0:T(8,128)}, bf16[6912,1024]{1,0:T(8,128)(2,1)}) custom-call(bf16[256,1024]{1,0:T(8,128)(2,1)} %refs_0_.3, bf16[1024,1024]{1,0:T(8,128)(2,1)} %get-tuple-element.57.refs_1_, f32[1024,128]{1,0:T(8,128)} %constant.11.clone.refs_1_.refs_2_, f32[1024,128]{1,0:T(8,128)} %constant.12.clone.refs_2_.refs_3_, ...), custom_call_target="tpu_custom_call" | custom-call | tf_op jit(solution)/shard_map/layers_backward/pallas_call | solution.py:1424
  387.3 0.0 copy-start.2
  387.3 0.0 copy-start
  387.3 0.0 copy-start.1
  387.3 15.2 %widen_gradients.1 = (f32[2,704,1024]{2,1,0:T(8,128)}, f32[2,704,1024]{2,1,0:T(8,128)}, f32[2,704,1024]{2,1,0:T(8,128)}, f32[2,256,1024]{2,1,0:T(8,128)}, f32[2,...) custom-call(bf16[6912,1024]{1,0:T(8,128)(2,1)} %get-tuple-element.89.refs_0_), custom_call_target="tpu_custom_call" | custom-call | tf_op jit(solution)/shard_map/widen_gradients/pallas_call | solution.py:1424
  402.5 0.0 copy-done.2
  402.5 0.1 slice_reduce_fusion
  402.7 0.7 sqrt.7
  403.3 0.0 copy-done
  403.3 0.8 copy.27
  404.1 0.0 copy-done.1
  404.1 0.8 copy.28
  (1 shorter events, 0.0 us)
Async XLA Ops:
  387.3 15.2 %copy-start.2 = (f32[8,128]{1,0:T(8,128)S(1)}, f32[8,128]{1,0:T(8,128)}, u32[]{:S(2)}) copy-start(f32[8,128]{1,0:T(8,128)} %get-tuple-element.98) | copy-start | bytes 12292
  387.3 16.0 %copy-start = (bf16[256,1024]{1,0:T(8,128)(2,1)S(1)}, bf16[256,1024]{1,0:T(8,128)(2,1)}, u32[]{:S(2)}) copy-start(bf16[256,1024]{1,0:T(8,128)(2,1)} %get-tuple-element.110) | copy-start | bytes 1572868
  387.3 16.8 %copy-start.1 = (bf16[256,1024]{1,0:T(8,128)(2,1)S(1)}, bf16[256,1024]{1,0:T(8,128)(2,1)}, u32[]{:S(2)}) copy-start(bf16[256,1024]{1,0:T(8,128)(2,1)} %get-tuple-element.111) | copy-start | bytes 1572868

commit v6 on v5

--- a/solution.py
+++ b/solution.py
@@ -452,7 +452,7 @@
 F32 = jnp.float32
 BF16 = jnp.bfloat16
 MESH = pl.DeviceIdType.MESH
-VMEM_LIMIT = 60 * 2**20
+VMEM_LIMIT = 62 * 2**20
 SUPER = 2
 CHUNK = 128
 HOP = 3
@@ -584,7 +584,7 @@
                 self.wire(part, number).wait_send()
 
 
-def gather_stage(gather, block_fn, beside):
+def gather_stage(gather, block_fn, beside, behind=None):
     @pl.loop(0, 4 * SUPER)
     def _(i):
         mixed = i - SUPER
@@ -596,6 +596,8 @@
             for one in range(SUPER):
                 beside(one)
                 gather.forward(one)
+            if behind is not None:
+                behind()
 
         @pl.when(i == 3 * SUPER)
         def _():
@@ -740,37 +742,30 @@
     return types.SimpleNamespace(**dict(zip(names, refs)))
 
 
-def fwd_kernel(cfg, names, *refs):
-    r = namespace(names, refs)
-    layer, block, length, width, local = cfg.layer, cfg.block, cfg.length, cfg.width, cfg.local
+def forward_front(cfg, r, place, copies, layer, x, save, third, back_block):
+    block, length, width = cfg.block, cfg.length, cfg.width
     heads_here, size = cfg.heads_here, cfg.block
-    place = Place(cfg.pairs)
     first_head = layer * HEADS + place.me * heads_here
-    copies = Local(r.local_sem)
     w_in = [copies.start(h.at[layer], v) for h, v in (
         (r.wq_h, r.wq), (r.wk_h, r.wk), (r.wv_h, r.wv), (r.wg_h, r.wg))]
     w_out = copies.start(r.wo_h.at[layer], r.wo)
     w_glu = [copies.start(h.at[layer], v) for h, v in ((r.wl_h, r.wl), (r.wr_h, r.wr), (r.wd_h, r.wd))]
-    saves = []
-    first = Gather(place, r.n1, r.ag1_send, r.ag1_recv, block)
-    mid_sum = Scatter(place, r.part1, r.land1, r.rs1_send, r.rs1_recv, block)
-    second = Gather(place, r.n2, r.ag2_send, r.ag2_recv, block)
-    out_sum = Scatter(place, r.part2, r.land2, r.rs2_send, r.rs2_recv, block)
-    share = Share(place, r.ss, r.ss_land, r.ss_send, r.ss_recv)
-    third = Gather(place, r.gd, r.ag3_send, r.ag3_recv, block) if cfg.last else None
-    if cfg.last:
-        load_up = copies.start(r.up_h, r.gd.at[aligned(place.me * block, block), :])
+    first = Gather(place, r.n1, r.fag1_send, r.fag1_recv, block)
+    mid_sum = Scatter(place, r.part1, r.land1, r.frs1_send, r.frs1_recv, block)
+    second = Gather(place, r.n2, r.fag2_send, r.fag2_recv, block)
+    out_sum = Scatter(place, r.part2, r.land2, r.frs2_send, r.frs2_recv, block)
+    share = Share(place, r.ss_mine, r.ss_land, r.ss_send, r.ss_recv)
     half, step_rows = first.half, 32
     own_start = place.me * block
 
     @pl.loop(0, block // step_rows)
     def _(i):
         rows = aligned(i * step_rows, step_rows)
-        v = r.x[rows, :].astype(F32)
+        v = x[rows, :].astype(F32)
         scale = lax.rsqrt(jnp.mean(v * v, axis=1, keepdims=True) + epsilon)
         r.n1[aligned(own_start + i * step_rows, step_rows), :] = (v * scale).astype(BF16)
 
-    place.greet(False)
+    place.greet(third is not None)
     for part in range(SUPER):
         first.start(part)
     decay_tiles(r.dec, first_head, r.tiles, heads_here, size)
@@ -803,11 +798,8 @@
         r.v[rows, :] = nn(a, r.wv[...]).astype(BF16)
         r.gate[rows, :] = nn(a, r.wg[...])
 
-    for v, h in ((r.n1, r.n1_h), (r.ql, r.ql_h), (r.kl, r.kl_h), (r.q, r.q_h), (r.k, r.k_h), (r.v, r.v_h), (r.gate, r.gate_h)):
-        saves.append(copies.start(v, h))
-
-    if cfg.last:
-        load_up.wait()
+    save("n1", "ql", "kl", "q", "k", "v", "gate")
+    if third is not None:
         for part in range(SUPER):
             third.start(part)
     tiles_here = length // size
@@ -827,14 +819,14 @@
                 term = nn(scores, r.v[cols, thin])
                 acc = term if acc is None else acc + term
             r.heads[rows, thin] = acc
-            r.u[rows, thin] = (acc * r.gate[rows, thin]).astype(BF16)
+            r.dh[rows, thin] = (acc * r.gate[rows, thin]).astype(BF16)
 
     for chunk in range(length // 128):
         v = r.heads[chunk * 128 : (chunk + 1) * 128, :]
-        row_sums(v * v, r.ss, chunk)
+        row_sums(v * v, r.ss_mine, chunk)
     share.start()
-    saves.append(copies.start(r.heads, r.heads_h))
-    if cfg.last:
+    save("heads")
+    if third is not None:
         for part in range(SUPER):
             third.forward(part)
     w_out.wait()
@@ -843,16 +835,16 @@
     for part in range(SUPER):
         for step in (3, 1, 2, 0):
             rows = aligned(place.member(step) * block + part * part_rows, part_rows)
-            r.part1[rows, :] = nn(r.u[rows, :], r.wo[...]).astype(BF16)
+            r.part1[rows, :] = nn(r.dh[rows, :], r.wo[...]).astype(BF16)
             mid_sum.send_block(part, step)
     for part in range(SUPER):
         mid_sum.middle(part)
-    r.sstot[...] = share.total()
-    saves.append(copies.start(r.sstot, r.ss_h))
-    scaling = lax.rsqrt(r.sstot[...] / width + epsilon)
+    r.ss[...] = share.total()
+    save("ss")
+    scaling = lax.rsqrt(r.ss[...] / width + epsilon)
     per_block = block // 128
     for chunk in range(per_block):
-        r.scale[chunk * 128 : (chunk + 1) * 128, :] = spread(scaling, place.me * per_block + chunk)
+        r.scale[aligned(own_start + chunk * 128, 128), :] = spread(scaling, place.me * per_block + chunk)
     r.stat_wide[...] = jnp.zeros_like(r.stat_wide)
 
     def add_stat(row, v):
@@ -865,59 +857,82 @@
             mid_sum.finish(part, h)
             for i in range(half // step_rows):
                 offset = (2 * part + h) * half + i * step_rows
-                scale = widen(r.scale[offset : offset + step_rows, :], width // 128)
+                scale = widen(r.scale[aligned(own_start + offset, step_rows), :], width // 128)
                 attn = mid_sum.total(part, h, i * step_rows, step_rows) * scale
-                middle = r.x[offset : offset + step_rows, :].astype(F32) + attn
+                middle = x[offset : offset + step_rows, :].astype(F32) + attn
                 r.mid[offset : offset + step_rows, :] = middle
                 add_stat(0, attn)
                 norm = lax.rsqrt(jnp.mean(middle * middle, axis=1, keepdims=True) + epsilon)
                 r.n2[aligned(own_start + offset, step_rows), :] = (middle * norm).astype(BF16)
         second.start(part)
-    saves.append(copies.start(r.mid, r.mid_h))
+    save("mid")
     for copy in w_glu:
         copy.wait()
+    if third is not None:
+        mid_sum.drain()
+        for part in range(SUPER):
+            for which in (1, 2, 3):
+                third.finish(part, which)
+
     def glu(part, step):
         rows = aligned(place.member(step) * block + part * part_rows, part_rows)
         a = r.n2[rows, :]
         left = nt(a, r.wl[...])
         right = nt(a, r.wr[...])
         hidden = (left * right).astype(BF16)
-        r.left[rows, :] = left.astype(BF16)
-        r.right[rows, :] = right.astype(BF16)
         r.hid[rows, :] = hidden
+        if back_block is not None:
+            back_block(rows, left, right, part, step)
+        else:
+            r.left[rows, :] = left.astype(BF16)
+            r.right[rows, :] = right.astype(BF16)
         r.part2[rows, :] = nn(hidden, r.wd[...]).astype(BF16)
-        for which in (1, 2, 3):
-            @pl.when(step == which)
-            def _():
-                out_sum.send_block(part, which)
+        if back_block is None:
+            for which in (1, 2, 3):
+                @pl.when(step == which)
+                def _():
+                    out_sum.send_block(part, which)
 
     gather_stage(second, glu, lambda i: None)
-    for v, h in ((r.n2, r.n2_h), (r.left, r.left_h), (r.right, r.right_h), (r.hid, r.hid_h)):
-        saves.append(copies.start(v, h))
+
+    def finish():
+        for part in range(SUPER):
+            for h in range(2):
+                out_sum.finish(part, h)
+                for i in range(half // step_rows):
+                    offset = (2 * part + h) * half + i * step_rows
+                    glu_rows = out_sum.total(part, h, i * step_rows, step_rows)
+                    after = r.mid[offset : offset + step_rows, :] + glu_rows
+                    r.xo[offset : offset + step_rows, :] = after.astype(r.xo.dtype)
+                    add_stat(1, glu_rows)
+                    add_stat(2, after)
+        folded = r.stat_wide[:, :128]
+        for n in range(1, width // 128):
+            folded = folded + r.stat_wide[:, n * 128 : (n + 1) * 128]
+        return folded
+
+    groups = [first, second, share] + ([third] if third is not None else [mid_sum])
+    return out_sum, finish, groups
+
+
+def fwd_kernel(cfg, names, *refs):
+    r = namespace(names, refs)
+    place = Place(cfg.pairs)
+    copies = Local(r.local_sem)
+    saves = []
+
+    def save(*keys):
+        for key in keys:
+            saves.append(copies.start(getattr(r, key), getattr(r, key + "_h")))
+
+    out_sum, finish, groups = forward_front(cfg, r, place, copies, cfg.layer, r.x, save, None, None)
+    save("n2", "left", "right", "hid")
     for part in range(SUPER):
         out_sum.middle(part)
-    if cfg.last:
-        for part in range(SUPER):
-            for which in (1, 2, 3):
-                third.finish(part, which)
-        saves.append(copies.start(r.gd, r.gd_h))
-    for part in range(SUPER):
-        for h in range(2):
-            out_sum.finish(part, h)
-            for i in range(half // step_rows):
-                offset = (2 * part + h) * half + i * step_rows
-                glu_rows = out_sum.total(part, h, i * step_rows, step_rows)
-                after = r.mid[offset : offset + step_rows, :] + glu_rows
-                r.xo[offset : offset + step_rows, :] = after.astype(r.xo.dtype)
-                add_stat(1, glu_rows)
-                add_stat(2, after)
-    folded = r.stat_wide[:, :128]
-    for n in range(1, width // 128):
-        folded = folded + r.stat_wide[:, n * 128 : (n + 1) * 128]
-    r.stat[...] = folded
+    r.stat[...] = finish()
     for copy in saves:
         copy.wait()
-    for group in (first, mid_sum, second, out_sum, share) + ((third,) if cfg.last else ()):
+    for group in (*groups, out_sum):
         group.drain()
 
 
@@ -1168,13 +1183,11 @@
         for key in keys:
             loads[key].wait()
 
-    loads["gd"] = copies.start(r.gd_h, r.gd)
     glu_in = ("wd", "left", "right", "wl", "wr")
-    glu_grad = ("hid", "n2", "mid")
+    glu_grad = ("hid", "n2")
     out_in = ("ss", "wo", "gate", "heads")
     attn_in = ("q", "k", "v", "ql", "kl")
     in_in = ("wq", "wk", "wv", "wg")
-    load(layers - 1, *glu_in, *glu_grad, *out_in, *attn_in, *in_in, "n1")
 
     def gather_one(layer):
         return Gather(place, r.gd, r.ag1_send.at[layer], r.ag1_recv.at[layer], block)
@@ -1186,16 +1199,32 @@
         rows = aligned(i * 32, 32)
         r.g[rows, :] = r.up[rows, :].astype(F32)
 
-    r.stat_mine[...] = jnp.zeros_like(r.stat_mine)
-    for layer in range(layers):
-        r.stat_mine[3 * layer : 3 * layer + 3, :] = getattr(r, "stat%d" % layer)[0:3, :]
-    place.greet(True)
-    stats.square()
-    spread_segments(r, length)
+        r.gd[aligned(own_start + i * 32, 32), :] = r.up[rows, :]
+
     for start, stop in ((gate_end, base_qkv), (base_qkv + 3 * local, cfg.chunks * CHUNK)):
         if stop > start:
             r.grads[start:stop, :] = jnp.zeros((stop - start, width), BF16)
-    stats.pair()
+    top = layers - 1
+    third = Gather(place, r.gd, r.ag3_send, r.ag3_recv, block)
+    top_sum = Scatter(place, r.part1, r.land1, r.rs1_send.at[top], r.rs1_recv.at[top], block)
+
+    def back_block(rows, left, right, part, step):
+        grad_hidden = nt(r.gd[rows, :], r.wd[...])
+        grad_left = (grad_hidden * right).astype(BF16)
+        grad_right = (grad_hidden * left).astype(BF16)
+        r.right[rows, :] = grad_left
+        r.left[rows, :] = grad_right
+        r.part1[rows, :] = (nn(grad_left, r.wl[...]) + nn(grad_right, r.wr[...])).astype(BF16)
+        for which in (1, 2, 3):
+            @pl.when(step == which)
+            def _():
+                top_sum.send_block(part, which)
+
+    out_sum, finish_forward, groups = forward_front(
+        cfg, r, place, copies, top, getattr(r, "x%d" % top), lambda *keys: None, third, back_block
+    )
+    for group in groups:
+        group.drain()
 
     def back_rows(total, values, grad):
         norm = lax.rsqrt(jnp.mean(values * values, axis=1, keepdims=True) + epsilon)
@@ -1205,24 +1234,22 @@
 
     for turn, layer in enumerate(reversed(range(layers))):
         first = firsts[layer]
-        mid_sum = Scatter(place, r.part, r.land, r.rs1_send.at[layer], r.rs1_recv.at[layer], block)
+        mid_sum = top_sum if turn == 0 else Scatter(place, r.part1, r.land1, r.rs1_send.at[layer], r.rs1_recv.at[layer], block)
         second = Gather(place, r.ga, r.ag2_send.at[layer], r.ag2_recv.at[layer], block)
-        in_sum = Scatter(place, r.part, r.land, r.rs2_send.at[layer], r.rs2_recv.at[layer], block)
+        in_sum = Scatter(place, r.part1, r.land1, r.rs2_send.at[layer], r.rs2_recv.at[layer], block)
         share = Share(place, r.inner, r.inner_land.at[layer], r.in_send.at[layer], r.in_recv.at[layer])
         first_head = layer * HEADS + place.me * heads_here
 
         def ready(rows):
             return turn * cfg.chunks + rows // CHUNK
 
-        decay_tiles(r.dec, first_head, r.tiles, heads_here, size)
-        await_loads(*glu_in)
-        await_loads(*out_in)
+        if turn > 0:
+            decay_tiles(r.dec, first_head, r.tiles, heads_here, size)
+            await_loads(*glu_in)
+            await_loads(*out_in)
         scaling = lax.rsqrt(r.ss[...] / width + epsilon)
         for chunk in range(length // 128):
             r.scale[chunk * 128 : (chunk + 1) * 128, :] = spread(scaling, chunk)
-        if turn == 0:
-            stats.stage(0)
-
         def glu_back(part, step):
             rows = aligned(place.member(step) * block + part * part_rows, part_rows)
             grad_hidden = nt(r.gd[rows, :], r.wd[...])
@@ -1230,19 +1257,13 @@
             grad_right = (grad_hidden * r.left[rows, :].astype(F32)).astype(BF16)
             r.right[rows, :] = grad_left
             r.left[rows, :] = grad_right
-            r.part[rows, :] = (nn(grad_left, r.wl[...]) + nn(grad_right, r.wr[...])).astype(BF16)
+            r.part1[rows, :] = (nn(grad_left, r.wl[...]) + nn(grad_right, r.wr[...])).astype(BF16)
             for which in (1, 2, 3):
                 @pl.when(step == which)
                 def _():
                     mid_sum.send_block(part, which)
 
-        if turn == 0:
-            await_loads("gd")
-            for part in range(SUPER):
-                @pl.loop(0, 4)
-                def _(i):
-                    glu_back(part, 3 - i)
-        else:
+        if turn > 0:
             gather_stage(first, glu_back, lambda i: line.pump(ready(0), 2))
             first.drain()
         grad_left_ref, grad_right_ref = r.right, r.left
@@ -1253,10 +1274,18 @@
                 cols = slice(n * 256, (n + 1) * 256)
                 r.grads[base : base + ff, cols] = tn(a_ref[...], b_ref[:, cols]).astype(BF16)
 
-        await_loads(*glu_grad)
+        if turn > 0:
+            await_loads(*glu_grad)
         glu_grad_rows(base_down, r.hid, r.gd)
-        if turn == 0:
-            stats.stage(1)
+        if turn == 1:
+            folded = finish_forward()
+            r.stat_mine[...] = jnp.zeros_like(r.stat_mine)
+            for one in range(top):
+                r.stat_mine[3 * one : 3 * one + 3, :] = getattr(r, "stat%d" % one)[0:3, :]
+            r.stat_mine[3 * top : 3 * top + 3, :] = folded[0:3, :]
+            stats.square()
+        if turn > 0:
+            load(layer, "mid")
         line.pump(ready(base_left), 1 + turn)
         mid_sum.middle(0)
         glu_grad_rows(base_left, grad_left_ref, r.n2)
@@ -1264,6 +1293,10 @@
         for part in range(1, SUPER):
             mid_sum.middle(part)
         glu_grad_rows(base_right, grad_right_ref, r.n2)
+        if turn == 1:
+            stats.pair()
+        if turn > 0:
+            await_loads("mid")
         for part in range(SUPER):
             line.pump(ready(base_out), 2 if part == 0 else 1)
             for h in range(2):
@@ -1277,12 +1310,14 @@
                     r.ga[aligned(own_start + offset, step_rows), :] = new.astype(BF16)
             second.start(part)
         mid_sum.drain()
-        if turn == 0:
-            stats.stage(2)
         if turn + 1 < layers:
             load(layer - 1, *glu_in, *glu_grad)
-        if turn == 0:
-            stats.stage(3)
+
+        def send_out():
+            for part in range(SUPER):
+                for which in (1, 2, 3):
+                    out_sum.send_block(part, which)
+
         def out_back(part, step):
             member = place.member(step)
             for chunk in range(part_rows // 128):
@@ -1297,7 +1332,8 @@
                 r.gate[rows, :] = grad_normed
                 row_sums(grad_normed * normed, r.inner, member * per_block + number)
 
-        gather_stage(second, out_back, lambda i: line.pump(ready(base_out), 3 if i == SUPER else 2))
+        gather_stage(second, out_back, lambda i: line.pump(ready(base_out), 3 if i == SUPER else 2),
+                     send_out if turn == 0 else None)
         share.start()
         line.release(turn, base_gate)
         r.grads[base_out : base_out + local, :] = tn(r.branch[...], r.ga[...]).astype(BF16)
@@ -1310,10 +1346,14 @@
                 part_grad = tn(r.n1[:, n * local : (n + 1) * local], r.dx[:, cols])
                 r.grads[base : base + local, n * local : (n + 1) * local] = part_grad.astype(BF16)
 
-        await_loads("n1")
+        if turn > 0:
+            await_loads("n1")
+        if turn == 1:
+            stats.stage(0)
         in_grad_rows(3, base_gate)
         line.pump(ready(base_qkv), 1)
-        await_loads(*attn_in)
+        if turn > 0:
+            await_loads(*attn_in)
         r.intot[...] = share.total() / width
         for chunk in range(length // 128):
             rows = slice(chunk * 128, (chunk + 1) * 128)
@@ -1373,7 +1413,10 @@
 
         if turn + 1 < layers:
             load(layer - 1, *attn_in)
-        await_loads(*in_in)
+        if turn > 0:
+            await_loads(*in_in)
+        if turn == 1:
+            stats.stage(1)
         last = turn == layers - 1
         if last:
             for number in range(3):
@@ -1385,7 +1428,7 @@
                 for n, w in enumerate((r.wq, r.wk, r.wv, r.wg)):
                     term = nt(r.dx[rows, n * local : (n + 1) * local], w[...])
                     total = term if total is None else total + term
-                r.part[rows, :] = total.astype(BF16)
+                r.part1[rows, :] = total.astype(BF16)
                 in_sum.send_block(part, step)
             line.pump(ready(cfg.chunks * CHUNK if last else base_qkv), 2 if last else 1)
         for number in range(3):
@@ -1394,6 +1437,11 @@
             line.pump(ready(base_qkv + (number + 1) * local), 2 if last else 1)
             if number < SUPER:
                 in_sum.middle(number)
+        if turn == 0:
+            for part in range(SUPER):
+                out_sum.middle(part)
+        if turn == 1:
+            stats.stage(2)
         if turn + 1 < layers:
             load(layer - 1, *in_in, "n1")
         for part in range(SUPER):
@@ -1414,6 +1462,9 @@
             if layer > 0:
                 firsts[layer - 1].start(part)
         in_sum.drain()
+    out_sum.drain()
+    for number in range(3, cfg.pairs):
+        stats.stage(number)
     stats.finish()
     line.finish()
 
@@ -1440,8 +1491,9 @@
     half = cfg.block // (2 * SUPER)
     out = {}
     for name in ("ag1", "ag2", "rs1", "rs2"):
-        out[name + "_send"] = dma((*lead, SUPER, 6))
-        out[name + "_recv"] = dma((*lead, SUPER, 6))
+        out["f" + name + "_send"] = out["f" + name + "_recv"] = dma((SUPER, 6))
+        if lead:
+            out[name + "_send"] = out[name + "_recv"] = dma((*lead, SUPER, 6))
     for name in copies:
         out["land" + name] = pltpu.VMEM((SUPER, 6, half, cfg.width), BF16)
         out["part" + name] = pltpu.VMEM((cfg.length, cfg.width), BF16)
@@ -1467,30 +1519,28 @@
     )
 
 
-def run_forward(cfg, x, upstream, tables, weights):
-    v, dma, s = pltpu.VMEM, pltpu.SemaphoreType.DMA, jax.ShapeDtypeStruct
+def forward_scratch(cfg):
+    v, dma = pltpu.VMEM, pltpu.SemaphoreType.DMA
     rows, wide, local, ff, block = cfg.length, cfg.width, cfg.local, cfg.ff, cfg.block
+    return dict(
+        n1=v((rows, wide), BF16), ql=v((rows, local), BF16), kl=v((rows, local), BF16), q=v((rows, 2 * local), BF16),
+        k=v((rows, 2 * local), BF16), v=v((rows, local), BF16), gate=v((rows, local), F32), heads=v((rows, local), F32),
+        mid=v((block, wide), F32), n2=v((rows, wide), BF16), left=v((rows, ff), BF16), right=v((rows, ff), BF16),
+        hid=v((rows, ff), BF16), ss=v((8, 128), F32), ss_mine=v((8, 128), F32), dh=v((rows, local), BF16),
+        stat_wide=v((8, wide), F32), scale=v((rows, 128), F32), ss_land=v((3, 8, 128), F32), ss_send=dma((3,)), ss_recv=dma((3,)),
+    )
+
+
+def run_forward(cfg, x, tables, weights):
+    s = jax.ShapeDtypeStruct
     inputs = dict(x=(x, True), **{k: (a, True) for k, a in tables.items()}, **{k + "_h": (a, False) for k, a in weights.items()})
-    kept = dict(
-        n1=((rows, wide), BF16), ql=((rows, local), BF16), kl=((rows, local), BF16),
-        q=((rows, 2 * local), BF16), k=((rows, 2 * local), BF16), v=((rows, local), BF16),
-        gate=((rows, local), F32), heads=((rows, local), F32), mid=((block, wide), F32),
-        n2=((rows, wide), BF16), left=((rows, ff), BF16), right=((rows, ff), BF16), hid=((rows, ff), BF16),
+    scratch = dict(
+        **weight_scratch(cfg), **collective_scratch(cfg, ("1", "2"), ()), **table_scratch(cfg), **forward_scratch(cfg),
     )
     outputs = dict(
-        xo=(s((block, wide), BF16 if cfg.last else F32), True), stat=(s((8, 128), F32), True), ss_h=(s((8, 128), F32), False),
-        **{k + "_h": (s(*a), False) for k, a in kept.items()},
-    )
-    scratch = dict(
-        **weight_scratch(cfg), **collective_scratch(cfg, ("1", "2"), ()), **table_scratch(cfg),
-        **{k: v(*a) for k, a in kept.items()}, u=v((rows, local), BF16), stat_wide=v((8, wide), F32),
-        ss=v((8, 128), F32), sstot=v((8, 128), F32), scale=v((block, 128), F32),
-        ss_land=v((3, 8, 128), F32), ss_send=dma((3,)), ss_recv=dma((3,)),
-    )
-    if cfg.last:
-        inputs.update(up_h=(upstream, False))
-        outputs.update(gd_h=(s((rows, wide), BF16), False))
-        scratch.update(gd=v((rows, wide), BF16), ag3_send=dma((SUPER, 6)), ag3_recv=dma((SUPER, 6)))
+        xo=(s((cfg.block, cfg.width), F32), True), stat=(s((8, 128), F32), True),
+        **{k + "_h": (s(scratch[k].shape, scratch[k].dtype), False) for k in SAVED},
+    )
     return call_kernel(fwd_kernel, cfg, inputs, outputs, scratch, cfg.layer, "layer_forward")
 
 
@@ -1500,30 +1550,28 @@
 def run_backward(cfg, upstream, xs, saved, tables, weights):
     v, dma, s = pltpu.VMEM, pltpu.SemaphoreType.DMA, jax.ShapeDtypeStruct
     rows, wide, local, ff, block = cfg.length, cfg.width, cfg.local, cfg.ff, cfg.block
-    inputs = dict(up=(upstream, True), gd_h=(saved[-1]["gd_h"], False), **{k: (a, True) for k, a in tables.items()}, **{k + "_h": (a, False) for k, a in weights.items()})
+    inputs = dict(up=(upstream, True), **{k: (a, True) for k, a in tables.items()}, **{k + "_h": (a, False) for k, a in weights.items()})
     for layer in range(cfg.layers):
         inputs["x%d" % layer] = (xs[layer], True)
+    for layer in range(cfg.layers - 1):
         inputs["stat%d" % layer] = (saved[layer]["stat"], True)
         for key in SAVED:
             inputs["%s%d_h" % (key, layer)] = (saved[layer][key + "_h"], False)
     total_rows = cfg.chunks * CHUNK
     outputs = dict(
-        go=(s((block, wide), BF16), True), stat_total=(s((8, 128), F32), True),
+        xo=(s((block, wide), BF16), True), go=(s((block, wide), BF16), True), stat_total=(s((8, 128), F32), True),
         out_h=(s((cfg.layers * total_rows, wide), BF16), False),
     )
     small, ring, ring_sem = v((8, 128), F32), v((SLOTS, CHUNK // 2, wide), BF16), dma((SLOTS,))
     scratch = dict(
-        **weight_scratch(cfg), **collective_scratch(cfg, ("",), (cfg.layers,)), **table_scratch(cfg),
-        n1=v((rows, wide), BF16), ql=v((rows, local), BF16), kl=v((rows, local), BF16),
-        q=v((rows, 2 * local), BF16), k=v((rows, 2 * local), BF16), v=v((rows, local), BF16),
-        gate=v((rows, local), F32), heads=v((rows, local), F32), n2=v((rows, wide), BF16),
-        left=v((rows, ff), BF16), right=v((rows, ff), BF16), hid=v((rows, ff), BF16),
+        **weight_scratch(cfg), **collective_scratch(cfg, ("1", "2"), (cfg.layers,)), **table_scratch(cfg), **forward_scratch(cfg),
+        ag3_send=dma((SUPER, 6)), ag3_recv=dma((SUPER, 6)),
         gd=v((rows, wide), BF16), ga=v((rows, wide), BF16),
-        g=v((block, wide), F32), gm=v((block, wide), F32), mid=v((block, wide), F32),
-        dh=v((rows, local), BF16), branch=v((rows, local), BF16), dx=v((rows, 4 * local), BF16),
+        g=v((block, wide), F32), gm=v((block, wide), F32),
+        branch=v((rows, local), BF16), dx=v((rows, 4 * local), BF16),
         dq=v((rows, 2 * HDIM), F32), dk=v((rows, 2 * HDIM), F32),
-        grads=v((total_rows, wide), BF16), scale=v((rows, 128), F32),
-        ss=small, inner=small, intot=small,
+        grads=v((total_rows, wide), BF16),
+        inner=small, intot=small,
         inner_land=v((cfg.layers, 3, 8, 128), F32), in_send=dma((cfg.layers, 3)), in_recv=dma((cfg.layers, 3)),
         pair_land=ring, right_land=ring, left_land=ring,
         pair_send=ring_sem, pair_recv=ring_sem, right_send=ring_sem, right_recv=ring_sem, left_send=ring_sem,
@@ -1634,18 +1682,17 @@
         layers=layers, block=block, length=length, width=width, local=local, ff=ff, heads_here=heads_here,
         pairs=lax.axis_size("dp") // 2, bases=ends, chunks=ends[-1] // CHUNK,
     )
-    current, xs, saved = tokens, [], []
-    for layer in range(layers):
+    current, xs, saved = tokens, [tokens], []
+    for layer in range(layers - 1):
+        saved.append(run_forward(types.SimpleNamespace(layer=layer, **common), current, tables, weights))
+        current = saved[-1]["xo"]
         xs.append(current)
-        cfg = types.SimpleNamespace(layer=layer, last=layer == layers - 1, **common)
-        saved.append(run_forward(cfg, current, upstream, tables, weights))
-        current = saved[-1]["xo"]
     back = run_backward(types.SimpleNamespace(**common), upstream, xs, saved, tables, weights)
     stats = jnp.sum(back["stat_total"][: 3 * layers], axis=1).reshape(layers, 3)
     rms_stats = jnp.sqrt(stats / (length * lax.axis_size("dp") * width))
     wide = run_widen(types.SimpleNamespace(**common), back["out_h"])
     return (
-        current, back["go"], wide["query"], wide["key"], wide["value"], wide["gate"], wide["out"],
+        back["xo"], back["go"], wide["query"], wide["key"], wide["value"], wide["gate"], wide["out"],
         jnp.swapaxes(wide["left"], 1, 2), jnp.swapaxes(wide["right"], 1, 2), wide["down"], rms_stats,
     )
 

time: 413 us -> 396 us (0.959)
  Pallas kernels: 402 us -> 386 us
    pallas_call x4 -> x3, Pallas kernels: 402 us -> 386 us  [call_kernel(): pl.pallas_call(functools.partial(body, cfg, names), out_shape=[shape for...]
where the time goes in v6:
time: 396 us; the launch traced here: 390 us
  Pallas kernels  386 us (97%)
    pallas_call x3, Pallas kernels, call_kernel(): pl.pallas_call(functools.partial(body, cfg, names), out_shape=[shape for...  386 us

profile of v6, /device:TPU:0, one launch (start us, length us, event | category | flops | bytes accessed | tf_op | source)
XLA Modules:
  0.0 390.0 jit_solution(6243384808552808929)
XLA Ops:
  0.6 83.7 %layer_forward.1 = (f32[256,1024]{1,0:T(8,128)}, f32[8,128]{1,0:T(8,128)}, f32[8,128]{1,0:T(8,128)}, f32[256,1024]{1,0:T(8,128)}, bf16[1024,1024]{1,0:T(8,128)(2...) custom-call(bf16[256,1024]{1,0:T(8,128)(2,1)} %refs_13_.1, ...), custom_call_target="tpu_custom_call" | custom-call | tf_op jit(solution)/shard_map/layer_forward/pallas_call | solution.py:1475
  84.4 287.0 %layers_backward.1 = (bf16[256,1024]{1,0:T(8,128)(2,1)}, bf16[256,1024]{1,0:T(8,128)(2,1)}, f32[8,128]{1,0:T(8,128)}, bf16[6912,1024]{1,0:T(8,128)(2,1)}) custom-call(bf16[256,1024]{1,0:T(8,128)(2,1)} %refs_0_.3, f32[1024,128]{1,0:T(8,128)} %constant.11.clone.refs_1_, f32[1024,128]{1,0:T(8,128)} %constant.12.clone.refs_2_, ...), custom_call_target="tpu_custom_call" | custom-call | tf_op jit(solution)/shard_map/layers_backward/pallas_call | solution.py:1475
  371.4 0.8 slice_reduce_fusion
  372.2 0.7 sqrt.7
  372.8 0.0 copy-start.1
  372.8 0.0 copy-start
  372.8 15.2 %widen_gradients.1 = (f32[2,704,1024]{2,1,0:T(8,128)}, f32[2,704,1024]{2,1,0:T(8,128)}, f32[2,704,1024]{2,1,0:T(8,128)}, f32[2,256,1024]{2,1,0:T(8,128)}, f32[2,...) custom-call(bf16[6912,1024]{1,0:T(8,128)(2,1)} %get-tuple-element.57.refs_0_), custom_call_target="tpu_custom_call" | custom-call | tf_op jit(solution)/shard_map/widen_gradients/pallas_call | solution.py:1475
  388.0 0.0 copy-done.1
  388.0 0.8 copy.27
  388.8 0.0 copy-done
  388.8 0.8 copy.28
  (1 shorter events, 0.0 us)
Async XLA Ops:
  372.8 15.2 %copy-start.1 = (bf16[256,1024]{1,0:T(8,128)(2,1)S(1)}, bf16[256,1024]{1,0:T(8,128)(2,1)}, u32[]{:S(2)}) copy-start(bf16[256,1024]{1,0:T(8,128)(2,1)} %get-tuple-element.78) | copy-start | bytes 1572868
  372.8 16.0 %copy-start = (bf16[256,1024]{1,0:T(8,128)(2,1)S(1)}, bf16[256,1024]{1,0:T(8,128)(2,1)}, u32[]{:S(2)}) copy-start(bf16[256,1024]{1,0:T(8,128)(2,1)} %get-tuple-element.79) | copy-start | bytes 1572868

commit v7 on v6

--- a/solution.py
+++ b/solution.py
@@ -454,6 +454,7 @@
 MESH = pl.DeviceIdType.MESH
 VMEM_LIMIT = 62 * 2**20
 SUPER = 2
+EARLY = (0,)
 CHUNK = 128
 HOP = 3
 SLOTS = 16
@@ -578,13 +579,13 @@
         for number in {0: (), 1: (2,), 2: (3,), 3: (4, 5)}[step]:
             self.wire(part, number).wait_recv()
 
-    def drain(self):
-        for part in range(SUPER):
+    def drain(self, parts=range(SUPER)):
+        for part in parts:
             for number in range(6):
                 self.wire(part, number).wait_send()
 
 
-def gather_stage(gather, block_fn, beside, behind=None):
+def gather_stage(gather, block_fn, beside):
     @pl.loop(0, 4 * SUPER)
     def _(i):
         mixed = i - SUPER
@@ -596,8 +597,6 @@
             for one in range(SUPER):
                 beside(one)
                 gather.forward(one)
-            if behind is not None:
-                behind()
 
         @pl.when(i == 3 * SUPER)
         def _():
@@ -742,7 +741,7 @@
     return types.SimpleNamespace(**dict(zip(names, refs)))
 
 
-def forward_front(cfg, r, place, copies, layer, x, save, third, back_block):
+def forward_front(cfg, r, place, copies, layer, x, save, third, third_parts, back_block):
     block, length, width = cfg.block, cfg.length, cfg.width
     heads_here, size = cfg.heads_here, cfg.block
     first_head = layer * HEADS + place.me * heads_here
@@ -765,7 +764,7 @@
         scale = lax.rsqrt(jnp.mean(v * v, axis=1, keepdims=True) + epsilon)
         r.n1[aligned(own_start + i * step_rows, step_rows), :] = (v * scale).astype(BF16)
 
-    place.greet(third is not None)
+    place.greet(back_block is not None)
     for part in range(SUPER):
         first.start(part)
     decay_tiles(r.dec, first_head, r.tiles, heads_here, size)
@@ -800,7 +799,7 @@
 
     save("n1", "ql", "kl", "q", "k", "v", "gate")
     if third is not None:
-        for part in range(SUPER):
+        for part in third_parts:
             third.start(part)
     tiles_here = length // size
 
@@ -827,7 +826,7 @@
     share.start()
     save("heads")
     if third is not None:
-        for part in range(SUPER):
+        for part in third_parts:
             third.forward(part)
     w_out.wait()
 
@@ -869,10 +868,11 @@
     for copy in w_glu:
         copy.wait()
     if third is not None:
-        mid_sum.drain()
-        for part in range(SUPER):
+        for part in third_parts:
             for which in (1, 2, 3):
                 third.finish(part, which)
+    if back_block is not None:
+        mid_sum.drain()
 
     def glu(part, step):
         rows = aligned(place.member(step) * block + part * part_rows, part_rows)
@@ -911,8 +911,13 @@
             folded = folded + r.stat_wide[:, n * 128 : (n + 1) * 128]
         return folded
 
-    groups = [first, second, share] + ([third] if third is not None else [mid_sum])
+    groups = [first, second, share] + ([mid_sum] if back_block is None else [])
     return out_sum, finish, groups
+
+
+def early_rows(cfg):
+    part_rows = cfg.block // SUPER
+    return [pl.ds(start + part * part_rows, part_rows) for start in range(0, cfg.length, cfg.block) for part in EARLY]
 
 
 def fwd_kernel(cfg, names, *refs):
@@ -925,8 +930,17 @@
         for key in keys:
             saves.append(copies.start(getattr(r, key), getattr(r, key + "_h")))
 
-    out_sum, finish, groups = forward_front(cfg, r, place, copies, cfg.layer, r.x, save, None, None)
+    third = None
+    if cfg.gathers:
+        third = Gather(place, r.gd, r.ag3_send, r.ag3_recv, cfg.block)
+        part_rows = cfg.block // SUPER
+        for part in EARLY:
+            r.gd[aligned(place.me * cfg.block + part * part_rows, part_rows), :] = r.up[part * part_rows : (part + 1) * part_rows, :]
+    out_sum, finish, groups = forward_front(cfg, r, place, copies, cfg.layer, r.x, save, third, EARLY, None)
     save("n2", "left", "right", "hid")
+    if cfg.gathers:
+        for rows in early_rows(cfg):
+            saves.append(copies.start(r.gd.at[rows, :], r.gd_h.at[rows, :]))
     for part in range(SUPER):
         out_sum.middle(part)
     r.stat[...] = finish()
@@ -934,6 +948,8 @@
         copy.wait()
     for group in (*groups, out_sum):
         group.drain()
+    if cfg.gathers:
+        third.drain(EARLY)
 
 
 def turns_of(k, size, count):
@@ -1088,12 +1104,8 @@
             self.pump(turn * self.per, needed - self.done)
             assert self.done >= needed
 
-    def finish(self):
-        start, self.done = self.done, self.ticks
-
-        @pl.loop(start, self.ticks)
-        def _(n):
-            self.tick(n)
+    def more(self, most):
+        self.pump(self.ticks, most)
 
 
 class StatLine:
@@ -1199,8 +1211,11 @@
         rows = aligned(i * 32, 32)
         r.g[rows, :] = r.up[rows, :].astype(F32)
 
-        r.gd[aligned(own_start + i * 32, 32), :] = r.up[rows, :]
-
+
+    for part in range(SUPER):
+        if part not in EARLY:
+            r.gd[aligned(own_start + part * part_rows, part_rows), :] = r.up[part * part_rows : (part + 1) * part_rows, :]
+    early = [copies.start(r.gd_h.at[rows, :], r.gd.at[rows, :]) for rows in early_rows(cfg)]
     for start, stop in ((gate_end, base_qkv), (base_qkv + 3 * local, cfg.chunks * CHUNK)):
         if stop > start:
             r.grads[start:stop, :] = jnp.zeros((stop - start, width), BF16)
@@ -1220,11 +1235,18 @@
             def _():
                 top_sum.send_block(part, which)
 
+    def no_save(*keys):
+        if "mid" in keys:
+            for copy in early:
+                copy.wait()
+
+    late = [part for part in range(SUPER) if part not in EARLY]
     out_sum, finish_forward, groups = forward_front(
-        cfg, r, place, copies, top, getattr(r, "x%d" % top), lambda *keys: None, third, back_block
+        cfg, r, place, copies, top, getattr(r, "x%d" % top), no_save, third, late, back_block
     )
     for group in groups:
         group.drain()
+    third.drain(late)
 
     def back_rows(total, values, grad):
         norm = lax.rsqrt(jnp.mean(values * values, axis=1, keepdims=True) + epsilon)
@@ -1276,16 +1298,9 @@
 
         if turn > 0:
             await_loads(*glu_grad)
+            for copy in mid_pieces:
+                copy.wait()
         glu_grad_rows(base_down, r.hid, r.gd)
-        if turn == 1:
-            folded = finish_forward()
-            r.stat_mine[...] = jnp.zeros_like(r.stat_mine)
-            for one in range(top):
-                r.stat_mine[3 * one : 3 * one + 3, :] = getattr(r, "stat%d" % one)[0:3, :]
-            r.stat_mine[3 * top : 3 * top + 3, :] = folded[0:3, :]
-            stats.square()
-        if turn > 0:
-            load(layer, "mid")
         line.pump(ready(base_left), 1 + turn)
         mid_sum.middle(0)
         glu_grad_rows(base_left, grad_left_ref, r.n2)
@@ -1293,10 +1308,6 @@
         for part in range(1, SUPER):
             mid_sum.middle(part)
         glu_grad_rows(base_right, grad_right_ref, r.n2)
-        if turn == 1:
-            stats.pair()
-        if turn > 0:
-            await_loads("mid")
         for part in range(SUPER):
             line.pump(ready(base_out), 2 if part == 0 else 1)
             for h in range(2):
@@ -1305,18 +1316,18 @@
                     offset = (2 * part + h) * half + i * step_rows
                     rows = slice(offset, offset + step_rows)
                     total = mid_sum.total(part, h, i * step_rows, step_rows)
-                    new = back_rows(total, r.mid[rows, :], r.g[rows, :])
+                    if turn == 0:
+                        values = r.mid[rows, :]
+                    else:
+                        pieces = range(width // (2 * HDIM))
+                        values = jnp.concatenate([r.dq[n * block + offset : n * block + offset + step_rows, :] for n in pieces], axis=1)
+                    new = back_rows(total, values, r.g[rows, :])
                     r.gm[rows, :] = new
                     r.ga[aligned(own_start + offset, step_rows), :] = new.astype(BF16)
             second.start(part)
         mid_sum.drain()
         if turn + 1 < layers:
             load(layer - 1, *glu_in, *glu_grad)
-
-        def send_out():
-            for part in range(SUPER):
-                for which in (1, 2, 3):
-                    out_sum.send_block(part, which)
 
         def out_back(part, step):
             member = place.member(step)
@@ -1332,8 +1343,7 @@
                 r.gate[rows, :] = grad_normed
                 row_sums(grad_normed * normed, r.inner, member * per_block + number)
 
-        gather_stage(second, out_back, lambda i: line.pump(ready(base_out), 3 if i == SUPER else 2),
-                     send_out if turn == 0 else None)
+        gather_stage(second, out_back, lambda i: line.pump(ready(base_out), 3 if i == SUPER else 2))
         share.start()
         line.release(turn, base_gate)
         r.grads[base_out : base_out + local, :] = tn(r.branch[...], r.ga[...]).astype(BF16)
@@ -1348,8 +1358,6 @@
 
         if turn > 0:
             await_loads("n1")
-        if turn == 1:
-            stats.stage(0)
         in_grad_rows(3, base_gate)
         line.pump(ready(base_qkv), 1)
         if turn > 0:
@@ -1413,10 +1421,13 @@
 
         if turn + 1 < layers:
             load(layer - 1, *attn_in)
+            source = getattr(r, "mid%d_h" % (layer - 1))
+            mid_pieces = [
+                copies.start(source.at[:, pl.ds(n * 2 * HDIM, 2 * HDIM)], r.dq.at[pl.ds(n * block, block), :])
+                for n in range(width // (2 * HDIM))
+            ]
         if turn > 0:
             await_loads(*in_in)
-        if turn == 1:
-            stats.stage(1)
         last = turn == layers - 1
         if last:
             for number in range(3):
@@ -1437,11 +1448,10 @@
             line.pump(ready(base_qkv + (number + 1) * local), 2 if last else 1)
             if number < SUPER:
                 in_sum.middle(number)
-        if turn == 0:
+        if last:
             for part in range(SUPER):
-                out_sum.middle(part)
-        if turn == 1:
-            stats.stage(2)
+                for which in (1, 2, 3):
+                    out_sum.send_block(part, which)
         if turn + 1 < layers:
             load(layer - 1, *in_in, "n1")
         for part in range(SUPER):
@@ -1462,11 +1472,24 @@
             if layer > 0:
                 firsts[layer - 1].start(part)
         in_sum.drain()
+    line.more(2)
+    for part in range(SUPER):
+        out_sum.middle(part)
+        line.more(2)
+    folded = finish_forward()
+    r.stat_mine[...] = jnp.zeros_like(r.stat_mine)
+    for one in range(top):
+        r.stat_mine[3 * one : 3 * one + 3, :] = getattr(r, "stat%d" % one)[0:3, :]
+    r.stat_mine[3 * top : 3 * top + 3, :] = folded[0:3, :]
+    stats.square()
+    line.more(1)
+    stats.pair()
+    for number in range(cfg.pairs):
+        line.more(1)
+        stats.stage(number)
     out_sum.drain()
-    for number in range(3, cfg.pairs):
-        stats.stage(number)
     stats.finish()
-    line.finish()
+    line.more(line.ticks)
 
 
 def call_kernel(body, cfg, inputs, outputs, scratch, collective_id, name):
@@ -1531,7 +1554,7 @@
     )
 
 
-def run_forward(cfg, x, tables, weights):
+def run_forward(cfg, x, upstream, tables, weights):
     s = jax.ShapeDtypeStruct
     inputs = dict(x=(x, True), **{k: (a, True) for k, a in tables.items()}, **{k + "_h": (a, False) for k, a in weights.items()})
     scratch = dict(
@@ -1541,7 +1564,17 @@
         xo=(s((cfg.block, cfg.width), F32), True), stat=(s((8, 128), F32), True),
         **{k + "_h": (s(scratch[k].shape, scratch[k].dtype), False) for k in SAVED},
     )
+    if cfg.gathers:
+        gathered = (cfg.length, cfg.width)
+        inputs.update(up=(upstream, True))
+        outputs.update(gd_h=(s(gathered, BF16), False))
+        scratch.update(gd=pltpu.VMEM(gathered, BF16), **gather_sems())
     return call_kernel(fwd_kernel, cfg, inputs, outputs, scratch, cfg.layer, "layer_forward")
+
+
+def gather_sems():
+    sems = pltpu.SemaphoreType.DMA((SUPER, 6))
+    return dict(ag3_send=sems, ag3_recv=sems)
 
 
 SAVED = ("ss", "mid", "n1", "ql", "kl", "q", "k", "v", "gate", "heads", "n2", "left", "right", "hid")
@@ -1550,7 +1583,7 @@
 def run_backward(cfg, upstream, xs, saved, tables, weights):
     v, dma, s = pltpu.VMEM, pltpu.SemaphoreType.DMA, jax.ShapeDtypeStruct
     rows, wide, local, ff, block = cfg.length, cfg.width, cfg.local, cfg.ff, cfg.block
-    inputs = dict(up=(upstream, True), **{k: (a, True) for k, a in tables.items()}, **{k + "_h": (a, False) for k, a in weights.items()})
+    inputs = dict(up=(upstream, True), gd_h=(saved[-1]["gd_h"], False), **{k: (a, True) for k, a in tables.items()}, **{k + "_h": (a, False) for k, a in weights.items()})
     for layer in range(cfg.layers):
         inputs["x%d" % layer] = (xs[layer], True)
     for layer in range(cfg.layers - 1):
@@ -1565,7 +1598,7 @@
     small, ring, ring_sem = v((8, 128), F32), v((SLOTS, CHUNK // 2, wide), BF16), dma((SLOTS,))
     scratch = dict(
         **weight_scratch(cfg), **collective_scratch(cfg, ("1", "2"), (cfg.layers,)), **table_scratch(cfg), **forward_scratch(cfg),
-        ag3_send=dma((SUPER, 6)), ag3_recv=dma((SUPER, 6)),
+        **gather_sems(),
         gd=v((rows, wide), BF16), ga=v((rows, wide), BF16),
         g=v((block, wide), F32), gm=v((block, wide), F32),
         branch=v((rows, local), BF16), dx=v((rows, 4 * local), BF16),
@@ -1684,7 +1717,8 @@
     )
     current, xs, saved = tokens, [tokens], []
     for layer in range(layers - 1):
-        saved.append(run_forward(types.SimpleNamespace(layer=layer, **common), current, tables, weights))
+        cfg = types.SimpleNamespace(layer=layer, gathers=layer == layers - 2, **common)
+        saved.append(run_forward(cfg, current, upstream, tables, weights))
         current = saved[-1]["xo"]
         xs.append(current)
     back = run_backward(types.SimpleNamespace(**common), upstream, xs, saved, tables, weights)

time: 396 us -> 385 us (0.972)
  Pallas kernels: 386 us -> 375 us
    pallas_call x3, Pallas kernels: 386 us -> 375 us  [call_kernel(): pl.pallas_call(functools.partial(body, cfg, names), out_shape=[shape for...]
where the time goes in v7:
time: 385 us; the launch traced here: 379 us
  Pallas kernels  375 us (97%)
    pallas_call x3, Pallas kernels, call_kernel(): pl.pallas_call(functools.partial(body, cfg, names), out_shape=[shape for...  375 us

profile of v7, /device:TPU:0, one launch (start us, length us, event | category | flops | bytes accessed | tf_op | source)
XLA Modules:
  0.0 378.7 jit_solution(10529874708363966365)
XLA Ops:
  0.6 88.7 %layer_forward.1 = (f32[256,1024]{1,0:T(8,128)}, f32[8,128]{1,0:T(8,128)}, f32[8,128]{1,0:T(8,128)}, f32[256,1024]{1,0:T(8,128)}, bf16[1024,1024]{1,0:T(8,128)(2...) custom-call(bf16[256,1024]{1,0:T(8,128)(2,1)} %refs_14_.1, ...), custom_call_target="tpu_custom_call" | custom-call | tf_op jit(solution)/shard_map/layer_forward/pallas_call | solution.py:1498
  89.3 270.9 %layers_backward.1 = (bf16[256,1024]{1,0:T(8,128)(2,1)}, bf16[256,1024]{1,0:T(8,128)(2,1)}, f32[8,128]{1,0:T(8,128)}, bf16[6912,1024]{1,0:T(8,128)(2,1)}) custom-call(bf16[256,1024]{1,0:T(8,128)(2,1)} %refs_0_.3, bf16[1024,1024]{1,0:T(8,128)(2,1)} %get-tuple-element.40.refs_1_, f32[1024,128]{1,0:T(8,128)} %constant.11.clone.refs_1_.refs_2_, ...), custom_call_target="tpu_custom_call" | custom-call | tf_op jit(solution)/shard_map/layers_backward/pallas_call | solution.py:1498
  360.2 0.8 slice_reduce_fusion
  361.0 0.7 sqrt.7
  361.6 0.0 copy-start.1
  361.6 0.0 copy-start
  361.6 15.2 %widen_gradients.1 = (f32[2,704,1024]{2,1,0:T(8,128)}, f32[2,704,1024]{2,1,0:T(8,128)}, f32[2,704,1024]{2,1,0:T(8,128)}, f32[2,256,1024]{2,1,0:T(8,128)}, f32[2,...) custom-call(bf16[6912,1024]{1,0:T(8,128)(2,1)} %get-tuple-element.59.refs_0_), custom_call_target="tpu_custom_call" | custom-call | tf_op jit(solution)/shard_map/widen_gradients/pallas_call | solution.py:1498
  376.8 0.0 copy-done.1
  376.8 0.8 copy.27
  377.6 0.0 copy-done
  377.6 0.8 copy.28
  (1 shorter events, 0.0 us)
Async XLA Ops:
  361.6 15.2 %copy-start.1 = (bf16[256,1024]{1,0:T(8,128)(2,1)S(1)}, bf16[256,1024]{1,0:T(8,128)(2,1)}, u32[]{:S(2)}) copy-start(bf16[256,1024]{1,0:T(8,128)(2,1)} %get-tuple-element.80) | copy-start | bytes 1572868
  361.6 16.0 %copy-start = (bf16[256,1024]{1,0:T(8,128)(2,1)S(1)}, bf16[256,1024]{1,0:T(8,128)(2,1)}, u32[]{:S(2)}) copy-start(bf16[256,1024]{1,0:T(8,128)(2,1)} %get-tuple-element.81) | copy-start | bytes 1572868
